TPU v7x, 32 devices: a whole 2x2x4 slice. The times are simulated.
32 devices in a mesh: groups: 2 (over x), rows: 16 (over z, y, core).
Axes of the slice: x: 2, y: 2, z: 4, core: 2. Of those that a mesh axis runs over, the one named last changes fastest.
Arguments:
- single_rep: bfloat16 [256, 384], P(('groups', 'rows')), parts along dimension 0, may hold values from -6 to 6
- pair_grid: bfloat16 [256, 128, 128], P('groups', 'rows'), parts along dimension 0, may hold values from -6 to 6
- frames: float32 [12, 256], P(None, ('groups', 'rows')), parts along dimension 1, may hold values from -60 to 60, as said below
- chain_ids: int32 [256], P('groups'), parts along dimension 0, may hold values from 0 to 3, never falling along the last dimension, each value on 1 to 64 neighbouring positions
- pad_mask: int32 [256], P('groups'), parts along dimension 0, may hold values from 0 to 1, as said below
- ln_pair_gain: float32 [128], replicated, may hold values from 0.5 to 1.5
- w_swiglu: bfloat16 [128, 1024], replicated, may hold values from -0.5 to 0.5
- w_pair_down: bfloat16 [512, 128], replicated, may hold values from -0.25 to 0.25
- w_bias: bfloat16 [128, 12], replicated, may hold values from -2 to 2
- w_qkv: bfloat16 [384, 576], replicated, may hold values from -0.3125 to 0.3125
- w_points: bfloat16 [384, 576], replicated, may hold values from -0.3125 to 0.3125
- gamma_raw: float32 [12], replicated, may hold values from -2 to 2
- chain_bias: float32 [2, 12], replicated, may hold values from -2 to 2
- w_out: bfloat16 [2112, 384], replicated, may hold values from -0.125 to 0.125
- ln_single_gain: float32 [384], replicated, may hold values from 0.5 to 1.5
Outputs:
- single_out: bfloat16 [256, 384], P(('groups', 'rows')), parts along dimension 0
- pair_out: bfloat16 [256, 128, 128], P('groups', 'rows'), parts along dimension 0
There are 2 independent parts, one for each index of `groups`. A program takes and returns all parts, laid end to end along the dimension named above; an argument that names none is the same for every part. Nothing has to cross between parts.
Inputs may be any that keep to these rules, and one draw needn't show every extreme that they name: `frames`: each column is a proper rotation followed by a translation. `pad_mask`: the first residue is real and the last residue is padding.
All inputs are finite; a program needn't handle non-finite values.
Results may differ from a plain program's by a relative error of at most 0.0064.
Values may be sent and summed in bfloat16 or wider, within the bound.
No kernel may reach another device: no remote copies, remote signals or barrier semaphores. Data moves between devices by JAX's collectives and lax.ppermute only.
A program may use at most 128 MiB of HBM per device.

v0:
```python
import math

import jax
import jax.numpy as jnp
from jax import lax
from jax.sharding import PartitionSpec as P

H = 512
HEADS = 12
CH = 16
QP = 4
VP = 8


PRECISE = lax.Precision.HIGHEST


def layer_norm(values, gain):
    centre = jnp.mean(values, axis=-1, keepdims=True)
    centred = values - centre
    spread = jnp.mean(centred * centred, axis=-1, keepdims=True)
    return centred * lax.rsqrt(spread + 1e-05) * gain


def transition_block(pair_rows, ln_pair_gain, w_swiglu, w_pair_down):
    values = pair_rows.astype(jnp.float32)
    normed = layer_norm(values, ln_pair_gain).astype(jnp.bfloat16)
    both_parts = jnp.dot(normed, w_swiglu, preferred_element_type=jnp.float32)
    hidden = (jax.nn.silu(both_parts[:, :H]) * both_parts[:, H:]).astype(jnp.bfloat16)
    update = jnp.dot(hidden, w_pair_down, preferred_element_type=jnp.float32)
    return (values + update).astype(jnp.bfloat16)


def pair_transition(pair_grid, ln_pair_gain, w_swiglu, w_pair_down):
    layout = pair_grid.shape
    flat = pair_grid.reshape(-1, layout[-1])
    total = flat.shape[0]
    block = math.gcd(total, 2048)
    blocks = flat.reshape(total // block, block, layout[-1])
    done = lax.map(
        lambda piece_rows: transition_block(piece_rows, ln_pair_gain, w_swiglu, w_pair_down), blocks
    )
    return done.reshape(layout)


def frame_parts(frames):
    rotation = jnp.transpose(frames[:9]).reshape(-1, 3, 3)
    offset = jnp.transpose(frames[9:])
    return (rotation, offset)


def project_heads(single_rep, frames, w_qkv, w_points):
    features = jnp.dot(single_rep, w_qkv, preferred_element_type=jnp.float32)
    local_pts = jnp.dot(single_rep, w_points, preferred_element_type=jnp.float32)
    rotation, offset = frame_parts(frames)
    residues = single_rep.shape[0]
    points = local_pts.reshape(residues, -1, 3)
    placed = jnp.einsum("rxy,rmy->rmx", rotation, points, precision=PRECISE) + offset[:, None, :]
    placed = placed.reshape(residues, -1)
    width = HEADS * CH
    qwidth = HEADS * QP * 3
    return (
        features[:, :width],
        features[:, width : 2 * width],
        features[:, 2 * width :],
        placed[:, :qwidth],
        placed[:, qwidth : 2 * qwidth],
        placed[:, 2 * qwidth :],
    )


def pair_bias(pair_rows, w_bias):
    query_count, key_count = (pair_rows.shape[0], pair_rows.shape[1])
    flat = jnp.dot(
        pair_rows.reshape(-1, pair_rows.shape[2]), w_bias, preferred_element_type=jnp.float32
    )
    return jnp.transpose(flat.reshape(query_count, key_count, HEADS), (0, 2, 1))


def attention_logits(
    queries, query_pts, keys, key_pts, bias, same_chain, key_valid, gamma_raw, chain_bias
):
    query_count, key_count = (queries.shape[0], keys.shape[0])
    query_heads = queries.reshape(query_count, HEADS, CH)
    key_heads = keys.reshape(key_count, HEADS, CH)
    dots = jnp.einsum("ihc,jhc->ihj", query_heads, key_heads, precision=PRECISE) / math.sqrt(CH)
    query_pth = query_pts.reshape(query_count, HEADS, QP * 3)
    key_pth = key_pts.reshape(key_count, HEADS, QP * 3)
    cross = jnp.einsum("ihc,jhc->ihj", query_pth, key_pth, precision=PRECISE)
    query_sq = jnp.sum(query_pth * query_pth, axis=-1)
    key_sq = jnp.sum(key_pth * key_pth, axis=-1)
    distance = query_sq[:, :, None] + jnp.transpose(key_sq)[None, :, :] - 2.0 * cross
    weight_c = math.sqrt(2.0 / (9.0 * QP))
    weight_l = math.sqrt(1.0 / 3.0)
    gamma = jax.nn.softplus(gamma_raw)
    chain_term = jnp.where(
        same_chain[:, None, :], chain_bias[0][None, :, None], chain_bias[1][None, :, None]
    )
    scores = weight_l * (
        dots + bias + chain_term - gamma[None, :, None] * (0.5 * weight_c) * distance
    )
    return jnp.where(key_valid[None, None, :], scores, -1000000000.0)


def value_sums(attention, values, value_pts):
    query_count, key_count = (attention.shape[0], values.shape[0])
    value_out = jnp.einsum(
        "ihj,jhc->ihc", attention, values.reshape(key_count, HEADS, CH), precision=PRECISE
    )
    point_out = jnp.einsum(
        "ihj,jhm->ihm", attention, value_pts.reshape(key_count, HEADS, VP * 3), precision=PRECISE
    )
    return (value_out.reshape(query_count, -1), point_out.reshape(query_count, -1))


def pair_sums(attention16, pair_rows):
    summed = jnp.einsum("ihj,ijc->ihc", attention16, pair_rows, preferred_element_type=jnp.float32)
    return summed.reshape(attention16.shape[0], -1)


def finish_rows(value_out, point_out, pair_total, frames, single_rep, w_out, ln_single_gain):
    rotation, offset = frame_parts(frames)
    residues = single_rep.shape[0]
    shifted = point_out.reshape(residues, -1, 3) - offset[:, None, :]
    local_out = jnp.einsum("rxy,rmx->rmy", rotation, shifted, precision=PRECISE)
    lengths = jnp.sqrt(jnp.sum(local_out * local_out, axis=-1) + 1.0)
    joined = jnp.concatenate(
        [value_out, local_out.reshape(residues, -1), lengths, pair_total], axis=1
    ).astype(jnp.bfloat16)
    update = jnp.dot(joined, w_out, preferred_element_type=jnp.float32)
    return layer_norm(single_rep.astype(jnp.float32) + update, ln_single_gain).astype(jnp.bfloat16)


def on_device(
    single_rep,
    pair_grid,
    frames,
    chain_ids,
    pad_mask,
    ln_pair_gain,
    w_swiglu,
    w_pair_down,
    w_bias,
    w_qkv,
    w_points,
    gamma_raw,
    chain_bias,
    w_out,
    ln_single_gain,
):
    pair_out = pair_transition(pair_grid, ln_pair_gain, w_swiglu, w_pair_down)
    local_rows = single_rep.shape[0]
    first_row = lax.axis_index("rows") * local_rows
    own_chain = lax.dynamic_slice_in_dim(chain_ids, first_row, local_rows, 0)
    own_valid = lax.dynamic_slice_in_dim(pad_mask, first_row, local_rows, 0) > 0
    queries, keys, values, query_pts, key_pts, value_pts = project_heads(
        single_rep, frames, w_qkv, w_points
    )
    all_queries, all_qpts = (
        lax.all_gather(queries, "rows", axis=0, tiled=True),
        lax.all_gather(query_pts, "rows", axis=0, tiled=True),
    )
    bias = pair_bias(pair_out, w_bias)
    same_chain = chain_ids[:, None] == own_chain[None, :]
    scores = attention_logits(
        all_queries, all_qpts, keys, key_pts, bias, same_chain, own_valid, gamma_raw, chain_bias
    )
    peak = lax.pmax(jnp.max(scores, axis=-1).astype(jnp.bfloat16), "rows").astype(jnp.float32)
    expo = jnp.exp(scores - peak[:, :, None])
    row_sums = lax.psum(jnp.sum(expo, axis=-1), "rows")
    attention = expo / row_sums[:, :, None]
    attention16 = attention.astype(jnp.bfloat16)
    part_values, part_points = value_sums(attention, values, value_pts)
    summed = lax.psum_scatter(
        jnp.concatenate([part_values, part_points, pair_sums(attention16, pair_out)], axis=1),
        "rows",
        scatter_dimension=0,
        tiled=True,
    )
    value_width = HEADS * CH
    point_width = HEADS * VP * 3
    value_out = summed[:, :value_width]
    point_out = summed[:, value_width : value_width + point_width]
    pair_total = summed[:, value_width + point_width :]
    single_out = finish_rows(
        value_out, point_out, pair_total, frames, single_rep, w_out, ln_single_gain
    )
    return (single_out, pair_out)


def solution(mesh):
    placed = (
        P(("groups", "rows"), None),
        P("groups", "rows", None),
        P(None, ("groups", "rows")),
        P("groups"),
        P("groups"),
        P(),
        P(),
        P(),
        P(),
        P(),
        P(),
        P(),
        P(),
        P(),
        P(),
    )
    return jax.shard_map(
        on_device,
        mesh=mesh,
        in_specs=placed,
        out_specs=(P(("groups", "rows"), None), P("groups", "rows", None)),
        check_vma=False,
    )
```

profile of v0, /device:TPU:0, one launch (start us, length us, event | category | flops | bytes accessed | tf_op | source)
XLA Modules:
  0.0 191.1 jit_solution(4573413157735390411)
XLA Ops:
  7.2 1.3 convert_reduce_fusion
  8.5 1.3 fusion.18
  9.9 0.1 div.41
  10.0 0.7 slice_bitcast_fusion.1
  10.7 0.8 slice_bitcast_fusion
  11.6 0.1 copy.95
  11.7 1.3 fusion.43
  13.0 0.1 reshape.138
  13.1 0.2 copy.79
  13.3 0.3 convolution_add_fusion.1
  13.6 0.2 copy.81
  13.8 0.1 reshape.140
  14.2 0.1 rsqrt.21
  14.3 0.8 fusion.19
  15.1 0.1 copy-done.17
  15.2 0.7 fusion.2
  16.0 0.2 fusion.30
  16.2 0.2 copy.76
  16.4 0.2 fusion.42
  16.7 23.4 %all_gather.6 = f32[128,192]{1,0:T(8,128)S(1)} all-gather(f32[8,192]{1,0:T(8,128)S(1)} %get-tuple-element.17), channel_id=1, replica_groups=mesh['groups'=2,'rows'=16] {'rows'}, dimensions={0}, use_global_device_ids=true | all-gather | bytes 104448 | tf_op jit(solution)/shard_map/all_gather | solution.py:160
  40.1 0.1 copy.74
  40.5 17.8 %all_gather.7 = f32[128,144]{1,0:T(8,128)S(1)} all-gather(f32[8,144]{1,0:T(8,128)S(1)} %copy.82), channel_id=1, replica_groups=mesh['groups'=2,'rows'=16] {'rows'}, dimensions={0}, use_global_device_ids=true | all-gather | bytes 78336 | tf_op jit(solution)/shard_map/all_gather | solution.py:161
  58.3 0.1 copy.83
  58.5 0.1 reshape.142
  58.6 0.1 multiply_reduce_fusion.1
  58.7 0.1 copy.85
  58.8 0.2 fusion.9
  59.0 0.2 fusion.40
  59.2 31.1 %pmax.7 = bf16[128,12]{0,1:T(8,128)(2,1)S(1)} all-reduce(bf16[128,12]{0,1:T(8,128)(2,1)S(1)} %get-tuple-element.29), channel_id=1, replica_groups=mesh['groups'=2,'rows'=16] {'rows'}, use_global_device_ids=true, to_apply=%region_5.6 | all-reduce | flops 1536 | bytes 6144 | tf_op jit(solution)/shard_map/pmax | solution.py:168
  90.4 30.0 %psum.7 = f32[128,12]{0,1:T(8,128)S(1)} all-reduce(f32[128,12]{0,1:T(8,128)S(1)} %fusion.29), channel_id=1, replica_groups=mesh['groups'=2,'rows'=16] {'rows'}, use_global_device_ids=true, to_apply=%region_7.8 | all-reduce | flops 1536 | bytes 12288 | tf_op jit(solution)/shard_map/psum | solution.py:170
  120.5 0.4 fusion.24
  120.9 1.0 fusion.35
  122.0 0.2 copy.90
  122.2 0.4 fusion.44
  122.6 0.3 copy.91
  122.9 1.0 pad_maximum_fusion
  123.9 1.3 copy.101
  125.4 54.8 %reduce-scatter.4.cloned.1.call-done = f32[8,2016]{1,0:T(8,128)} async-done(((f32[128,2016]{1,0:T(8,128)}), f32[8,2016]{1,0:T(8,128)}) %reduce-scatter.4.cloned.1.call-update) | async-done | bytes 64528 | tf_op jit(solution)/shard_map/reduce_scatter | solution.py:174
  180.2 0.8 convert.14
  181.1 0.8 slice.75
  181.9 0.1 copy.103
  182.1 0.1 copy.94
  182.2 0.2 multiply_reduce_fusion.2
  182.4 0.2 copy.96
  182.8 0.1 concatenate.8
  182.9 0.4 fusion.41
  183.3 0.2 multiply_reduce_fusion.3
  183.5 0.7 multiply_convert_fusion
  (72 shorter events, 1.4 us)
Async XLA Ops:
  7.2 175.7 %copy-start = (bf16[2112,384]{1,0:T(8,128)(2,1)S(1)}, bf16[2112,384]{1,0:T(8,128)(2,1)}, u32[]{:S(2)}) copy-start(bf16[2112,384]{1,0:T(8,128)(2,1)} %param.28) | copy-start | bytes 4866052
  7.2 173.0 %reduce-scatter.4.cloned.1.call-start = ((), (), s32[]{:S(2)}) async-start(), calls=%async_computation.1 | async-start | bytes 1114112 | tf_op jit(solution)/shard_map/reduce_scatter | solution.py:174
  8.5 5.4 %copy-start.16 = (s32[128]{0:T(128)S(1)}, s32[128]{0:T(128)}, u32[]{:S(2)}) copy-start(s32[128]{0:T(128)} %param.18) | copy-start | bytes 1540
  9.9 4.4 %copy-start.1 = (bf16[128,8,128]{2,1,0:T(8,128)(2,1)S(1)}, bf16[128,8,128]{2,1,0:T(8,128)(2,1)}, u32[]{:S(2)}) copy-start(bf16[128,8,128]{2,1,0:T(8,128)(2,1)} %param.16) | copy-start | bytes 786436
  9.9 4.4 %copy-start.5 = (bf16[128,1024]{1,0:T(8,128)(2,1)S(1)}, bf16[128,1024]{1,0:T(8,128)(2,1)}, u32[]{:S(2)}) copy-start(bf16[128,1024]{1,0:T(8,128)(2,1)} %param.21) | copy-start | bytes 786436
  9.9 4.4 %copy-start.15 = (f32[128]{0:T(128)S(1)}, f32[128]{0:T(128)}, u32[]{:S(2)}) copy-start(f32[128]{0:T(128)} %param.20) | copy-start | bytes 1540
  11.5 2.3 %copy-start.10 = (f32[8,3]{1,0:T(8,128)}, f32[8,3]{1,0:T(8,128)S(1)}, u32[]{:S(2)}) copy-start(f32[8,3]{1,0:T(8,128)S(1)} %slice_bitcast_fusion) | copy-start | bytes 292
  11.7 2.1 %copy-start.6 = (f32[8,3,3]{1,2,0:T(4,128)}, f32[8,3,3]{1,2,0:T(4,128)S(1)}, u32[]{:S(2)}) copy-start(f32[8,3,3]{1,2,0:T(4,128)S(1)} %copy.95) | copy-start | bytes 868
  13.9 1.1 copy-start.2
  14.3 0.9 copy-start.17
  15.2 0.7 copy-start.12
  15.2 1.2 copy-start.4
  15.2 1.2 copy-start.8
  15.9 106.3 %copy-start.3 = (bf16[128,8,128]{2,1,0:T(8,128)(2,1)}, bf16[128,8,128]{2,1,0:T(8,128)(2,1)S(1)}, u32[]{:S(2)}) copy-start(bf16[128,8,128]{2,1,0:T(8,128)(2,1)S(1)} %fusion.2) | copy-start | bytes 786436
  15.9 24.4 %copy-start.14 = (f32[2,12]{1,0:T(2,128)S(1)}, f32[2,12]{1,0:T(2,128)}, u32[]{:S(2)}) copy-start(f32[2,12]{1,0:T(2,128)} %param.27) | copy-start | bytes 292
  15.9 24.4 %copy-start.18 = (s32[128]{0:T(128)S(1)}, s32[128]{0:T(128)}, u32[]{:S(2)}) copy-start(s32[128]{0:T(128)} %param.19) | copy-start | bytes 1540
  15.9 42.8 %copy-start.19 = (f32[12]{0:T(128)S(1)}, f32[12]{0:T(128)}, u32[]{:S(2)}) copy-start(f32[12]{0:T(128)} %param.26) | copy-start | bytes 148
  16.0 105.0 %slice-start = ((f32[8,576]{0,1:T(8,128)}), f32[8,288]{0,1:T(8,128)S(1)}, s32[]{:S(2)}) async-start(f32[8,576]{0,1:T(8,128)} %copy-done.2), calls=%async_computation.2 | async-start | bytes 294912 | tf_op jit(solution)/shard_map/slice | solution.py:68
  123.9 1.4 copy-start.11
  123.9 58.3 %copy-start.7 = (f32[8,3,3]{1,2,0:T(4,128)S(1)}, f32[8,3,3]{1,2,0:T(4,128)}, u32[]{:S(2)}) copy-start(f32[8,3,3]{1,2,0:T(4,128)} %copy-done.6) | copy-start | bytes 868
  123.9 58.9 %copy-start.9 = (bf16[8,384]{1,0:T(8,128)(2,1)S(1)}, bf16[8,384]{1,0:T(8,128)(2,1)}, u32[]{:S(2)}) copy-start(bf16[8,384]{1,0:T(8,128)(2,1)} %param.15) | copy-start | bytes 18436
  125.3 58.3 %copy-start.13 = (f32[384]{0:T(512)S(1)}, f32[384]{0:T(512)}, u32[]{:S(2)}) copy-start(f32[384]{0:T(512)} %param.29) | copy-start | bytes 4612
Sparse Core Ops, SparseCore 0:
  125.4 54.6 reduce-scatter.3
where the time goes:
time: 191 us
  blocking collectives  102 us (53%)
  waiting for transfers between devices  54.8 us (29%)
  between operations  14.6 us (8%)
  local copies, waits for them, and re-layouts  7.28 us (4%)
  matrix products  6.34 us (3%)
  other arithmetic  5.69 us (3%)
    reduce_scatter x1, waiting for transfers between devices, on_device(): lax.psum_scatter(jnp.concatenate([part_values, part_points, pair_sums(att...  54.8 us
    pmax x1, blocking collectives, on_device(): lax.pmax(jnp.max(scores, axis=-1).astype(jnp.bfloat16), 'rows')  31.1 us
    psum x1, blocking collectives, on_device(): row_sums = lax.psum(jnp.sum(expo, axis=-1), 'rows')  30 us
    all_gather x1, blocking collectives, on_device(): lax.all_gather(queries, 'rows', axis=0, tiled=True)  23.4 us
    all_gather x1, blocking collectives, on_device(): lax.all_gather(query_pts, 'rows', axis=0, tiled=True)  17.8 us
  transfers between devices with their start and end apart: 1, of which 1 were waited for; matrix products, arithmetic and copies ran while one was open for 0% of the time, Pallas kernels for 0%

commit v1 on v0

v1 whole, which is shorter than its diff:
```python
import functools
import math

import jax
import jax.numpy as jnp
from jax import lax
from jax.experimental import pallas as pl
from jax.experimental.pallas import tpu as pltpu
from jax.sharding import PartitionSpec as P

C = 128
S = 384
H = 512
HEADS = 12
CH = 16
QP = 4
VP = 8
HPAD = 16
FEAT = HEADS * CH
QPTS = HEADS * QP * 3
PLANE = HEADS * VP
F32 = jnp.float32
BF16 = jnp.bfloat16
PRECISE = lax.Precision.HIGHEST
NT = (((1,), (1,)), ((), ()))
SMALL = S // 128 + 1
VMEM_LIMIT = 40 * 1024 * 1024


def iota(shape, dim):
    return lax.broadcasted_iota(jnp.int32, shape, dim)


def layer_norm(values, gain):
    centre = jnp.mean(values, axis=-1, keepdims=True)
    centred = values - centre
    spread = jnp.mean(centred * centred, axis=-1, keepdims=True)
    return centred * lax.rsqrt(spread + 1e-05) * gain


def transition(values, gain, w_swiglu_ref, w_down_ref):
    normed = layer_norm(values, gain).astype(BF16)
    both = jnp.dot(normed, w_swiglu_ref[...], preferred_element_type=F32)
    gate = 0.5 * both[:, :H]
    hidden = (gate * (1.0 + jnp.tanh(gate)) * both[:, H:]).astype(BF16)
    update = jnp.dot(hidden, w_down_ref[...], preferred_element_type=F32)
    return (values + update).astype(BF16)


def pack_kernel(pair_ref, single_ref, frames_ref, out_ref, small_ref, sems):
    local = single_ref.shape[0]
    pair_copy = pltpu.make_async_copy(pair_ref, out_ref.at[:, :local], sems.at[0])
    pair_copy.start()
    rows = frames_ref[...]
    blank = jnp.zeros((local, 128 - 36), F32)
    turned = jnp.concatenate([rows, rows, rows, blank], axis=1)
    high = turned.astype(BF16).astype(F32)
    middle = (turned - high).astype(BF16).astype(F32)
    low = turned - high - middle
    lane = iota(turned.shape, 1)
    parts = jnp.where(lane < 12, high, jnp.where(lane < 24, middle, low)).astype(BF16)
    for dest in range(small_ref.shape[0]):
        for piece in range(SMALL - 1):
            small_ref[dest, piece] = single_ref[:, piece * 128 : piece * 128 + 128]
        small_ref[dest, SMALL - 1] = parts
    small_copy = pltpu.make_async_copy(small_ref, out_ref.at[:, local:], sems.at[1])
    small_copy.start()
    pair_copy.wait()
    small_copy.wait()


def own_kernel(pair_ref, gain_ref, w_swiglu_ref, w_down_ref, out_ref):
    local = pair_ref.shape[1]
    values = pair_ref[...].astype(F32).reshape(-1, C)
    done = transition(values, gain_ref[...], w_swiglu_ref, w_down_ref)
    out_ref[...] = done.astype(F32).reshape(-1, local, C).astype(BF16)


def attend_kernel(
    recv_ref,
    single_ref,
    frames_ref,
    turned_ref,
    chain_row_ref,
    chain_own_ref,
    pad_ref,
    gain_ref,
    w_swiglu_ref,
    w_down_ref,
    wb_ref,
    wq_ref,
    wp_ref,
    gamma_ref,
    cb_ref,
    w_out_ref,
    w_loc_ref,
    gain2_ref,
    _,
    out_ref,
    pair_scr,
    feat_scr,
    pts_scr,
    qf_scr,
    qp_scr,
    attn_scr,
    sums_scr,
):
    nsrc, _, local, _ = recv_ref.shape
    n = nsrc * local

    def piece(index):
        return recv_ref[:, index].astype(F32).reshape(n, 128)

    all_single = jnp.concatenate([piece(local + k).astype(BF16) for k in range(SMALL - 1)], axis=1)
    parts = piece(local + SMALL - 1).astype(BF16)
    rows16, lanes16 = iota((16, 128), 0), iota((16, 128), 1)
    pick = ((lanes16 % 12 == rows16) & (lanes16 < 36)).astype(BF16)
    frame_rows = lax.dot_general(pick, parts, NT, preferred_element_type=F32)
    feats = lax.dot_general(wq_ref[FEAT:, :], all_single, NT, preferred_element_type=F32)
    points = lax.dot_general(wp_ref[QPTS:, :], all_single, NT, preferred_element_type=F32)
    tiles, _, lane = feat_scr.shape
    for t in range(tiles):
        feat_scr[t] = feats[:FEAT, t * lane : (t + 1) * lane]
        pts_scr[t] = points[:, t * lane : (t + 1) * lane]

    def strided(ref, start, count, stride):
        return jnp.concatenate(
            [ref[t, pl.ds(start, count, stride=stride), :] for t in range(tiles)], axis=1
        )

    own_single = single_ref[...]
    qf_scr[...] = lax.dot_general(wq_ref[:FEAT, :], own_single, NT, preferred_element_type=F32)
    qp_scr[...] = lax.dot_general(wp_ref[:QPTS, :], own_single, NT, preferred_element_type=F32)
    own_frames = frames_ref[...]

    def rot(rows, x, y):
        return rows[3 * x + y : 3 * x + y + 1, :]

    def place(rows, triple):
        return [
            rot(rows, x, 0) * triple[0]
            + rot(rows, x, 1) * triple[1]
            + rot(rows, x, 2) * triple[2]
            + rows[9 + x : 10 + x, :]
            for x in range(3)
        ]

    key_feats = [strided(feat_scr, c, HEADS, CH) for c in range(CH)]
    query_feats = [qf_scr[pl.ds(c, HEADS, stride=CH), :] for c in range(CH)]
    key_pts, query_pts = [], []
    for p in range(QP):
        key_pts += place(
            frame_rows, [strided(pts_scr, 3 * p + y, HEADS, 3 * QP) for y in range(3)]
        )
        query_pts += place(
            own_frames, [qp_scr[pl.ds(3 * p + y, HEADS, stride=3 * QP), :] for y in range(3)]
        )
    value_planes = place(
        frame_rows, [strided(pts_scr, QPTS + y, PLANE, 3) for y in range(3)]
    )
    gap = jnp.zeros((128 - PLANE, n), F32)
    values = [feats[FEAT:], jnp.zeros((256 - FEAT, n), F32)]
    for plane in value_planes:
        values += [plane, gap]
    values = jnp.concatenate(values, axis=0)

    gain = gain_ref[...]
    group = max(1, min(local, 512 // n))
    for start in range(0, local, group):
        block = recv_ref[:, start : start + group].astype(F32)
        block = jnp.concatenate([block[:, k].reshape(n, C) for k in range(group)], axis=0)
        done = transition(block, gain, w_swiglu_ref, w_down_ref)
        for k in range(group):
            pair_scr[start + k] = done[k * n : (k + 1) * n]

    weight_c = math.sqrt(2.0 / (9.0 * QP))
    weight_l = math.sqrt(1.0 / 3.0)
    gamma = jax.nn.softplus(gamma_ref[...])
    point_scale = jnp.broadcast_to(gamma * (-0.5 * weight_c), (HEADS, n))
    same_bias = jnp.broadcast_to(cb_ref[:, 0:1], (HEADS, n))
    cross_bias = jnp.broadcast_to(cb_ref[:, 1:2], (HEADS, n))
    chain_row = jnp.broadcast_to(chain_row_ref[...], (HEADS, n))
    real = jnp.broadcast_to(pad_ref[...], (HEADS, n)) > 0
    for i in range(local):
        rows = pair_scr[i]
        bias = lax.dot_general(wb_ref[...], rows, NT, preferred_element_type=F32)[:HEADS]
        dots = sum(q[:, i : i + 1] * k for q, k in zip(query_feats, key_feats))
        distance = 0.0
        for q, k in zip(query_pts, key_pts):
            apart = q[:, i : i + 1] - k
            distance = distance + apart * apart
        chain = jnp.where(chain_row == chain_own_ref[i], same_bias, cross_bias)
        scores = weight_l * (dots * (1.0 / math.sqrt(CH)) + bias + chain + point_scale * distance)
        scores = jnp.where(real, scores, -1000000000.0)
        expo = jnp.exp(scores - jnp.max(scores, axis=-1, keepdims=True))
        attention = expo / jnp.sum(expo, axis=-1, keepdims=True)
        attention = jnp.concatenate([attention, jnp.zeros((HPAD - HEADS, n), F32)], axis=0)
        attn_scr[i * HPAD : (i + 1) * HPAD, :] = attention
        sums_scr[i * HPAD : (i + 1) * HPAD, :] = jnp.dot(
            attention.astype(BF16), rows, preferred_element_type=F32
        )

    every = lax.dot_general(
        attn_scr[...], values, NT, precision=PRECISE, preferred_element_type=F32
    )
    width = every.shape[1]
    heads, lanes = iota((HPAD, width), 0), iota((HPAD, width), 1)
    owner = jnp.where(lanes < 256, lanes // CH, (lanes % 128) // VP)
    every = every.reshape(local, HPAD, width)
    summed = jnp.sum(jnp.where((owner == heads)[None], every, 0.0), axis=1)

    turned = turned_ref[...]
    shifted = [
        summed[:, 256 + 128 * x : 384 + 128 * x] - turned[:, 9 + x : 10 + x] for x in range(3)
    ]
    local_out = [
        turned[:, y : y + 1] * shifted[0]
        + turned[:, 3 + y : 4 + y] * shifted[1]
        + turned[:, 6 + y : 7 + y] * shifted[2]
        for y in range(3)
    ]
    lengths = jnp.sqrt(
        local_out[0] * local_out[0] + local_out[1] * local_out[1] + local_out[2] * local_out[2] + 1.0
    )
    update = jnp.dot(
        summed[:, :FEAT].astype(BF16), w_out_ref[:FEAT, :], preferred_element_type=F32
    )
    for y in range(3):
        update += jnp.dot(
            local_out[y][:, :PLANE].astype(BF16), w_loc_ref[y], preferred_element_type=F32
        )
    at = FEAT + 3 * PLANE
    update += jnp.dot(
        lengths[:, :PLANE].astype(BF16), w_out_ref[at : at + PLANE, :], preferred_element_type=F32
    )
    at += PLANE
    pair_total = jnp.concatenate(
        [sums_scr[pl.ds(h, local, stride=HPAD), :] for h in range(HEADS)], axis=1
    )
    update += jnp.dot(pair_total.astype(BF16), w_out_ref[at:, :], preferred_element_type=F32)
    out_ref[...] = layer_norm(own_single.astype(F32) + update, gain2_ref[...]).astype(BF16)


def whole(memory=pltpu.VMEM):
    return pl.BlockSpec(memory_space=memory)


def on_device(
    single_rep,
    pair_grid,
    frames,
    chain_ids,
    pad_mask,
    ln_pair_gain,
    w_swiglu,
    w_pair_down,
    w_bias,
    w_qkv,
    w_points,
    gamma_raw,
    chain_bias,
    w_out,
    ln_single_gain,
):
    n, local, _ = pair_grid.shape
    nsrc = n // local
    tiles = max(1, n // 128)
    gain = ln_pair_gain.reshape(1, C)

    packed = pl.pallas_call(
        pack_kernel,
        out_shape=jax.ShapeDtypeStruct((nsrc, local + SMALL, local, C), BF16),
        in_specs=[whole(pl.ANY), whole(), whole()],
        out_specs=whole(pl.ANY),
        scratch_shapes=[
            pltpu.VMEM((nsrc, SMALL, local, C), BF16),
            pltpu.SemaphoreType.DMA((2,)),
        ],
        compiler_params=pltpu.CompilerParams(vmem_limit_bytes=VMEM_LIMIT),
        name="pack",
    )(pair_grid.reshape(nsrc, local, local, C), single_rep, frames.T)
    received = lax.all_to_all(packed, "rows", 0, 0, tiled=True)

    block = math.gcd(n, 128)
    pair_out = pl.pallas_call(
        own_kernel,
        out_shape=jax.ShapeDtypeStruct(pair_grid.shape, BF16),
        grid=(n // block,),
        in_specs=[
            pl.BlockSpec((block, local, C), lambda g: (g, 0, 0)),
            pl.BlockSpec((1, C), lambda g: (0, 0)),
            pl.BlockSpec(w_swiglu.shape, lambda g: (0, 0)),
            pl.BlockSpec(w_pair_down.shape, lambda g: (0, 0)),
        ],
        out_specs=pl.BlockSpec((block, local, C), lambda g: (g, 0, 0)),
        compiler_params=pltpu.CompilerParams(vmem_limit_bytes=VMEM_LIMIT),
        cost_estimate=pl.CostEstimate(
            flops=6 * n * local * C * H, bytes_accessed=4 * n * local * C, transcendentals=0
        ),
        name="own_transition",
    )(pair_grid, gain, w_swiglu, w_pair_down)

    first_row = lax.axis_index("rows") * local
    chain_own = lax.dynamic_slice_in_dim(chain_ids, first_row, local, 0)
    at = FEAT + 3 * PLANE
    w_loc = jnp.transpose(w_out[FEAT:at].reshape(PLANE, 3, S), (1, 0, 2))
    wb = jnp.pad(w_bias.T, ((0, HPAD - HEADS), (0, 0)))
    operands = [
        received,
        single_rep,
        frames,
        frames.T,
        chain_ids.reshape(1, n),
        chain_own,
        pad_mask.reshape(1, n),
        gain,
        w_swiglu,
        w_pair_down,
        wb,
        w_qkv.T,
        w_points.T,
        gamma_raw.reshape(HEADS, 1),
        chain_bias.T,
        w_out,
        w_loc,
        ln_single_gain.reshape(1, S),
        pair_out,
    ]
    memories = {5: pltpu.SMEM, len(operands) - 1: pl.ANY}
    specs = [whole(memories.get(k, pltpu.VMEM)) for k in range(len(operands))]
    single_out = pl.pallas_call(
        attend_kernel,
        out_shape=jax.ShapeDtypeStruct((local, S), BF16),
        in_specs=specs,
        out_specs=whole(),
        scratch_shapes=[
            pltpu.VMEM((local, n, C), BF16),
            pltpu.VMEM((tiles, FEAT, n // tiles), F32),
            pltpu.VMEM((tiles, QPTS + 3 * PLANE, n // tiles), F32),
            pltpu.VMEM((FEAT, local), F32),
            pltpu.VMEM((QPTS, local), F32),
            pltpu.VMEM((local * HPAD, n), F32),
            pltpu.VMEM((local * HPAD, C), F32),
        ],
        compiler_params=pltpu.CompilerParams(vmem_limit_bytes=VMEM_LIMIT),
        name="attend",
    )(*operands)
    return (single_out, pair_out)


def solution(mesh):
    placed = (
        P(("groups", "rows"), None),
        P("groups", "rows", None),
        P(None, ("groups", "rows")),
        P("groups"),
        P("groups"),
    ) + (P(),) * 10
    return jax.shard_map(
        on_device,
        mesh=mesh,
        in_specs=placed,
        out_specs=(P(("groups", "rows"), None), P("groups", "rows", None)),
        check_vma=False,
    )
```

time: 191 us -> 34.1 us (0.18)
  blocking collectives: 102 us -> 0 us
  waiting for transfers between devices: 54.8 us -> 1.6 us
  between operations: 14.6 us -> 0.77 us
  Pallas kernels: 0 us -> 8.84 us
  local copies, waits for them, and re-layouts: 7.28 us -> 14.9 us
  starting transfers between devices: 0.04 us -> 7.4 us
  matrix products: 6.34 us -> 0 us
  other arithmetic: 5.69 us -> 0 us
    reduce_scatter x1 -> x0, waiting for transfers between devices: 54.8 us -> none  [on_device(): lax.psum_scatter(jnp.concatenate([part_values, part_points, pair_sums(att...]
    all_gather x2 -> x0, blocking collectives: 41.2 us -> none  [the longest x1 23.4 us: on_device(): lax.all_gather(queries, 'rows', axis=0, tiled=True)]
    pmax x1 -> x0, blocking collectives: 31.1 us -> none  [on_device(): lax.pmax(jnp.max(scores, axis=-1).astype(jnp.bfloat16), 'rows')]
    psum x1 -> x0, blocking collectives: 30 us -> none  [on_device(): row_sums = lax.psum(jnp.sum(expo, axis=-1), 'rows')]
    pallas_call x0 -> x3, Pallas kernels: none -> 8.84 us  [the longest x1 5.88 us: on_device(): pl.pallas_call(attend_kernel, out_shape=jax.ShapeDtypeStruct((local, S),...]
    unnamed x42 -> x40, local copies, waits for them, and re-layouts: 1.69 us -> 9.87 us
    all_to_all x0 -> x1, starting transfers between devices: none -> 7.4 us  [on_device(): received = lax.all_to_all(packed, 'rows', 0, 0, tiled=True)]
    dot_general x13 -> x0, matrix products: 6.34 us -> none  [the longest x1 1.28 us: project_heads(): jnp.dot(single_rep, w_points, preferred_element_type=jnp.float32)]
  transfers between devices with their start and end apart: 1 -> 1, of which waited for: 1 -> 1; matrix products, arithmetic and copies ran while one was open for 0% -> 20% of each run, Pallas kernels for 0% -> 7%
where the time goes in v1:
time: 34.1 us; the launch traced here: 33.5 us
  local copies, waits for them, and re-layouts  14.9 us (44%)
  Pallas kernels  8.84 us (26%)
  starting transfers between devices  7.4 us (22%)
  waiting for transfers between devices  1.6 us (5%)
  between operations  0.77 us (2%)
    unnamed x40, local copies, waits for them, and re-layouts  9.87 us
    all_to_all x1, starting transfers between devices, on_device(): received = lax.all_to_all(packed, 'rows', 0, 0, tiled=True)  7.4 us
    pallas_call x1, Pallas kernels, on_device(): pl.pallas_call(attend_kernel, out_shape=jax.ShapeDtypeStruct((local, S),...  5.88 us
    pallas_call x1, Pallas kernels, on_device(): pl.pallas_call(own_kernel, out_shape=jax.ShapeDtypeStruct(pair_grid.shape...  2.2 us
    reshape x2, local copies, waits for them, and re-layouts, on_device(): w_loc = jnp.transpose(w_out[FEAT:at].reshape(PLANE, 3, S), (1, 0, 2))  1.81 us
    all_to_all x1, waiting for transfers between devices, on_device(): received = lax.all_to_all(packed, 'rows', 0, 0, tiled=True)  1.6 us
    reshape x1, local copies, waits for them, and re-layouts, on_device(): ln_single_gain.reshape(1, S)  1.25 us
    pallas_call x1, Pallas kernels, on_device(): pl.pallas_call(pack_kernel, out_shape=jax.ShapeDtypeStruct((nsrc, local +...  0.77 us
  transfers between devices with their start and end apart: 1, of which 1 were waited for; matrix products, arithmetic and copies ran while one was open for 20% of the time, Pallas kernels for 7%

profile of v1, /device:TPU:0, one launch (start us, length us, event | category | flops | bytes accessed | tf_op | source)
XLA Modules:
  0.0 33.5 jit_solution(8393020764745833650)
XLA Ops:
  0.6 0.0 slice-start
  0.6 0.0 copy-start.3
  0.7 0.0 copy-start.5
  0.7 1.0 %copy-done.5 = bf16[128,8,128]{2,1,0:T(8,128)(2,1)S(1)} copy-done((bf16[128,8,128]{2,1,0:T(8,128)(2,1)S(1)}, bf16[128,8,128]{2,1,0:T(8,128)(2,1)}, u32[]{:S(2)}) %copy-start.5) | copy-done | bytes 262168
  1.7 0.0 copy-start.8
  1.7 0.7 %copy-done.8 = f32[12,8]{0,1:T(8,128)S(1)} copy-done((f32[12,8]{0,1:T(8,128)S(1)}, f32[12,8]{0,1:T(8,128)}, u32[]{:S(2)}) %copy-start.8) | copy-done | bytes 408
  2.3 0.0 copy-start.10
  2.4 0.7 %copy-done.10 = bf16[8,384]{1,0:T(8,128)(2,1)S(1)} copy-done((bf16[8,384]{1,0:T(8,128)(2,1)S(1)}, bf16[8,384]{1,0:T(8,128)(2,1)}, u32[]{:S(2)}) %copy-start.10) | copy-done | bytes 6168
  3.0 0.0 copy-start.13
  3.0 0.8 %pack.1 = bf16[16,12,8,128]{3,2,1,0:T(8,128)(2,1)} custom-call(bf16[16,8,8,128]{3,2,1,0:T(8,128)(2,1)S(1)} %bitcast.16, bf16[8,384]{1,0:T(8,128)(2,1)S(1)} %copy-done.10, f32[8,12]{1,0:T(8,128)S(1)} %bitcast.17), custom_call_target="tpu_custom_call" | custom-call | tf_op jit(solution)/shard_map/pack/pallas_call | solution.py:270
  3.8 0.0 copy-start.9
  3.8 0.0 copy-start.11
  3.8 7.4 %all-to-all-start = ((bf16[16,12,8,128]{3,2,1,0:T(8,128)(2,1)}), bf16[16,12,8,128]{3,2,1,0:T(8,128)(2,1)S(1)}, u32[]{:S(2)}, u32[]{:S(2)}) async-start(bf16[16,12,8,128]{3,2,1,0:T(8,128)(2,1)} %pack.1), calls=%async_computation | async-start | bytes 786432 | tf_op jit(solution)/shard_map/all_to_all | solution.py:282
  11.2 0.0 copy-start
  11.3 0.0 copy-start.1
  11.3 0.0 copy-start.2
  11.3 0.9 %copy.22.frames_ref = f32[12,8]{1,0:T(8,128)S(1)} copy(f32[12,8]{0,1:T(8,128)} %param.17) | data formatting | bytes 768 | tf_op args[2]
  12.2 0.7 %copy.23.gamma_ref = f32[12,1]{1,0:T(8,128)S(1)} copy(f32[12,1]{0,1:T(1,128)} %bitcast.25) | data formatting | bytes 96 | tf_op jit(solution)/shard_map/reshape | solution.py:322
  12.9 0.8 %copy.20 = f32[2,12]{0,1:T(8,128)S(1)} copy(f32[2,12]{1,0:T(2,128)} %param.27) | data formatting | bytes 192 | tf_op args[12]
  13.7 0.0 slice-done
  13.7 0.8 %reshape.30 = bf16[96,3,384]{2,1,0:T(4,128)(2,1)} reshape(bf16[288,384]{1,0:T(8,128)(2,1)S(1)} %slice-done) | data formatting | bytes 442368 | tf_op jit(solution)/shard_map/reshape | solution.py:306
  14.5 1.0 %copy.25 = bf16[96,3,384]{2,0,1:T(8,128)(2,1)S(1)} copy(bf16[96,3,384]{2,1,0:T(4,128)(2,1)} %reshape.30) | data formatting | bytes 442368 | tf_op jit(solution)/shard_map/reshape | solution.py:306
  15.5 1.2 %reshape.31.gain2_ref = f32[1,384]{1,0:T(1,128)} reshape(f32[384]{0:T(512)} %param.29) | data formatting | bytes 3072 | tf_op jit(solution)/shard_map/reshape | solution.py:326
  16.8 0.0 copy-done.13
  16.8 0.6 %dynamic_slice.3.chain_own_ref = s32[8]{0:T(128)} dynamic-slice(s32[128]{0:T(128)S(1)} %copy-done.13, s32[]{:T(128)S(6)} %select_n.3), dynamic_slice_sizes={8} | dynamic-slice | bytes 68 | tf_op jit(solution)/shard_map/dynamic_slice | solution.py:304
  17.3 0.7 %pad.4.wb_ref = bf16[16,128]{1,0:T(8,128)(2,1)S(1)} pad(bf16[12,128]{1,0:T(8,128)(2,1)} %bitcast.24, bf16[]{:T(256)} %constant.11.clone.1), padding=0_4x0_0 | pad | bytes 7170 | tf_op jit(solution)/shard_map/jit(_pad)/pad | solution.py:307
  18.0 0.0 copy-done.3
  18.0 0.0 copy-done.7
  18.0 0.0 copy-start.6
  18.0 0.9 %copy-done.6 = bf16[128,8,128]{2,1,0:T(8,128)(2,1)S(1)} copy-done((bf16[128,8,128]{2,1,0:T(8,128)(2,1)S(1)}, bf16[128,8,128]{2,1,0:T(8,128)(2,1)}, u32[]{:S(2)}) %copy-start.6) | copy-done | bytes 262168
  19.0 0.0 copy-start.16
  19.0 0.7 %copy-done.16 = f32[128]{0:T(128)S(1)} copy-done((f32[128]{0:T(128)S(1)}, f32[128]{0:T(128)}, u32[]{:S(2)}) %copy-start.16) | copy-done | bytes 536
  19.6 2.2 %own_transition.1._ = bf16[128,8,128]{2,1,0:T(8,128)(2,1)} custom-call(bf16[128,8,128]{2,1,0:T(8,128)(2,1)S(1)} %copy-done.6, f32[1,128]{1,0:T(1,128)S(1)} %bitcast.22, bf16[128,1024]{1,0:T(8,128)(2,1)S(1)} %copy-done.3, bf16[512,128]{1,0:T(8,128)(2,1)S(1)} %copy-done.7), custom_call_target="tpu_custom_call" | custom-call | flops 402653184 | bytes 524288 | tf_op jit(solution)/shard_map/own_transition/pallas_call | solution.py:285
  21.8 1.6 %all-to-all-done.recv_ref = bf16[16,12,8,128]{3,2,1,0:T(8,128)(2,1)S(1)} async-done(((bf16[16,12,8,128]{3,2,1,0:T(8,128)(2,1)}), bf16[16,12,8,128]{3,2,1,0:T(8,128)(2,1)S(1)}, u32[]{:S(2)}, u32[]{:S(2)}) %all-to-all-start) | async-done | bytes 393248 | tf_op jit(solution)/shard_map/all_to_all | solution.py:282
  23.4 0.0 copy-done.9
  23.4 0.0 copy-done.11
  23.5 0.0 copy-done
  23.5 0.0 copy-done.1
  23.5 0.0 copy-done.2
  23.5 0.0 copy-start.4
  23.5 0.9 %copy-done.4 = bf16[128,8,128]{2,1,0:T(8,128)(2,1)S(1)} copy-done((bf16[128,8,128]{2,1,0:T(8,128)(2,1)S(1)}, bf16[128,8,128]{2,1,0:T(8,128)(2,1)}, u32[]{:S(2)}) %copy-start.4) | copy-done | bytes 262168
  24.4 0.0 copy-start.12
  24.4 0.7 %copy-done.12 = f32[1,384]{1,0:T(1,128)S(1)} copy-done((f32[1,384]{1,0:T(1,128)S(1)}, f32[1,384]{1,0:T(1,128)}, u32[]{:S(2)}) %copy-start.12) | copy-done | bytes 1560
  25.1 0.7 %copy-done.14 = s32[128]{0:T(128)S(1)} copy-done((s32[128]{0:T(128)S(1)}, s32[128]{0:T(128)}, u32[]{:S(2)}) %copy-start.14) | copy-done | bytes 536
  25.8 0.7 %copy-done.15 = s32[128]{0:T(128)S(1)} copy-done((s32[128]{0:T(128)S(1)}, s32[128]{0:T(128)}, u32[]{:S(2)}) %copy-start.15) | copy-done | bytes 536
  26.4 0.7 %copy-done.17 = f32[128]{0:T(128)S(1)} copy-done((f32[128]{0:T(128)S(1)}, f32[128]{0:T(128)}, u32[]{:S(2)}) %copy-start.17) | copy-done | bytes 536
  27.1 0.6 %copy-done.18 = s32[8]{0:T(128)S(1)} copy-done((s32[8]{0:T(128)S(1)}, s32[8]{0:T(128)}, u32[]{:S(2)}) %copy-start.18) | copy-done | bytes 56
  27.7 5.9 %attend.1 = bf16[8,384]{1,0:T(8,128)(2,1)} custom-call(bf16[16,12,8,128]{3,2,1,0:T(8,128)(2,1)S(1)} %all-to-all-done.recv_ref, bf16[8,384]{1,0:T(8,128)(2,1)S(1)} %copy-done.11, f32[12,8]{1,0:T(8,128)S(1)} %copy.22.frames_ref, f32[8,12]{1,0:T(8,128)S(1)} %bitcast.18, s32[1,128]{1,0:T(1,128)S(1)} %bitcast.20, s32[8]{0:T(128)S(1)} %copy-done.18, ...), custom_call_target="tpu_custom_call" | custom-call | tf_op jit(solution)/shard_map/attend/pallas_call | solution.py:331
  (5 shorter events, 0.0 us)
Async XLA Ops:
  0.6 13.1 %slice-start = ((bf16[2112,384]{1,0:T(8,128)(2,1)}), bf16[288,384]{1,0:T(8,128)(2,1)S(1)}, s32[]{:S(2)}) async-start(bf16[2112,384]{1,0:T(8,128)(2,1)} %w_out_ref.1), calls=%async_computation.1 | async-start | bytes 442368 | tf_op jit(solution)/shard_map/slice | solution.py:306
  0.6 17.4 %copy-start.3 = (bf16[128,1024]{1,0:T(8,128)(2,1)S(1)}, bf16[128,1024]{1,0:T(8,128)(2,1)}, u32[]{:S(2)}) copy-start(bf16[128,1024]{1,0:T(8,128)(2,1)} %w_swiglu_ref.3) | copy-start | bytes 786436
  0.7 1.0 %copy-start.5 = (bf16[128,8,128]{2,1,0:T(8,128)(2,1)S(1)}, bf16[128,8,128]{2,1,0:T(8,128)(2,1)}, u32[]{:S(2)}) copy-start(bf16[128,8,128]{2,1,0:T(8,128)(2,1)} %pair_ref.1) | copy-start | bytes 786436
  1.7 0.7 %copy-start.8 = (f32[12,8]{0,1:T(8,128)S(1)}, f32[12,8]{0,1:T(8,128)}, u32[]{:S(2)}) copy-start(f32[12,8]{0,1:T(8,128)} %param.17) | copy-start | bytes 1156
  2.3 0.7 %copy-start.10 = (bf16[8,384]{1,0:T(8,128)(2,1)S(1)}, bf16[8,384]{1,0:T(8,128)(2,1)}, u32[]{:S(2)}) copy-start(bf16[8,384]{1,0:T(8,128)(2,1)} %single_ref.3) | copy-start | bytes 18436
  3.0 13.7 %copy-start.13 = (s32[128]{0:T(128)S(1)}, s32[128]{0:T(128)}, u32[]{:S(2)}) copy-start(s32[128]{0:T(128)} %param.18) | copy-start | bytes 1540
  3.0 15.0 %copy-start.7 = (bf16[512,128]{1,0:T(8,128)(2,1)S(1)}, bf16[512,128]{1,0:T(8,128)(2,1)}, u32[]{:S(2)}) copy-start(bf16[512,128]{1,0:T(8,128)(2,1)} %w_down_ref.3) | copy-start | bytes 393220
  3.8 19.6 %copy-start.9 = (f32[12,8]{0,1:T(8,128)S(1)}, f32[12,8]{0,1:T(8,128)}, u32[]{:S(2)}) copy-start(f32[12,8]{0,1:T(8,128)} %param.17) | copy-start | bytes 1156
  3.8 19.6 %copy-start.11 = (bf16[8,384]{1,0:T(8,128)(2,1)S(1)}, bf16[8,384]{1,0:T(8,128)(2,1)}, u32[]{:S(2)}) copy-start(bf16[8,384]{1,0:T(8,128)(2,1)} %single_ref.3) | copy-start | bytes 18436
  3.8 19.6 %all-to-all-start = ((bf16[16,12,8,128]{3,2,1,0:T(8,128)(2,1)}), bf16[16,12,8,128]{3,2,1,0:T(8,128)(2,1)S(1)}, u32[]{:S(2)}, u32[]{:S(2)}) async-start(bf16[16,12,8,128]{3,2,1,0:T(8,128)(2,1)} %pack.1), calls=%async_computation | async-start | bytes 786432 | tf_op jit(solution)/shard_map/all_to_all | solution.py:282
  11.2 12.2 %copy-start = (bf16[2112,384]{1,0:T(8,128)(2,1)S(1)}, bf16[2112,384]{1,0:T(8,128)(2,1)}, u32[]{:S(2)}) copy-start(bf16[2112,384]{1,0:T(8,128)(2,1)} %w_out_ref.1) | copy-start | bytes 4866052
  11.3 12.2 %copy-start.1 = (bf16[384,576]{0,1:T(8,128)(2,1)S(1)}, bf16[384,576]{0,1:T(8,128)(2,1)}, u32[]{:S(2)}) copy-start(bf16[384,576]{0,1:T(8,128)(2,1)} %param.24) | copy-start | bytes 1327108
  11.3 12.2 %copy-start.2 = (bf16[384,576]{0,1:T(8,128)(2,1)S(1)}, bf16[384,576]{0,1:T(8,128)(2,1)}, u32[]{:S(2)}) copy-start(bf16[384,576]{0,1:T(8,128)(2,1)} %param.25) | copy-start | bytes 1327108
  18.0 1.0 %copy-start.6 = (bf16[128,8,128]{2,1,0:T(8,128)(2,1)S(1)}, bf16[128,8,128]{2,1,0:T(8,128)(2,1)}, u32[]{:S(2)}) copy-start(bf16[128,8,128]{2,1,0:T(8,128)(2,1)} %pair_ref.1) | copy-start | bytes 786436
  19.0 0.7 %copy-start.16 = (f32[128]{0:T(128)S(1)}, f32[128]{0:T(128)}, u32[]{:S(2)}) copy-start(f32[128]{0:T(128)} %param.20) | copy-start | bytes 1540
  23.5 1.0 %copy-start.4 = (bf16[128,8,128]{2,1,0:T(8,128)(2,1)S(1)}, bf16[128,8,128]{2,1,0:T(8,128)(2,1)}, u32[]{:S(2)}) copy-start(bf16[128,8,128]{2,1,0:T(8,128)(2,1)} %own_transition.1._) | copy-start | bytes 786436
  24.4 0.7 %copy-start.12 = (f32[1,384]{1,0:T(1,128)S(1)}, f32[1,384]{1,0:T(1,128)}, u32[]{:S(2)}) copy-start(f32[1,384]{1,0:T(1,128)} %reshape.31.gain2_ref) | copy-start | bytes 4612
  25.1 0.7 %copy-start.14 = (s32[128]{0:T(128)S(1)}, s32[128]{0:T(128)}, u32[]{:S(2)}) copy-start(s32[128]{0:T(128)} %param.18) | copy-start | bytes 1540
  25.8 0.7 %copy-start.15 = (s32[128]{0:T(128)S(1)}, s32[128]{0:T(128)}, u32[]{:S(2)}) copy-start(s32[128]{0:T(128)} %param.19) | copy-start | bytes 1540
  26.4 0.7 %copy-start.17 = (f32[128]{0:T(128)S(1)}, f32[128]{0:T(128)}, u32[]{:S(2)}) copy-start(f32[128]{0:T(128)} %param.20) | copy-start | bytes 1540
  27.1 0.6 %copy-start.18 = (s32[8]{0:T(128)S(1)}, s32[8]{0:T(128)}, u32[]{:S(2)}) copy-start(s32[8]{0:T(128)} %dynamic_slice.3.chain_own_ref) | copy-start | bytes 100

commit v2 on v1

v2 whole, which is shorter than its diff:
```python
import math

import jax
import jax.numpy as jnp
from jax import lax
from jax.experimental import pallas as pl
from jax.experimental.pallas import tpu as pltpu
from jax.sharding import PartitionSpec as P

C = 128
S = 384
H = 512
HEADS = 12
CH = 16
QP = 4
VP = 8
HPAD = 16
FEAT = HEADS * CH
QPTS = HEADS * QP * 3
PLANE = HEADS * VP
WIDE = 256 + 3 * 128
F32 = jnp.float32
BF16 = jnp.bfloat16
NT = (((1,), (1,)), ((), ()))
MIB = 1024 * 1024
PREP_FLOPS = 10**9
WEIGHT_L = math.sqrt(1.0 / 3.0)
WEIGHT_C = math.sqrt(2.0 / (9.0 * QP))


def iota(shape, dim):
    return lax.broadcasted_iota(jnp.int32, shape, dim)


def nt_dot(a, b):
    return lax.dot_general(a, b, NT, preferred_element_type=F32)


def layer_norm(values, gain):
    centre = jnp.mean(values, axis=-1, keepdims=True)
    centred = values - centre
    spread = jnp.mean(centred * centred, axis=-1, keepdims=True)
    return centred * lax.rsqrt(spread + 1e-05) * gain


def transition(values, gain, w_swiglu_ref, w_down_ref):
    normed = layer_norm(values, gain).astype(BF16)
    both = jnp.dot(normed, w_swiglu_ref[...], preferred_element_type=F32)
    gate = 0.5 * both[:, :H]
    hidden = (gate * (1.0 + jnp.tanh(gate)) * both[:, H:]).astype(BF16)
    update = jnp.dot(hidden, w_down_ref[...], preferred_element_type=F32)
    return (values + update).astype(BF16)


def split(values):
    high = values.astype(BF16)
    return high, (values - high.astype(F32)).astype(BF16)


def pack_kernel(single_hbm, frames_hbm, out_ref, single_ref, frames_ref, sems):
    copies = [
        pltpu.make_async_copy(single_hbm, single_ref, sems.at[0]),
        pltpu.make_async_copy(frames_hbm, frames_ref, sems.at[1]),
    ]
    for copy in copies:
        copy.start()
    for copy in copies:
        copy.wait()
    rows = frames_ref[...]
    blank = jnp.zeros((rows.shape[0], 128 - 36), F32)
    turned = jnp.concatenate([rows, rows, rows, blank], axis=1)
    high = turned.astype(BF16).astype(F32)
    middle = (turned - high).astype(BF16).astype(F32)
    low = turned - high - middle
    lane = iota(turned.shape, 1)
    out_ref[:, :S] = single_ref[...]
    out_ref[:, S:] = jnp.where(lane < 12, high, jnp.where(lane < 24, middle, low)).astype(BF16)


def strided(ref, start, count, stride):
    return jnp.concatenate(
        [ref[t, pl.ds(start, count, stride=stride), :] for t in range(ref.shape[0])], axis=1
    )


def own_kernel(*refs):
    sources, refs = refs[:13], refs[13:]
    out_ref, heads_ref, rows_ref, gains_ref, wb_out_ref, w_loc_ref, wq_ref, wp_ref = refs[:8]
    held, refs = refs[8:19], refs[19:]
    loc_scr, sems = refs
    pair_hbm, *_ = sources
    n, local, _ = pair_hbm.shape
    targets = list(held) + [wq_ref, wp_ref]
    copies = []
    for k, (source, target) in enumerate(zip(sources, targets)):
        if k == 10:
            source = source.at[pl.ds(FEAT, 3 * PLANE)]
        copies.append(pltpu.make_async_copy(source, target, sems.at[k]))
        copies[k].start()
    pair_ref, w_swiglu_ref, w_down_ref, gain_ref, gamma_ref, cb_ref = held[:6]
    chain_ref, pad_ref, gain2_ref, wb_ref, loc_ref = held[6:]
    for copy in copies[:4]:
        copy.wait()
    gain = gain_ref[...].reshape(1, C)
    block = math.gcd(n, 128)

    def step(at):
        values = pair_ref[pl.ds(at, block)].astype(F32).reshape(-1, C)
        done = transition(values, gain, w_swiglu_ref, w_down_ref)
        out_ref[pl.ds(at, block)] = done.astype(F32).reshape(-1, local, C).astype(BF16)

    if n == block:
        step(0)
    else:
        pl.loop(0, n, step=block)(step)
    for copy in copies[4:]:
        copy.wait()

    diagonal = iota((HPAD, HEADS), 0) == iota((HPAD, HEADS), 1)

    def column(row):
        turned = jnp.sum(jnp.where(diagonal, row, 0.0), axis=1, keepdims=True)
        return jnp.broadcast_to(turned, (HPAD, 128))

    gamma = jax.nn.softplus(gamma_ref[...].reshape(1, HEADS))
    heads_ref[0] = column(gamma * (-0.5 * WEIGHT_C))
    heads_ref[1] = column(cb_ref[0:1, :])
    heads_ref[2] = column(cb_ref[1:2, :])
    rows_ref[0:1, :] = chain_ref[...].reshape(1, n)
    rows_ref[1:2, :] = pad_ref[...].reshape(1, n)
    gains_ref[0:1, :S] = gain2_ref[...].reshape(1, S)
    gains_ref[0:1, S:] = gain
    wb_out_ref[...] = jnp.concatenate(
        [wb_ref[...], jnp.zeros((HPAD - HEADS, C), BF16)], axis=0
    )
    local_rows = loc_ref[...].astype(F32)
    for t in range(S // 128):
        loc_scr[t] = local_rows[:, t * 128 : (t + 1) * 128]
    for y in range(3):
        w_loc_ref[y] = strided(loc_scr, y, PLANE, 3).astype(BF16)


def prepare_kernel(offsets, *refs):
    pieces, refs = refs[: len(offsets)], refs[len(offsets) :]
    heads_ref, rows_ref, wq_ref, wp_ref = refs[:4]
    base_ref, value_ref = refs[4:6]
    all_scr, feat_scr, pts_scr, qf_scr, qp_scr = refs[6:]
    tiles, _, lane = feat_scr.shape
    n = all_scr.shape[0]
    local = pieces[0].shape[1]
    me = lax.axis_index("rows")

    for piece, origins in zip(pieces, offsets):
        for k, origin in enumerate(origins):
            at = pl.multiple_of(jnp.bitwise_xor(me, origin) * local, local)
            all_scr[pl.ds(at, local), :] = piece[k].astype(F32)
    all_single = all_scr[:, :S].astype(BF16)
    all_parts = all_scr[:, S:].astype(BF16)
    own_single = pieces[0][0, :, :S]
    own_parts = pieces[0][0, :, S:]
    rows16, lanes16 = iota((16, 128), 0), iota((16, 128), 1)
    pick = ((lanes16 % 12 == rows16) & (lanes16 < 36)).astype(BF16)
    frames = nt_dot(pick, all_parts)
    own_frames = nt_dot(pick, own_parts)

    feats = nt_dot(wq_ref[FEAT : 2 * FEAT, :], all_single)
    points = nt_dot(wp_ref[QPTS:, :], all_single)
    for t in range(tiles):
        feat_scr[t] = feats[:, t * lane : (t + 1) * lane]
        pts_scr[t] = points[:, t * lane : (t + 1) * lane]
    qf_scr[...] = nt_dot(wq_ref[:FEAT, :], own_single)
    qp_scr[...] = nt_dot(wp_ref[:QPTS, :], own_single)

    def place(frame, triple):
        return [
            frame[3 * x : 3 * x + 1, :] * triple[0]
            + frame[3 * x + 1 : 3 * x + 2, :] * triple[1]
            + frame[3 * x + 2 : 3 * x + 3, :] * triple[2]
            + frame[9 + x : 10 + x, :]
            for x in range(3)
        ]

    key_feats = [strided(feat_scr, c, HEADS, CH) for c in range(CH)]
    query_feats = [qf_scr[pl.ds(c, HEADS, stride=CH), :] for c in range(CH)]
    key_pts, query_pts = [], []
    for p in range(QP):
        key_pts += place(frames, [strided(pts_scr, 3 * p + y, HEADS, 3 * QP) for y in range(3)])
        query_pts += place(
            own_frames, [qp_scr[pl.ds(3 * p + y, HEADS, stride=3 * QP), :] for y in range(3)]
        )

    def spread(index):
        return jnp.concatenate([heads_ref[index, :HEADS, :]] * max(1, n // 128), axis=1)[:, :n]

    point_scale, same_bias, cross_bias = spread(0), spread(1), spread(2)
    chain_row = rows_ref[0:1, :]
    lanes = iota((1, n), 1)
    for i in range(local):
        dots = sum(q[:, i : i + 1] * k for q, k in zip(query_feats, key_feats))
        distance = 0.0
        for q, k in zip(query_pts, key_pts):
            apart = q[:, i : i + 1] - k
            distance = distance + apart * apart
        mine = jnp.sum(jnp.where(lanes == me * local + i, chain_row, 0), axis=1, keepdims=True)
        chain = jnp.where(chain_row == mine, same_bias, cross_bias)
        base = WEIGHT_L * (dots * (1.0 / math.sqrt(CH)) + chain + point_scale * distance)
        base_ref[i] = jnp.concatenate([base, jnp.zeros((HPAD - HEADS, n), F32)], axis=0)

    planes = place(frames, [strided(pts_scr, QPTS + y, PLANE, 3) for y in range(3)])
    gap = jnp.zeros((n, 128 - PLANE), F32)
    values = [nt_dot(all_single, wq_ref[2 * FEAT :, :]), jnp.zeros((n, 256 - FEAT), F32)]
    for plane in planes:
        values += [plane.T, gap]
    high, low = split(jnp.concatenate(values, axis=1))
    value_ref[0] = high
    value_ref[1] = low


def attend_kernel(
    recv_ref,
    own_ref,
    base_ref,
    rows_ref,
    gains_ref,
    value_ref,
    w_swiglu_ref,
    w_down_ref,
    wb_ref,
    w_out_ref,
    w_loc_ref,
    out_ref,
    pair_scr,
    attn_scr,
    sums_scr,
):
    nsrc, local, _, _ = recv_ref.shape
    n = nsrc * local
    half = local * HPAD

    gain = gains_ref[0:1, S:]
    group = max(1, min(local, 512 // n))
    for start in range(0, local, group):
        block = recv_ref[:, start : start + group].astype(F32)
        block = jnp.concatenate([block[:, k].reshape(n, C) for k in range(group)], axis=0)
        done = transition(block, gain, w_swiglu_ref, w_down_ref)
        for k in range(group):
            pair_scr[start + k] = done[k * n : (k + 1) * n]

    bias = jnp.concatenate([nt_dot(wb_ref[...], pair_scr[i]) for i in range(local)], axis=0)
    real = jnp.broadcast_to(rows_ref[1:2, :], (half, n)) > 0
    scores = base_ref[...].reshape(half, n) + WEIGHT_L * bias
    scores = jnp.where(real, scores, -1000000000.0)
    expo = jnp.exp(scores - jnp.max(scores, axis=-1, keepdims=True))
    high, low = split(expo / jnp.sum(expo, axis=-1, keepdims=True))
    attn_scr[:half] = high
    attn_scr[half:] = low
    for i in range(local):
        at = i * HPAD
        sums_scr[at : at + HPAD, :] = jnp.dot(
            high[at : at + HPAD], pair_scr[i], preferred_element_type=F32
        )

    both = jnp.dot(attn_scr[...], value_ref[0], preferred_element_type=F32)
    every = both[:half] + both[half:]
    every += jnp.dot(attn_scr[:half], value_ref[1], preferred_element_type=F32)
    heads, lanes = iota((HPAD, WIDE), 0), iota((HPAD, WIDE), 1)
    owner = jnp.where(lanes < 256, lanes // CH, (lanes % 128) // VP)
    every = every.reshape(local, HPAD, WIDE)
    summed = jnp.sum(jnp.where((owner == heads)[None], every, 0.0), axis=1)

    parts = own_ref[:, S:].astype(F32)
    turned = parts[:, 0:12] + parts[:, 12:24] + parts[:, 24:36]
    shifted = [
        summed[:, 256 + 128 * x : 384 + 128 * x] - turned[:, 9 + x : 10 + x] for x in range(3)
    ]
    local_out = [
        turned[:, y : y + 1] * shifted[0]
        + turned[:, 3 + y : 4 + y] * shifted[1]
        + turned[:, 6 + y : 7 + y] * shifted[2]
        for y in range(3)
    ]
    lengths = jnp.sqrt(
        local_out[0] * local_out[0] + local_out[1] * local_out[1] + local_out[2] * local_out[2] + 1.0
    )
    update = jnp.dot(
        summed[:, :FEAT].astype(BF16), w_out_ref[:FEAT, :], preferred_element_type=F32
    )
    for y in range(3):
        update += jnp.dot(
            local_out[y][:, :PLANE].astype(BF16), w_loc_ref[y], preferred_element_type=F32
        )
    at = FEAT + 3 * PLANE
    update += jnp.dot(
        lengths[:, :PLANE].astype(BF16), w_out_ref[at : at + PLANE, :], preferred_element_type=F32
    )
    at += PLANE
    pair_total = jnp.concatenate(
        [sums_scr[pl.ds(h, local, stride=HPAD), :] for h in range(HEADS)], axis=1
    )
    update += jnp.dot(pair_total.astype(BF16), w_out_ref[at:, :], preferred_element_type=F32)
    own_single = own_ref[:, :S].astype(F32)
    out_ref[...] = layer_norm(own_single + update, gains_ref[0:1, :S]).astype(BF16)


def in_hbm(arrays):
    return [pltpu.with_memory_space_constraint(array, pltpu.HBM) for array in arrays]


def whole(memory=pltpu.VMEM):
    return pl.BlockSpec(memory_space=memory)


def params(mib):
    return pltpu.CompilerParams(vmem_limit_bytes=mib * MIB)


def gather_rows(rows, size):
    stack, origins, span = rows[None], [0], size
    while span > 4:
        span //= 4
        hops = [k * span for k in range(1, 4)]
        got = [stack] + [
            lax.ppermute(stack, "rows", [(i, i ^ hop) for i in range(size)]) for hop in hops
        ]
        stack = jnp.concatenate(got, axis=0)
        origins = [origin ^ hop for hop in [0] + hops for origin in origins]
    hops = list(range(1, span))
    got = [stack] + [
        lax.ppermute(stack, "rows", [(i, i ^ hop) for i in range(size)]) for hop in hops
    ]
    return got, [[origin ^ hop for origin in origins] for hop in [0] + hops]


def on_device(
    single_rep,
    pair_grid,
    frames,
    chain_ids,
    pad_mask,
    ln_pair_gain,
    w_swiglu,
    w_pair_down,
    w_bias,
    w_qkv,
    w_points,
    gamma_raw,
    chain_bias,
    w_out,
    ln_single_gain,
):
    n, local, _ = pair_grid.shape
    nsrc = n // local
    tiles = max(1, n // 128)
    large = 4 * (n // 128)

    own = pl.pallas_call(
        pack_kernel,
        out_shape=jax.ShapeDtypeStruct((local, S + 128), BF16),
        in_specs=[whole(pltpu.HBM), whole(pltpu.HBM)],
        out_specs=whole(),
        scratch_shapes=[
            pltpu.VMEM((local, S), BF16),
            pltpu.VMEM((local, 12), F32),
            pltpu.SemaphoreType.DMA((2,)),
        ],
        name="pack",
    )(*in_hbm([single_rep, frames.T]))
    pieces, offsets = gather_rows(own, nsrc)
    received = lax.all_to_all(
        pair_grid.reshape(nsrc, local, local, C), "rows", 0, 0, tiled=True
    )

    sources = [
        pair_grid,
        w_swiglu,
        w_pair_down,
        ln_pair_gain,
        gamma_raw,
        chain_bias,
        chain_ids,
        pad_mask,
        ln_single_gain,
        w_bias.T,
        w_out,
        w_qkv.T,
        w_points.T,
    ]
    held = [pltpu.VMEM(x.shape, x.dtype) for x in sources[:10]]
    held.append(pltpu.VMEM((3 * PLANE, S), BF16))
    pair_out, heads, rows, gains, wb, w_loc, wq, wp = pl.pallas_call(
        own_kernel,
        out_shape=[
            jax.ShapeDtypeStruct(pair_grid.shape, BF16),
            jax.ShapeDtypeStruct((3, HPAD, 128), F32),
            jax.ShapeDtypeStruct((2, n), jnp.int32),
            jax.ShapeDtypeStruct((1, S + C), F32),
            jax.ShapeDtypeStruct((HPAD, C), BF16),
            jax.ShapeDtypeStruct((3, PLANE, S), BF16),
            jax.ShapeDtypeStruct(sources[11].shape, BF16),
            jax.ShapeDtypeStruct(sources[12].shape, BF16),
        ],
        in_specs=[whole(pltpu.HBM)] * len(sources),
        out_specs=[whole()] * 8,
        scratch_shapes=held
        + [
            pltpu.VMEM((S // 128, 3 * PLANE, 128), F32),
            pltpu.SemaphoreType.DMA((len(sources),)),
        ],
        compiler_params=params(18 + large),
        name="own_transition",
    )(*in_hbm(sources))

    base, value = pl.pallas_call(
        lambda *refs: prepare_kernel(offsets, *refs),
        out_shape=[
            jax.ShapeDtypeStruct((local, HPAD, n), F32),
            jax.ShapeDtypeStruct((2, n, WIDE), BF16),
        ],
        in_specs=[whole()] * (len(pieces) + 4),
        out_specs=[whole()] * 2,
        scratch_shapes=[
            pltpu.VMEM((n, S + 128), F32),
            pltpu.VMEM((tiles, FEAT, n // tiles), F32),
            pltpu.VMEM((tiles, QPTS + 3 * PLANE, n // tiles), F32),
            pltpu.VMEM((FEAT, local), F32),
            pltpu.VMEM((QPTS, local), F32),
        ],
        compiler_params=params(12 + large),
        cost_estimate=pl.CostEstimate(flops=PREP_FLOPS, bytes_accessed=MIB, transcendentals=0),
        name="prepare",
    )(*pieces, heads, rows, wq, wp)

    single_out = pl.pallas_call(
        attend_kernel,
        out_shape=jax.ShapeDtypeStruct((local, S), BF16),
        in_specs=[whole()] * 11,
        out_specs=whole(),
        scratch_shapes=[
            pltpu.VMEM((local, n, C), BF16),
            pltpu.VMEM((2 * local * HPAD, n), BF16),
            pltpu.VMEM((local * HPAD, C), F32),
        ],
        compiler_params=params(16 + large),
        name="attend",
    )(received, own, base, rows, gains, value, w_swiglu, w_pair_down, wb, w_out, w_loc)
    return (single_out, pair_out)


def solution(mesh):
    placed = (
        P(("groups", "rows"), None),
        P("groups", "rows", None),
        P(None, ("groups", "rows")),
        P("groups"),
        P("groups"),
    ) + (P(),) * 10
    return jax.shard_map(
        on_device,
        mesh=mesh,
        in_specs=placed,
        out_specs=(P(("groups", "rows"), None), P("groups", "rows", None)),
        check_vma=False,
    )
```

time: 34.1 us -> 30.5 us (0.89)
  local copies, waits for them, and re-layouts: 14.9 us -> 0.33 us
  starting transfers between devices: 7.4 us -> 13.7 us
  waiting for transfers between devices: 1.6 us -> 5.57 us
  other arithmetic: 0 us -> 0.7 us
    unnamed x40 -> x8, local copies, waits for them, and re-layouts: 9.87 us -> 0.33 us
    ppermute x0 -> x6, starting transfers between devices: none -> 6.31 us  [gather_rows(): lax.ppermute(stack, 'rows', [(i, i ^ hop) for i in range(size)])]
    ppermute x0 -> x6, waiting for transfers between devices: none -> 5.57 us  [gather_rows(): lax.ppermute(stack, 'rows', [(i, i ^ hop) for i in range(size)])]
    reshape x4 -> x0, local copies, waits for them, and re-layouts: 3.8 us -> none  [the longest x2 1.81 us: on_device(): w_loc = jnp.transpose(w_out[FEAT:at].reshape(PLANE, 3, S), (1, 0, 2))]
    pallas_call x2 -> x3, Pallas kernels: 2.97 us -> 5.94 us  [the longest x1 3.44 us: on_device(): pl.pallas_call(own_kernel, out_shape=[jax.ShapeDtypeStruct(pair_grid.shap...]
    pallas_call x1, Pallas kernels: 5.88 us -> 3.14 us  [on_device(): pl.pallas_call(attend_kernel, out_shape=jax.ShapeDtypeStruct((local, S),...]
    all_to_all x1, waiting for transfers between devices: 1.6 us -> 0.01 us  [on_device(): lax.all_to_all(pair_grid.reshape(nsrc, local, local, C), 'rows', 0, 0, ti...]
    concatenate x0 -> x1, other arithmetic: none -> 0.7 us  [gather_rows(): stack = jnp.concatenate(got, axis=0)]
  transfers between devices with their start and end apart: 1 -> 7, of which waited for: 1 -> 3; matrix products, arithmetic and copies ran while one was open for 20% -> 2% of each run, Pallas kernels for 7% -> 20%
where the time goes in v2:
time: 30.5 us; the launch traced here: 30.1 us
  starting transfers between devices  13.7 us (45%)
  Pallas kernels  9.08 us (30%)
  waiting for transfers between devices  5.57 us (18%)
  between operations  0.73 us (2%)
  other arithmetic  0.7 us (2%)
  local copies, waits for them, and re-layouts  0.33 us (1%)
    all_to_all x1, starting transfers between devices, on_device(): lax.all_to_all(pair_grid.reshape(nsrc, local, local, C), 'rows', 0, 0, ti...  7.4 us
    ppermute x6, starting transfers between devices, gather_rows(): lax.ppermute(stack, 'rows', [(i, i ^ hop) for i in range(size)])  6.31 us
    ppermute x6, waiting for transfers between devices, gather_rows(): lax.ppermute(stack, 'rows', [(i, i ^ hop) for i in range(size)])  5.57 us
    pallas_call x1, Pallas kernels, on_device(): pl.pallas_call(own_kernel, out_shape=[jax.ShapeDtypeStruct(pair_grid.shap...  3.44 us
    pallas_call x1, Pallas kernels, on_device(): pl.pallas_call(attend_kernel, out_shape=jax.ShapeDtypeStruct((local, S),...  3.14 us
    pallas_call x1, Pallas kernels, on_device(): pl.pallas_call(pack_kernel, out_shape=jax.ShapeDtypeStruct((local, S + 12...  1.4 us
    pallas_call x1, Pallas kernels, on_device(): pl.pallas_call(lambda *refs: prepare_kernel(offsets, *refs), out_shape=[j...  1.1 us
    concatenate x1, other arithmetic, gather_rows(): stack = jnp.concatenate(got, axis=0)  0.7 us
  transfers between devices with their start and end apart: 7, of which 3 were waited for; matrix products, arithmetic and copies ran while one was open for 2% of the time, Pallas kernels for 20%

profile of v2, /device:TPU:0, one launch (start us, length us, event | category | flops | bytes accessed | tf_op | source)
XLA Modules:
  0.0 30.1 jit_solution(8439826652900435494)
XLA Ops:
  0.6 7.4 %all-to-all-start = ((bf16[16,8,8,128]{3,2,1,0:T(8,128)(2,1)}), bf16[16,8,8,128]{3,2,1,0:T(8,128)(2,1)S(1)}, u32[]{:S(2)}, u32[]{:S(2)}) async-start(bf16[16,8,8,128]{3,2,1,0:T(8,128)(2,1)} %bitcast.10), calls=%async_computation | async-start | bytes 524288 | tf_op jit(solution)/shard_map/all_to_all | solution.py:369
  8.0 1.4 %pack.1.own_ref = bf16[8,512]{1,0:T(8,128)(2,1)} custom-call(bf16[8,384]{1,0:T(8,128)(2,1)} %single_hbm.1, f32[8,12]{1,0:T(8,128)} %bitcast.14), custom_call_target="tpu_custom_call" | custom-call | tf_op jit(solution)/shard_map/pack/pallas_call | solution.py:356
  9.4 2.0 %collective-permute-start = (bf16[1,8,512]{2,1,0:T(8,128)(2,1)}, bf16[1,8,512]{2,1,0:T(8,128)(2,1)S(1)}, u32[]{:S(2)}, u32[]{:S(2)}) collective-permute-start(bf16[1,8,512]{2,1,0:T(8,128)(2,1)} %bitcast.6), channel_id=1, source_target_pairs={{0,4},{1,5},{2,6},{3,7},{4,0},{5,1},{6,2},{7,3},{8,12},{9,13},{10,... | collective-permute-start | bytes 24584 | tf_op jit(solution)/shard_map/ppermute | solution.py:323
  11.4 2.4 %collective-permute-start.1 = (bf16[1,8,512]{2,1,0:T(8,128)(2,1)}, bf16[1,8,512]{2,1,0:T(8,128)(2,1)S(1)}, u32[]{:S(2)}, u32[]{:S(2)}) collective-permute-start(bf16[1,8,512]{2,1,0:T(8,128)(2,1)} %bitcast.7), channel_id=1, source_target_pairs={{0,8},{1,9},{2,10},{3,11},{4,12},{5,13},{6,14},{7,15},{8,0},{9,1},... | collective-permute-start | bytes 24584 | tf_op jit(solution)/shard_map/ppermute | solution.py:323
  13.8 0.1 collective-permute-start.2
  13.9 0.1 collective-permute-done
  13.9 4.3 %collective-permute-done.1 = bf16[1,8,512]{2,1,0:T(8,128)(2,1)S(1)} collective-permute-done((bf16[1,8,512]{2,1,0:T(8,128)(2,1)}, bf16[1,8,512]{2,1,0:T(8,128)(2,1)S(1)}, u32[]{:S(2)}, u32[]{:S(2)}) %collective-permute-start.1) | collective-permute-done | bytes 8224 | tf_op jit(solution)/shard_map/ppermute | solution.py:323
  18.2 1.2 %collective-permute-done.2 = bf16[1,8,512]{2,1,0:T(8,128)(2,1)S(1)} collective-permute-done((bf16[1,8,512]{2,1,0:T(8,128)(2,1)}, bf16[1,8,512]{2,1,0:T(8,128)(2,1)S(1)}, u32[]{:S(2)}, u32[]{:S(2)}) %collective-permute-start.2) | collective-permute-done | bytes 8224 | tf_op jit(solution)/shard_map/ppermute | solution.py:323
  19.5 0.7 %pad_maximum_fusion.refs_0_ = bf16[4,8,512]{2,1,0:T(8,128)(2,1)S(1)} fusion(bf16[1,8,512]{2,1,0:T(8,128)(2,1)S(1)} %collective-permute-done.2, bf16[1,8,512]{2,1,0:T(8,128)(2,1)S(1)} %collective-permute-done.1, bf16[1,8,512]{2,1,0:T(8,128)(2,1)S(1)} %collective-permute-done, bf16[1,8,512]{2,1,0:T(8,128)(2,1)} %bitcast.9), kind=kLoop, calls=%fused_computation | loop fusion | flops 49152 | bytes 65536 | tf_op jit(solution)/shard_map/concatenate | solution.py:325
  20.2 0.0 collective-permute-start.3
  20.2 1.5 %collective-permute-start.4 = (bf16[4,8,512]{2,1,0:T(8,128)(2,1)S(1)}, bf16[4,8,512]{2,1,0:T(8,128)(2,1)S(1)}, u32[]{:S(2)}, u32[]{:S(2)}) collective-permute-start(bf16[4,8,512]{2,1,0:T(8,128)(2,1)S(1)} %pad_maximum_fusion.refs_0_), channel_id=1, source_target_pairs={{0,2},{1,3},{2,0},{3,1},{4,6},{5,7},{6,4},{7,5},{8,10},{9,11},{10,... | collective-permute-start | bytes 98312 | tf_op jit(solution)/shard_map/ppermute | solution.py:329
  21.7 0.3 %collective-permute-start.5 = (bf16[4,8,512]{2,1,0:T(8,128)(2,1)S(1)}, bf16[4,8,512]{2,1,0:T(8,128)(2,1)S(1)}, u32[]{:S(2)}, u32[]{:S(2)}) collective-permute-start(bf16[4,8,512]{2,1,0:T(8,128)(2,1)S(1)} %pad_maximum_fusion.refs_0_), channel_id=1, source_target_pairs={{0,3},{1,2},{2,1},{3,0},{4,7},{5,6},{6,5},{7,4},{8,11},{9,10},{10,... | collective-permute-start | bytes 98312 | tf_op jit(solution)/shard_map/ppermute | solution.py:329
  22.0 3.4 %own_transition.1 = (bf16[128,8,128]{2,1,0:T(8,128)(2,1)}, f32[3,16,128]{2,1,0:T(8,128)S(1)}, s32[2,128]{1,0:T(2,128)S(1)}, f32[1,512]{1,0:T(1,128)S(1)}, bf16[1...) custom-call(bf16[128,8,128]{2,1,0:T(8,128)(2,1)} %refs_0_.1, ...), custom_call_target="tpu_custom_call" | custom-call | tf_op jit(solution)/shard_map/own_transition/pallas_call | solution.py:390
  25.5 0.0 collective-permute-done.3.refs_1_
  25.5 0.0 collective-permute-done.4.refs_2_
  25.5 0.0 collective-permute-done.5.refs_3_
  25.5 0.0 copy-start
  25.5 0.0 copy-start.1
  25.5 0.0 copy-start.2
  25.5 0.0 copy-start.3
  25.5 1.1 %prepare.1 = (f32[8,16,128]{2,1,0:T(8,128)S(1)}, bf16[2,128,640]{2,1,0:T(8,128)(2,1)S(1)}) custom-call(bf16[4,8,512]{2,1,0:T(8,128)(2,1)S(1)} %pad_maximum_fusion.refs_0_, bf16[4,8,512]{2,1,0:T(8,128)(2,1)S(1)} %collective-permute-done.3.refs_1_, bf16[4,8,512]{2,1,0:T(8,128)(2,1)S(1)} %collective-permute-done.4.refs_2_, ...), custom_call_target="tpu_custom_call" | custom-call | flops 1000000000 | bytes 1048576 | tf_op jit(solution)/shard_map/prepare/pallas_call | solution.py:413
  26.7 0.0 all-to-all-done.recv_ref
  26.7 0.3 copy-done
  26.9 0.0 copy-done.1
  26.9 0.0 copy-done.2
  27.0 0.0 copy-done.3
  27.0 3.1 %attend.1 = bf16[8,384]{1,0:T(8,128)(2,1)} custom-call(bf16[16,8,8,128]{3,2,1,0:T(8,128)(2,1)S(1)} %all-to-all-done.recv_ref, bf16[8,512]{1,0:T(8,128)(2,1)S(1)} %copy-done.3, f32[8,16,128]{2,1,0:T(8,128)S(1)} %get-tuple-element.16.base_ref, s32[2,128]{1,0:T(2,128)S(1)} %get-tuple-element.13.refs_5_.rows_ref, f32[1,512]{1,0:T(1,128)S(1)} %get-tuple-element.17.gains_ref, ...), custom_call_target="tpu_custom_call" | custom-call | tf_op jit(solution)/shard_map/attend/pallas_call | solution.py:433
Async XLA Ops:
  0.6 26.0 %all-to-all-start = ((bf16[16,8,8,128]{3,2,1,0:T(8,128)(2,1)}), bf16[16,8,8,128]{3,2,1,0:T(8,128)(2,1)S(1)}, u32[]{:S(2)}, u32[]{:S(2)}) async-start(bf16[16,8,8,128]{3,2,1,0:T(8,128)(2,1)} %bitcast.10), calls=%async_computation | async-start | bytes 524288 | tf_op jit(solution)/shard_map/all_to_all | solution.py:369
  9.4 4.5 %collective-permute-start = (bf16[1,8,512]{2,1,0:T(8,128)(2,1)}, bf16[1,8,512]{2,1,0:T(8,128)(2,1)S(1)}, u32[]{:S(2)}, u32[]{:S(2)}) collective-permute-start(bf16[1,8,512]{2,1,0:T(8,128)(2,1)} %bitcast.6), channel_id=1, source_target_pairs={{0,4},{1,5},{2,6},{3,7},{4,0},{5,1},{6,2},{7,3},{8,12},{9,13},{10,... | collective-permute-start | bytes 24584 | tf_op jit(solution)/shard_map/ppermute | solution.py:323
  11.4 6.8 %collective-permute-start.1 = (bf16[1,8,512]{2,1,0:T(8,128)(2,1)}, bf16[1,8,512]{2,1,0:T(8,128)(2,1)S(1)}, u32[]{:S(2)}, u32[]{:S(2)}) collective-permute-start(bf16[1,8,512]{2,1,0:T(8,128)(2,1)} %bitcast.7), channel_id=1, source_target_pairs={{0,8},{1,9},{2,10},{3,11},{4,12},{5,13},{6,14},{7,15},{8,0},{9,1},... | collective-permute-start | bytes 24584 | tf_op jit(solution)/shard_map/ppermute | solution.py:323
  13.8 5.7 %collective-permute-start.2 = (bf16[1,8,512]{2,1,0:T(8,128)(2,1)}, bf16[1,8,512]{2,1,0:T(8,128)(2,1)S(1)}, u32[]{:S(2)}, u32[]{:S(2)}) collective-permute-start(bf16[1,8,512]{2,1,0:T(8,128)(2,1)} %bitcast.8), channel_id=1, source_target_pairs={{0,12},{1,13},{2,14},{3,15},{4,8},{5,9},{6,10},{7,11},{8,4},{9,5},... | collective-permute-start | bytes 24584 | tf_op jit(solution)/shard_map/ppermute | solution.py:323
  20.2 5.3 %collective-permute-start.3 = (bf16[4,8,512]{2,1,0:T(8,128)(2,1)S(1)}, bf16[4,8,512]{2,1,0:T(8,128)(2,1)S(1)}, u32[]{:S(2)}, u32[]{:S(2)}) collective-permute-start(bf16[4,8,512]{2,1,0:T(8,128)(2,1)S(1)} %pad_maximum_fusion.refs_0_), channel_id=1, source_target_pairs={{0,1},{1,0},{2,3},{3,2},{4,5},{5,4},{6,7},{7,6},{8,9},{9,8},{10,11... | collective-permute-start | bytes 98312 | tf_op jit(solution)/shard_map/ppermute | solution.py:329
  20.2 5.3 %collective-permute-start.4 = (bf16[4,8,512]{2,1,0:T(8,128)(2,1)S(1)}, bf16[4,8,512]{2,1,0:T(8,128)(2,1)S(1)}, u32[]{:S(2)}, u32[]{:S(2)}) collective-permute-start(bf16[4,8,512]{2,1,0:T(8,128)(2,1)S(1)} %pad_maximum_fusion.refs_0_), channel_id=1, source_target_pairs={{0,2},{1,3},{2,0},{3,1},{4,6},{5,7},{6,4},{7,5},{8,10},{9,11},{10,... | collective-permute-start | bytes 98312 | tf_op jit(solution)/shard_map/ppermute | solution.py:329
  21.7 3.8 %collective-permute-start.5 = (bf16[4,8,512]{2,1,0:T(8,128)(2,1)S(1)}, bf16[4,8,512]{2,1,0:T(8,128)(2,1)S(1)}, u32[]{:S(2)}, u32[]{:S(2)}) collective-permute-start(bf16[4,8,512]{2,1,0:T(8,128)(2,1)S(1)} %pad_maximum_fusion.refs_0_), channel_id=1, source_target_pairs={{0,3},{1,2},{2,1},{3,0},{4,7},{5,6},{6,5},{7,4},{8,11},{9,10},{10,... | collective-permute-start | bytes 98312 | tf_op jit(solution)/shard_map/ppermute | solution.py:329
  25.5 1.4 %copy-start = (bf16[2112,384]{1,0:T(8,128)(2,1)S(1)}, bf16[2112,384]{1,0:T(8,128)(2,1)}, u32[]{:S(2)}) copy-start(bf16[2112,384]{1,0:T(8,128)(2,1)} %w_out_ref.1) | copy-start | bytes 4866052
  25.5 1.4 %copy-start.1 = (bf16[128,1024]{1,0:T(8,128)(2,1)S(1)}, bf16[128,1024]{1,0:T(8,128)(2,1)}, u32[]{:S(2)}) copy-start(bf16[128,1024]{1,0:T(8,128)(2,1)} %w_swiglu_ref.1) | copy-start | bytes 786436
  25.5 1.4 %copy-start.2 = (bf16[512,128]{1,0:T(8,128)(2,1)S(1)}, bf16[512,128]{1,0:T(8,128)(2,1)}, u32[]{:S(2)}) copy-start(bf16[512,128]{1,0:T(8,128)(2,1)} %w_down_ref.1) | copy-start | bytes 393220
  25.5 1.4 %copy-start.3 = (bf16[8,512]{1,0:T(8,128)(2,1)S(1)}, bf16[8,512]{1,0:T(8,128)(2,1)}, u32[]{:S(2)}) copy-start(bf16[8,512]{1,0:T(8,128)(2,1)} %pack.1.own_ref) | copy-start | bytes 24580

commit v3 on v2

v3 whole, which is shorter than its diff:
```python
import math

import jax
import jax.numpy as jnp
from jax import lax
from jax.experimental import pallas as pl
from jax.experimental.pallas import tpu as pltpu
from jax.sharding import PartitionSpec as P

C = 128
S = 384
H = 512
HEADS = 12
CH = 16
QP = 4
VP = 8
HPAD = 16
FEAT = HEADS * CH
QPTS = HEADS * QP * 3
PLANE = HEADS * VP
WIDE = 256 + 3 * 128
SMALL = S // 128 + 1
PARTS = HEADS + 2 * (WIDE // 128) + 1
F32 = jnp.float32
BF16 = jnp.bfloat16
NT = (((1,), (1,)), ((), ()))
MIB = 1024 * 1024
WEIGHT_L = math.sqrt(1.0 / 3.0)
WEIGHT_C = math.sqrt(2.0 / (9.0 * QP))


def iota(shape, dim):
    return lax.broadcasted_iota(jnp.int32, shape, dim)


def nt_dot(a, b):
    return lax.dot_general(a, b, NT, preferred_element_type=F32)


def layer_norm(values, gain):
    centre = jnp.mean(values, axis=-1, keepdims=True)
    centred = values - centre
    spread = jnp.mean(centred * centred, axis=-1, keepdims=True)
    return centred * lax.rsqrt(spread + 1e-05) * gain


def transition(values, gain, w_swiglu_ref, w_down_ref):
    normed = layer_norm(values, gain).astype(BF16)
    both = jnp.dot(normed, w_swiglu_ref[...], preferred_element_type=F32)
    gate = 0.5 * both[:, :H]
    hidden = (gate * (1.0 + jnp.tanh(gate)) * both[:, H:]).astype(BF16)
    update = jnp.dot(hidden, w_down_ref[...], preferred_element_type=F32)
    return (values + update).astype(BF16)


def split(values):
    high = values.astype(BF16)
    return high, (values - high.astype(F32)).astype(BF16)


def pack_kernel(pair_hbm, single_hbm, frames_hbm, out_ref, own_ref, frames_ref, sems):
    local = own_ref.shape[0]
    copies = [
        pltpu.make_async_copy(single_hbm, own_ref.at[:, :S], sems.at[0]),
        pltpu.make_async_copy(frames_hbm, frames_ref, sems.at[1]),
    ]
    for half in range(2):
        copies.append(
            pltpu.make_async_copy(
                pair_hbm.at[half], out_ref.at[:, pl.ds(half * local, local)], sems.at[2 + half]
            )
        )
    for copy in copies:
        copy.start()
    copies[0].wait()
    copies[1].wait()
    rows = frames_ref[...]
    blank = jnp.zeros((local, 128 - 36), F32)
    turned = jnp.concatenate([rows, rows, rows, blank], axis=1)
    high = turned.astype(BF16).astype(F32)
    middle = (turned - high).astype(BF16).astype(F32)
    low = turned - high - middle
    lane = iota(turned.shape, 1)
    own_ref[:, S:] = jnp.where(lane < 12, high, jnp.where(lane < 24, middle, low)).astype(BF16)
    for dest in range(out_ref.shape[0]):
        for piece in range(SMALL):
            out_ref[dest, 2 * local + piece] = own_ref[:, piece * 128 : piece * 128 + 128]
    copies[2].wait()
    copies[3].wait()


def strided(ref, start, count, stride):
    return jnp.concatenate(
        [ref[t, pl.ds(start, count, stride=stride), :] for t in range(ref.shape[0])], axis=1
    )


def own_kernel(*refs):
    sources, refs = refs[:13], refs[13:]
    out_ref, heads_ref, rows_ref, gains_ref, wb_out_ref, w_loc_ref, wq_ref, wp_ref = refs[:8]
    held, refs = refs[8:19], refs[19:]
    loc_scr, sems = refs
    pair_hbm, *_ = sources
    n, local, _ = pair_hbm.shape
    targets = list(held) + [wq_ref, wp_ref]
    copies = []
    for k, (source, target) in enumerate(zip(sources, targets)):
        if k == 10:
            source = source.at[pl.ds(FEAT, 3 * PLANE)]
        copies.append(pltpu.make_async_copy(source, target, sems.at[k]))
        copies[k].start()
    pair_ref, w_swiglu_ref, w_down_ref, gain_ref, gamma_ref, cb_ref = held[:6]
    chain_ref, pad_ref, gain2_ref, wb_ref, loc_ref = held[6:]
    for copy in copies[:4]:
        copy.wait()
    gain = gain_ref[...].reshape(1, C)
    block = math.gcd(n, 128)

    def step(at):
        values = pair_ref[pl.ds(at, block)].astype(F32).reshape(-1, C)
        done = transition(values, gain, w_swiglu_ref, w_down_ref)
        out_ref[pl.ds(at, block)] = done.astype(F32).reshape(-1, local, C).astype(BF16)

    if n == block:
        step(0)
    else:
        pl.loop(0, n, step=block)(step)
    for copy in copies[4:]:
        copy.wait()

    diagonal = iota((HPAD, HEADS), 0) == iota((HPAD, HEADS), 1)

    def column(row):
        turned = jnp.sum(jnp.where(diagonal, row, 0.0), axis=1, keepdims=True)
        return jnp.broadcast_to(turned, (HPAD, 128))

    gamma = jax.nn.softplus(gamma_ref[...].reshape(1, HEADS))
    heads_ref[0] = column(gamma * (-0.5 * WEIGHT_C))
    heads_ref[1] = column(cb_ref[0:1, :])
    heads_ref[2] = column(cb_ref[1:2, :])
    rows_ref[0:1, :] = chain_ref[...].reshape(1, n)
    rows_ref[1:2, :] = pad_ref[...].reshape(1, n)
    gains_ref[0:1, :S] = gain2_ref[...].reshape(1, S)
    gains_ref[0:1, S:] = gain
    wb_out_ref[...] = jnp.concatenate(
        [wb_ref[...], jnp.zeros((HPAD - HEADS, C), BF16)], axis=0
    )
    local_rows = loc_ref[...].astype(F32)
    for t in range(S // 128):
        loc_scr[t] = local_rows[:, t * 128 : (t + 1) * 128]
    for y in range(3):
        w_loc_ref[y] = strided(loc_scr, y, PLANE, 3).astype(BF16)


def place(frame, triple):
    return [
        frame[3 * x : 3 * x + 1, :] * triple[0]
        + frame[3 * x + 1 : 3 * x + 2, :] * triple[1]
        + frame[3 * x + 2 : 3 * x + 3, :] * triple[2]
        + frame[9 + x : 10 + x, :]
        for x in range(3)
    ]


def head_of_lane(rows):
    lanes = iota((rows, WIDE), 1)
    return jnp.where(lanes < 256, lanes // CH, (lanes % 128) // VP)


def partial_attention(
    recv_ref, at, base, real, high_value, low_value, gain, w_swiglu_ref, w_down_ref, wb_ref,
    pair_scr, attn_scr, sums_scr,
):
    nsrc, _, local, _ = recv_ref.shape
    n = nsrc * local
    rows = local * HPAD
    group = max(1, min(local, 512 // n))
    for start in range(0, local, group):
        block = recv_ref[:, pl.ds(at + start, group)].astype(F32)
        block = jnp.concatenate([block[:, k].reshape(n, C) for k in range(group)], axis=0)
        done = transition(block, gain, w_swiglu_ref, w_down_ref)
        for k in range(group):
            pair_scr[start + k] = done[k * n : (k + 1) * n]
    bias = jnp.concatenate([nt_dot(wb_ref[...], pair_scr[i]) for i in range(local)], axis=0)
    scores = base + WEIGHT_L * bias
    scores = jnp.where(jnp.broadcast_to(real, (rows, n)) > 0, scores, -1000000000.0)
    peak = jnp.max(scores, axis=-1, keepdims=True)
    expo = jnp.exp(scores - peak)
    total = jnp.sum(expo, axis=-1, keepdims=True)
    high, low = split(expo / total)
    attn_scr[:rows] = high
    attn_scr[rows:] = low
    for i in range(local):
        first = i * HPAD
        sums_scr[first : first + HPAD, :] = jnp.dot(
            high[first : first + HPAD], pair_scr[i], preferred_element_type=F32
        )
    both = jnp.dot(attn_scr[...], high_value, preferred_element_type=F32)
    every = both[:rows] + both[rows:]
    every += jnp.dot(attn_scr[:rows], low_value, preferred_element_type=F32)
    owned = head_of_lane(HPAD) == iota((HPAD, WIDE), 0)
    every = every.reshape(local, HPAD, WIDE)
    summed = jnp.sum(jnp.where(owned[None], every, 0.0), axis=1)
    diagonal = (iota((HPAD, HPAD), 0) == iota((HPAD, HPAD), 1))[None]

    def by_head(column):
        wide = jnp.broadcast_to(column.reshape(local, HPAD, 1), (local, HPAD, HPAD))
        return jnp.sum(jnp.where(diagonal, wide, 0.0), axis=1)

    pair_sums = [sums_scr[pl.ds(h, local, stride=HPAD), :] for h in range(HEADS)]
    return pair_sums, summed, by_head(peak), by_head(total)


def first_kernel(
    recv_ref,
    own_ref,
    partner_ref,
    heads_ref,
    rows_ref,
    gains_ref,
    wq_ref,
    wp_ref,
    wb_ref,
    w_swiglu_ref,
    w_down_ref,
    send_ref,
    base_ref,
    value_ref,
    real_ref,
    feat_scr,
    pts_scr,
    qf_scr,
    qp_scr,
    pair_scr,
    attn_scr,
    sums_scr,
):
    nsrc, _, local, _ = recv_ref.shape
    tiles, _, lane = feat_scr.shape
    n = nsrc * local
    me = lax.axis_index("rows")
    upper = me // nsrc

    def piece(index):
        return recv_ref[:, index].astype(F32).reshape(n, 128).astype(BF16)

    all_single = jnp.concatenate([piece(2 * local + k) for k in range(SMALL - 1)], axis=1)
    queries = jnp.concatenate(
        [partner_ref[...].astype(F32), own_ref[...].astype(F32)], axis=0
    ).astype(BF16)
    rows16, lanes16 = iota((16, 128), 0), iota((16, 128), 1)
    pick = ((lanes16 % 12 == rows16) & (lanes16 < 36)).astype(BF16)
    frames = nt_dot(pick, piece(2 * local + SMALL - 1))
    query_frames = nt_dot(pick, queries[:, S:])

    feats = nt_dot(wq_ref[FEAT : 2 * FEAT, :], all_single)
    points = nt_dot(wp_ref[QPTS:, :], all_single)
    for t in range(tiles):
        feat_scr[t] = feats[:, t * lane : (t + 1) * lane]
        pts_scr[t] = points[:, t * lane : (t + 1) * lane]
    qf_scr[...] = nt_dot(wq_ref[:FEAT, :], queries[:, :S])
    qp_scr[...] = nt_dot(wp_ref[:QPTS, :], queries[:, :S])

    key_feats = [strided(feat_scr, c, HEADS, CH) for c in range(CH)]
    query_feats = [qf_scr[pl.ds(c, HEADS, stride=CH), :] for c in range(CH)]
    key_pts, query_pts = [], []
    for p in range(QP):
        key_pts += place(frames, [strided(pts_scr, 3 * p + y, HEADS, 3 * QP) for y in range(3)])
        query_pts += place(
            query_frames, [qp_scr[pl.ds(3 * p + y, HEADS, stride=3 * QP), :] for y in range(3)]
        )

    def spread(index):
        return jnp.concatenate([heads_ref[index, :HEADS, :]] * max(1, n // 128), axis=1)[:, :n]

    point_scale, same_bias, cross_bias = spread(0), spread(1), spread(2)
    chain_all = rows_ref[0:1, :]
    chain_row = jnp.where(upper == 0, chain_all[:, :n], chain_all[:, n:])
    real = jnp.where(upper == 0, rows_ref[1:2, :n], rows_ref[1:2, n:])
    real_ref[...] = real
    lanes = iota((1, 2 * n), 1)
    starts = [jnp.bitwise_xor(me, nsrc) * local, me * local]
    bases = []
    for i in range(2 * local):
        dots = sum(q[:, i : i + 1] * k for q, k in zip(query_feats, key_feats))
        distance = 0.0
        for q, k in zip(query_pts, key_pts):
            apart = q[:, i : i + 1] - k
            distance = distance + apart * apart
        at = starts[i // local] + i % local
        mine = jnp.sum(jnp.where(lanes == at, chain_all, 0), axis=1, keepdims=True)
        chain = jnp.where(chain_row == mine, same_bias, cross_bias)
        base = WEIGHT_L * (dots * (1.0 / math.sqrt(CH)) + chain + point_scale * distance)
        base = jnp.concatenate([base, jnp.zeros((HPAD - HEADS, n), F32)], axis=0)
        if i < local:
            bases.append(base)
        else:
            base_ref[(i - local) * HPAD : (i - local + 1) * HPAD, :] = base

    planes = place(frames, [strided(pts_scr, QPTS + y, PLANE, 3) for y in range(3)])
    gap = jnp.zeros((n, 128 - PLANE), F32)
    values = [nt_dot(all_single, wq_ref[2 * FEAT :, :]), jnp.zeros((n, 256 - FEAT), F32)]
    for plane in planes:
        values += [plane.T, gap]
    high, low = split(jnp.concatenate(values, axis=1))
    value_ref[0] = high
    value_ref[1] = low

    pair_sums, summed, peak, total = partial_attention(
        recv_ref, (1 - upper) * local, jnp.concatenate(bases, axis=0), real, high, low,
        gains_ref[0:1, S:], w_swiglu_ref, w_down_ref, wb_ref, pair_scr, attn_scr, sums_scr,
    )
    for h in range(HEADS):
        send_ref[h] = pair_sums[h].astype(BF16)
    high, low = split(summed)
    pieces = WIDE // 128
    for k in range(pieces):
        send_ref[HEADS + k] = high[:, k * 128 : (k + 1) * 128]
        send_ref[HEADS + pieces + k] = low[:, k * 128 : (k + 1) * 128]
    both = jnp.concatenate([peak, total], axis=1)
    high = both.astype(BF16).astype(F32)
    middle = (both - high).astype(BF16).astype(F32)
    low = both - high - middle
    blank = jnp.zeros((local, 128 - 6 * HPAD), F32)
    send_ref[PARTS - 1] = jnp.concatenate([high, middle, low, blank], axis=1).astype(BF16)


def second_kernel(
    recv_ref,
    base_ref,
    value_ref,
    real_ref,
    gains_ref,
    wb_ref,
    w_swiglu_ref,
    w_down_ref,
    sums_ref,
    wide_ref,
    stats_ref,
    pair_scr,
    attn_scr,
    sums_scr,
):
    nsrc, _, local, _ = recv_ref.shape
    upper = lax.axis_index("rows") // nsrc
    pair_sums, summed, peak, total = partial_attention(
        recv_ref, upper * local, base_ref[...], real_ref[...], value_ref[0], value_ref[1],
        gains_ref[0:1, S:], w_swiglu_ref, w_down_ref, wb_ref, pair_scr, attn_scr, sums_scr,
    )
    for h in range(HEADS):
        sums_ref[h] = pair_sums[h]
    wide_ref[...] = summed
    stats_ref[...] = jnp.concatenate([peak, total], axis=1)


def finish_kernel(
    got_ref,
    sums_ref,
    wide_ref,
    stats_ref,
    own_ref,
    gains_ref,
    w_out_ref,
    w_loc_ref,
    out_ref,
):
    local = own_ref.shape[0]
    got = got_ref[PARTS - 1].astype(F32)
    width = 2 * HPAD
    got = got[:, :width] + got[:, width : 2 * width] + got[:, 2 * width : 3 * width]
    mine = stats_ref[...]
    peak = jnp.maximum(got[:, :HPAD], mine[:, :HPAD])
    got = got[:, HPAD:] * jnp.exp(got[:, :HPAD] - peak)
    mine = mine[:, HPAD:] * jnp.exp(mine[:, :HPAD] - peak)
    scale = 1.0 / (got + mine)
    got, mine = got * scale, mine * scale
    owner = head_of_lane(local)
    got_wide = jnp.zeros((local, WIDE), F32)
    mine_wide = jnp.zeros((local, WIDE), F32)
    pair_total = []
    for h in range(HEADS):
        got_share, mine_share = got[:, h : h + 1], mine[:, h : h + 1]
        got_wide = jnp.where(owner == h, got_share, got_wide)
        mine_wide = jnp.where(owner == h, mine_share, mine_wide)
        pair_total.append(got_share * got_ref[h].astype(F32) + mine_share * sums_ref[h])
    pieces = WIDE // 128
    sent = jnp.concatenate(
        [
            got_ref[HEADS + k].astype(F32) + got_ref[HEADS + pieces + k].astype(F32)
            for k in range(pieces)
        ],
        axis=1,
    )
    summed = got_wide * sent + mine_wide * wide_ref[...]

    parts = own_ref[:, S:].astype(F32)
    turned = parts[:, 0:12] + parts[:, 12:24] + parts[:, 24:36]
    shifted = [
        summed[:, 256 + 128 * x : 384 + 128 * x] - turned[:, 9 + x : 10 + x] for x in range(3)
    ]
    local_out = [
        turned[:, y : y + 1] * shifted[0]
        + turned[:, 3 + y : 4 + y] * shifted[1]
        + turned[:, 6 + y : 7 + y] * shifted[2]
        for y in range(3)
    ]
    lengths = jnp.sqrt(
        local_out[0] * local_out[0] + local_out[1] * local_out[1] + local_out[2] * local_out[2] + 1.0
    )
    update = jnp.dot(
        summed[:, :FEAT].astype(BF16), w_out_ref[:FEAT, :], preferred_element_type=F32
    )
    for y in range(3):
        update += jnp.dot(
            local_out[y][:, :PLANE].astype(BF16), w_loc_ref[y], preferred_element_type=F32
        )
    at = FEAT + 3 * PLANE
    update += jnp.dot(
        lengths[:, :PLANE].astype(BF16), w_out_ref[at : at + PLANE, :], preferred_element_type=F32
    )
    at += PLANE
    pair_total = jnp.concatenate(pair_total, axis=1).astype(BF16)
    update += jnp.dot(pair_total, w_out_ref[at:, :], preferred_element_type=F32)
    own_single = own_ref[:, :S].astype(F32)
    out_ref[...] = layer_norm(own_single + update, gains_ref[0:1, :S]).astype(BF16)


def in_hbm(arrays):
    return [pltpu.with_memory_space_constraint(array, pltpu.HBM) for array in arrays]


def whole(memory=pltpu.VMEM):
    return pl.BlockSpec(memory_space=memory)


def params(mib):
    return pltpu.CompilerParams(vmem_limit_bytes=mib * MIB)


def on_device(
    single_rep,
    pair_grid,
    frames,
    chain_ids,
    pad_mask,
    ln_pair_gain,
    w_swiglu,
    w_pair_down,
    w_bias,
    w_qkv,
    w_points,
    gamma_raw,
    chain_bias,
    w_out,
    ln_single_gain,
):
    n, local, _ = pair_grid.shape
    size = n // local
    nsrc = size // 2
    near = n // 2
    tiles = max(1, near // 128)
    large = 4 * (n // 128)
    halves = [list(range(nsrc)), list(range(nsrc, size))]
    across = [(i, i ^ nsrc) for i in range(size)]

    packed, own = pl.pallas_call(
        pack_kernel,
        out_shape=[
            jax.ShapeDtypeStruct((nsrc, 2 * local + SMALL, local, C), BF16),
            jax.ShapeDtypeStruct((local, S + 128), BF16),
        ],
        in_specs=[whole(pltpu.HBM)] * 3,
        out_specs=[whole(), whole()],
        scratch_shapes=[
            pltpu.VMEM((local, 12), F32),
            pltpu.SemaphoreType.DMA((4,)),
        ],
        compiler_params=params(4 + large),
        name="pack",
    )(*in_hbm([pair_grid.reshape(2, nsrc, local, local, C), single_rep, frames.T]))
    received = lax.all_to_all(
        packed, "rows", 0, 0, tiled=True, axis_index_groups=halves
    )
    partner = lax.ppermute(own, "rows", across)

    sources = [
        pair_grid,
        w_swiglu,
        w_pair_down,
        ln_pair_gain,
        gamma_raw,
        chain_bias,
        chain_ids,
        pad_mask,
        ln_single_gain,
        w_bias.T,
        w_out,
        w_qkv.T,
        w_points.T,
    ]
    held = [pltpu.VMEM(x.shape, x.dtype) for x in sources[:10]]
    held.append(pltpu.VMEM((3 * PLANE, S), BF16))
    pair_out, heads, rows, gains, wb, w_loc, wq, wp = pl.pallas_call(
        own_kernel,
        out_shape=[
            jax.ShapeDtypeStruct(pair_grid.shape, BF16),
            jax.ShapeDtypeStruct((3, HPAD, 128), F32),
            jax.ShapeDtypeStruct((2, n), jnp.int32),
            jax.ShapeDtypeStruct((1, S + C), F32),
            jax.ShapeDtypeStruct((HPAD, C), BF16),
            jax.ShapeDtypeStruct((3, PLANE, S), BF16),
            jax.ShapeDtypeStruct(sources[11].shape, BF16),
            jax.ShapeDtypeStruct(sources[12].shape, BF16),
        ],
        in_specs=[whole(pltpu.HBM)] * len(sources),
        out_specs=[whole()] * 8,
        scratch_shapes=held
        + [
            pltpu.VMEM((S // 128, 3 * PLANE, 128), F32),
            pltpu.SemaphoreType.DMA((len(sources),)),
        ],
        compiler_params=params(18 + large),
        name="own_transition",
    )(*in_hbm(sources))

    scratch = [
        pltpu.VMEM((local, near, C), BF16),
        pltpu.VMEM((2 * local * HPAD, near), BF16),
        pltpu.VMEM((local * HPAD, C), F32),
    ]
    send, base, value, real = pl.pallas_call(
        first_kernel,
        out_shape=[
            jax.ShapeDtypeStruct((PARTS, local, 128), BF16),
            jax.ShapeDtypeStruct((local * HPAD, near), F32),
            jax.ShapeDtypeStruct((2, near, WIDE), BF16),
            jax.ShapeDtypeStruct((1, near), jnp.int32),
        ],
        in_specs=[whole()] * 11,
        out_specs=[whole()] * 4,
        scratch_shapes=[
            pltpu.VMEM((tiles, FEAT, near // tiles), F32),
            pltpu.VMEM((tiles, QPTS + 3 * PLANE, near // tiles), F32),
            pltpu.VMEM((FEAT, 2 * local), F32),
            pltpu.VMEM((QPTS, 2 * local), F32),
        ]
        + scratch,
        compiler_params=params(16 + large),
        name="first_half",
    )(received, own, partner, heads, rows, gains, wq, wp, wb, w_swiglu, w_pair_down)
    got = lax.ppermute(send, "rows", across)

    sums, wide, stats = pl.pallas_call(
        second_kernel,
        out_shape=[
            jax.ShapeDtypeStruct((HEADS, local, 128), F32),
            jax.ShapeDtypeStruct((local, WIDE), F32),
            jax.ShapeDtypeStruct((local, 2 * HPAD), F32),
        ],
        in_specs=[whole()] * 8,
        out_specs=[whole()] * 3,
        scratch_shapes=scratch,
        compiler_params=params(12 + large),
        name="second_half",
    )(received, base, value, real, gains, wb, w_swiglu, w_pair_down)

    single_out = pl.pallas_call(
        finish_kernel,
        out_shape=jax.ShapeDtypeStruct((local, S), BF16),
        in_specs=[whole()] * 8,
        out_specs=whole(),
        compiler_params=params(12),
        name="finish",
    )(got, sums, wide, stats, own, gains, w_out, w_loc)
    return (single_out, pair_out)


def solution(mesh):
    placed = (
        P(("groups", "rows"), None),
        P("groups", "rows", None),
        P(None, ("groups", "rows")),
        P("groups"),
        P("groups"),
    ) + (P(),) * 10
    return jax.shard_map(
        on_device,
        mesh=mesh,
        in_specs=placed,
        out_specs=(P(("groups", "rows"), None), P("groups", "rows", None)),
        check_vma=False,
    )
```

time: 30.5 us -> 24.1 us (0.79)
  waiting for transfers between devices: 5.57 us -> 1.68 us
  starting transfers between devices: 13.7 us -> 10.5 us
  Pallas kernels: 9.08 us -> 10.9 us
  other arithmetic: 0.7 us -> 0 us
  local copies, waits for them, and re-layouts: 0.33 us -> 0.02 us
    ppermute x6 -> x2, waiting for transfers between devices: 5.57 us -> 0.91 us  [the longest x1 0.91 us: on_device(): got = lax.ppermute(send, 'rows', across)]
    all_to_all x1, starting transfers between devices: 7.4 us -> 5.27 us  [on_device(): lax.all_to_all(packed, 'rows', 0, 0, tiled=True, axis_index_groups=halves)]
    pallas_call x3 -> x4, Pallas kernels: 5.64 us -> 7.47 us  [the longest x1 2.81 us: on_device(): pl.pallas_call(first_kernel, out_shape=[jax.ShapeDtypeStruct((PARTS, loca...]
    ppermute x6 -> x2, starting transfers between devices: 6.31 us -> 5.26 us  [the longest x1 2.65 us: on_device(): partner = lax.ppermute(own, 'rows', across)]
    all_to_all x1, waiting for transfers between devices: 0.01 us -> 0.77 us  [on_device(): lax.all_to_all(packed, 'rows', 0, 0, tiled=True, axis_index_groups=halves)]
    concatenate x1 -> x0, other arithmetic: 0.7 us -> none  [gather_rows(): stack = jnp.concatenate(got, axis=0)]
    unnamed x8 -> x6, local copies, waits for them, and re-layouts: 0.33 us -> 0.02 us
  transfers between devices with their start and end apart: 7 -> 3, of which waited for: 3 -> 2; matrix products, arithmetic and copies ran while one was open for 2% -> 0% of each run, Pallas kernels for 20% -> 21%
where the time goes in v3:
time: 24.1 us; the launch traced here: 23.8 us
  Pallas kernels  10.9 us (45%)
  starting transfers between devices  10.5 us (44%)
  waiting for transfers between devices  1.68 us (7%)
  between operations  0.69 us (3%)
    all_to_all x1, starting transfers between devices, on_device(): lax.all_to_all(packed, 'rows', 0, 0, tiled=True, axis_index_groups=halves)  5.27 us
    pallas_call x1, Pallas kernels, on_device(): pl.pallas_call(own_kernel, out_shape=[jax.ShapeDtypeStruct(pair_grid.shap...  3.44 us
    pallas_call x1, Pallas kernels, on_device(): pl.pallas_call(first_kernel, out_shape=[jax.ShapeDtypeStruct((PARTS, loca...  2.81 us
    ppermute x1, starting transfers between devices, on_device(): partner = lax.ppermute(own, 'rows', across)  2.65 us
    ppermute x1, starting transfers between devices, on_device(): got = lax.ppermute(send, 'rows', across)  2.61 us
    pallas_call x1, Pallas kernels, on_device(): pl.pallas_call(pack_kernel, out_shape=[jax.ShapeDtypeStruct((nsrc, 2 * lo...  1.76 us
    pallas_call x1, Pallas kernels, on_device(): pl.pallas_call(second_kernel, out_shape=[jax.ShapeDtypeStruct((HEADS, loc...  1.52 us
    pallas_call x1, Pallas kernels, on_device(): pl.pallas_call(finish_kernel, out_shape=jax.ShapeDtypeStruct((local, S),...  1.38 us
  transfers between devices with their start and end apart: 3, of which 2 were waited for; matrix products, arithmetic and copies ran while one was open for 0% of the time, Pallas kernels for 21%

profile of v3, /device:TPU:0, one launch (start us, length us, event | category | flops | bytes accessed | tf_op | source)
XLA Modules:
  0.0 23.8 jit_solution(7501996510707491915)
XLA Ops:
  0.6 1.8 %pack.1 = (bf16[8,20,8,128]{3,2,1,0:T(8,128)(2,1)}, bf16[8,512]{1,0:T(8,128)(2,1)S(1)}) custom-call(bf16[2,8,8,8,128]{4,3,2,1,0:T(8,128)(2,1)} %bitcast.5, bf16[8,384]{1,0:T(8,128)(2,1)} %single_hbm.1, f32[8,12]{1,0:T(8,128)} %bitcast.8), custom_call_target="tpu_custom_call" | custom-call | tf_op jit(solution)/shard_map/pack/pallas_call | solution.py:466
  2.4 5.3 %all-to-all-start = ((bf16[8,20,8,128]{3,2,1,0:T(8,128)(2,1)}), bf16[8,20,8,128]{3,2,1,0:T(8,128)(2,1)S(1)}, u32[]{:S(2)}, u32[]{:S(2)}) async-start(bf16[8,20,8,128]{3,2,1,0:T(8,128)(2,1)} %get-tuple-element.19), calls=%async_computation | async-start | bytes 655360 | tf_op jit(solution)/shard_map/all_to_all | solution.py:481
  7.7 0.0 copy-start.1
  7.7 0.0 copy-start.2
  7.7 2.7 %collective-permute-start = (bf16[8,512]{1,0:T(8,128)(2,1)S(1)}, bf16[8,512]{1,0:T(8,128)(2,1)S(1)}, u32[]{:S(2)}, u32[]{:S(2)}) collective-permute-start(bf16[8,512]{1,0:T(8,128)(2,1)S(1)} %get-tuple-element.20.own_ref), channel_id=1, source_target_pairs={{0,8},{1,9},{2,10},{3,11},{4,12},{5,13},{6,14},{7,15},{8,0},{9,1},... | collective-permute-start | bytes 24584 | tf_op jit(solution)/shard_map/ppermute | solution.py:484
  10.3 3.4 %own_transition.1 = (bf16[128,8,128]{2,1,0:T(8,128)(2,1)}, f32[3,16,128]{2,1,0:T(8,128)S(1)}, s32[2,128]{1,0:T(2,128)S(1)}, f32[1,512]{1,0:T(1,128)S(1)}, bf16[1...) custom-call(bf16[128,8,128]{2,1,0:T(8,128)(2,1)} %refs_0_.1, ...), custom_call_target="tpu_custom_call" | custom-call | tf_op jit(solution)/shard_map/own_transition/pallas_call | solution.py:503
  13.8 0.0 copy-start
  13.8 0.0 collective-permute-done.partner_ref
  13.8 0.8 %all-to-all-done.recv_ref = bf16[8,20,8,128]{3,2,1,0:T(8,128)(2,1)S(1)} async-done(((bf16[8,20,8,128]{3,2,1,0:T(8,128)(2,1)}), bf16[8,20,8,128]{3,2,1,0:T(8,128)(2,1)S(1)}, u32[]{:S(2)}, u32[]{:S(2)}) %all-to-all-start) | async-done | bytes 327712 | tf_op jit(solution)/shard_map/all_to_all | solution.py:481
  14.6 0.0 copy-done.1
  14.6 0.0 copy-done.2
  14.6 2.8 %first_half.1 = (bf16[23,8,128]{2,1,0:T(8,128)(2,1)S(1)}, f32[128,64]{1,0:T(8,128)S(1)}, bf16[2,64,640]{2,1,0:T(8,128)(2,1)S(1)}, s32[1,64]{1,0:T(1,128)S(1)}) custom-call(bf16[8,20,8,128]{3,2,1,0:T(8,128)(2,1)S(1)} %all-to-all-done.recv_ref, bf16[8,512]{1,0:T(8,128)(2,1)S(1)} %get-tuple-element.20.own_ref, ...), custom_call_target="tpu_custom_call" | custom-call | tf_op jit(solution)/shard_map/first_half/pallas_call | solution.py:531
  17.4 2.6 %collective-permute-start.1 = (bf16[23,8,128]{2,1,0:T(8,128)(2,1)S(1)}, bf16[23,8,128]{2,1,0:T(8,128)(2,1)S(1)}, u32[]{:S(2)}, u32[]{:S(2)}) collective-permute-start(bf16[23,8,128]{2,1,0:T(8,128)(2,1)S(1)} %get-tuple-element.27), channel_id=1, source_target_pairs={{0,8},{1,9},{2,10},{3,11},{4,12},{5,13},{6,14},{7,15},{8,0},{9,1},... | collective-permute-start | bytes 141320 | tf_op jit(solution)/shard_map/ppermute | solution.py:551
  20.0 1.5 %second_half.1 = (f32[12,8,128]{2,1,0:T(8,128)S(1)}, f32[8,640]{1,0:T(8,128)S(1)}, f32[8,32]{1,0:T(8,128)S(1)}) custom-call(bf16[8,20,8,128]{3,2,1,0:T(8,128)(2,1)S(1)} %all-to-all-done.recv_ref, f32[128,64]{1,0:T(8,128)S(1)} %get-tuple-element.28.base_ref, bf16[2,64,640]{2,1,0:T(8,128)(2,1)S(1)} %get-tuple-element.29.value_ref, ...), custom_call_target="tpu_custom_call" | custom-call | tf_op jit(solution)/shard_map/second_half/pallas_call | solution.py:553
  21.5 0.9 %collective-permute-done.1.got_ref = bf16[23,8,128]{2,1,0:T(8,128)(2,1)S(1)} collective-permute-done((bf16[23,8,128]{2,1,0:T(8,128)(2,1)S(1)}, bf16[23,8,128]{2,1,0:T(8,128)(2,1)S(1)}, u32[]{:S(2)}, u32[]{:S(2)}) %collective-permute-start.1) | collective-permute-done | bytes 47136 | tf_op jit(solution)/shard_map/ppermute | solution.py:551
  22.4 0.0 copy-done
  22.4 1.4 %finish.1 = bf16[8,384]{1,0:T(8,128)(2,1)} custom-call(bf16[23,8,128]{2,1,0:T(8,128)(2,1)S(1)} %collective-permute-done.1.got_ref, f32[12,8,128]{2,1,0:T(8,128)S(1)} %get-tuple-element.31.sums_ref, f32[8,640]{1,0:T(8,128)S(1)} %get-tuple-element.32.wide_ref, f32[8,32]{1,0:T(8,128)S(1)} %get-tuple-element.33.stats_ref, ...), custom_call_target="tpu_custom_call" | custom-call | tf_op jit(solution)/shard_map/finish/pallas_call | solution.py:567
Async XLA Ops:
  2.4 12.2 %all-to-all-start = ((bf16[8,20,8,128]{3,2,1,0:T(8,128)(2,1)}), bf16[8,20,8,128]{3,2,1,0:T(8,128)(2,1)S(1)}, u32[]{:S(2)}, u32[]{:S(2)}) async-start(bf16[8,20,8,128]{3,2,1,0:T(8,128)(2,1)} %get-tuple-element.19), calls=%async_computation | async-start | bytes 655360 | tf_op jit(solution)/shard_map/all_to_all | solution.py:481
  7.7 6.9 %copy-start.1 = (bf16[128,1024]{1,0:T(8,128)(2,1)S(1)}, bf16[128,1024]{1,0:T(8,128)(2,1)}, u32[]{:S(2)}) copy-start(bf16[128,1024]{1,0:T(8,128)(2,1)} %w_swiglu_ref.3) | copy-start | bytes 786436
  7.7 6.9 %copy-start.2 = (bf16[512,128]{1,0:T(8,128)(2,1)S(1)}, bf16[512,128]{1,0:T(8,128)(2,1)}, u32[]{:S(2)}) copy-start(bf16[512,128]{1,0:T(8,128)(2,1)} %w_down_ref.3) | copy-start | bytes 393220
  7.7 6.1 %collective-permute-start = (bf16[8,512]{1,0:T(8,128)(2,1)S(1)}, bf16[8,512]{1,0:T(8,128)(2,1)S(1)}, u32[]{:S(2)}, u32[]{:S(2)}) collective-permute-start(bf16[8,512]{1,0:T(8,128)(2,1)S(1)} %get-tuple-element.20.own_ref), channel_id=1, source_target_pairs={{0,8},{1,9},{2,10},{3,11},{4,12},{5,13},{6,14},{7,15},{8,0},{9,1},... | collective-permute-start | bytes 24584 | tf_op jit(solution)/shard_map/ppermute | solution.py:484
  13.8 8.7 %copy-start = (bf16[2112,384]{1,0:T(8,128)(2,1)S(1)}, bf16[2112,384]{1,0:T(8,128)(2,1)}, u32[]{:S(2)}) copy-start(bf16[2112,384]{1,0:T(8,128)(2,1)} %w_out_ref.1) | copy-start | bytes 4866052
  17.4 5.0 %collective-permute-start.1 = (bf16[23,8,128]{2,1,0:T(8,128)(2,1)S(1)}, bf16[23,8,128]{2,1,0:T(8,128)(2,1)S(1)}, u32[]{:S(2)}, u32[]{:S(2)}) collective-permute-start(bf16[23,8,128]{2,1,0:T(8,128)(2,1)S(1)} %get-tuple-element.27), channel_id=1, source_target_pairs={{0,8},{1,9},{2,10},{3,11},{4,12},{5,13},{6,14},{7,15},{8,0},{9,1},... | collective-permute-start | bytes 141320 | tf_op jit(solution)/shard_map/ppermute | solution.py:551

commit v4 on v3

--- a/solution.py
+++ b/solution.py
@@ -165,6 +165,39 @@
 def head_of_lane(rows):
     lanes = iota((rows, WIDE), 1)
     return jnp.where(lanes < 256, lanes // CH, (lanes % 128) // VP)
+
+
+def base_scores(
+    queries, query_pts, high_keys, low_keys, key_pts, heads_ref, chain_all, chain_row, first
+):
+    local = queries.shape[0]
+    n = high_keys.shape[1]
+    rows = local * HPAD
+    owned = (iota((HPAD, FEAT), 1) // CH == iota((HPAD, FEAT), 0))[None]
+    spread = jnp.broadcast_to(queries.reshape(local, 1, FEAT), (local, HPAD, FEAT))
+    high, low = split(jnp.where(owned, spread, 0.0).reshape(rows, FEAT))
+    both = jnp.dot(jnp.concatenate([high, low], axis=0), high_keys, preferred_element_type=F32)
+    dots = both[:rows] + both[rows:] + jnp.dot(high, low_keys, preferred_element_type=F32)
+    distances = []
+    blank = jnp.zeros((HPAD - HEADS, n), F32)
+    for i in range(local):
+        distance = 0.0
+        for q, k in zip(query_pts, key_pts):
+            apart = q[:, i : i + 1] - k
+            distance = distance + apart * apart
+        distances += [distance, blank]
+    distance = jnp.concatenate(distances, axis=0)
+
+    def per_row(index):
+        wide = jnp.concatenate([heads_ref[index]] * max(1, n // 128), axis=1)[:, :n]
+        return jnp.concatenate([wide] * local, axis=0)
+
+    width = chain_all.shape[1]
+    lanes, order = iota((local, width), 1), iota((local, width), 0)
+    mine = jnp.sum(jnp.where(lanes == first + order, chain_all, 0), axis=1, keepdims=True)
+    mine = jnp.broadcast_to(mine.reshape(local, 1, 1), (local, HPAD, n)).reshape(rows, n)
+    chain = jnp.where(chain_row == mine, per_row(1), per_row(2))
+    return WEIGHT_L * (dots * (1.0 / math.sqrt(CH)) + chain + per_row(0) * distance)
 
 
 def partial_attention(
@@ -224,19 +257,20 @@
     w_swiglu_ref,
     w_down_ref,
     send_ref,
-    base_ref,
     value_ref,
-    real_ref,
-    feat_scr,
+    near_ref,
+    keys_ref,
+    key_pts_ref,
+    query_ref,
+    query_pts_ref,
     pts_scr,
-    qf_scr,
     qp_scr,
     pair_scr,
     attn_scr,
     sums_scr,
 ):
     nsrc, _, local, _ = recv_ref.shape
-    tiles, _, lane = feat_scr.shape
+    tiles, _, lane = pts_scr.shape
     n = nsrc * local
     me = lax.axis_index("rows")
     upper = me // nsrc
@@ -253,49 +287,35 @@
     frames = nt_dot(pick, piece(2 * local + SMALL - 1))
     query_frames = nt_dot(pick, queries[:, S:])
 
-    feats = nt_dot(wq_ref[FEAT : 2 * FEAT, :], all_single)
+    high_keys, low_keys = split(nt_dot(wq_ref[FEAT : 2 * FEAT, :], all_single))
+    keys_ref[0] = high_keys
+    keys_ref[1] = low_keys
     points = nt_dot(wp_ref[QPTS:, :], all_single)
     for t in range(tiles):
-        feat_scr[t] = feats[:, t * lane : (t + 1) * lane]
         pts_scr[t] = points[:, t * lane : (t + 1) * lane]
-    qf_scr[...] = nt_dot(wq_ref[:FEAT, :], queries[:, :S])
+    features = nt_dot(queries[:, :S], wq_ref[:FEAT, :])
     qp_scr[...] = nt_dot(wp_ref[:QPTS, :], queries[:, :S])
 
-    key_feats = [strided(feat_scr, c, HEADS, CH) for c in range(CH)]
-    query_feats = [qf_scr[pl.ds(c, HEADS, stride=CH), :] for c in range(CH)]
     key_pts, query_pts = [], []
     for p in range(QP):
         key_pts += place(frames, [strided(pts_scr, 3 * p + y, HEADS, 3 * QP) for y in range(3)])
         query_pts += place(
             query_frames, [qp_scr[pl.ds(3 * p + y, HEADS, stride=3 * QP), :] for y in range(3)]
         )
-
-    def spread(index):
-        return jnp.concatenate([heads_ref[index, :HEADS, :]] * max(1, n // 128), axis=1)[:, :n]
-
-    point_scale, same_bias, cross_bias = spread(0), spread(1), spread(2)
+    for k in range(3 * QP):
+        key_pts_ref[k] = key_pts[k]
+        query_pts_ref[k] = query_pts[k][:, local:]
+    query_ref[...] = features[local:]
+
     chain_all = rows_ref[0:1, :]
     chain_row = jnp.where(upper == 0, chain_all[:, :n], chain_all[:, n:])
     real = jnp.where(upper == 0, rows_ref[1:2, :n], rows_ref[1:2, n:])
-    real_ref[...] = real
-    lanes = iota((1, 2 * n), 1)
-    starts = [jnp.bitwise_xor(me, nsrc) * local, me * local]
-    bases = []
-    for i in range(2 * local):
-        dots = sum(q[:, i : i + 1] * k for q, k in zip(query_feats, key_feats))
-        distance = 0.0
-        for q, k in zip(query_pts, key_pts):
-            apart = q[:, i : i + 1] - k
-            distance = distance + apart * apart
-        at = starts[i // local] + i % local
-        mine = jnp.sum(jnp.where(lanes == at, chain_all, 0), axis=1, keepdims=True)
-        chain = jnp.where(chain_row == mine, same_bias, cross_bias)
-        base = WEIGHT_L * (dots * (1.0 / math.sqrt(CH)) + chain + point_scale * distance)
-        base = jnp.concatenate([base, jnp.zeros((HPAD - HEADS, n), F32)], axis=0)
-        if i < local:
-            bases.append(base)
-        else:
-            base_ref[(i - local) * HPAD : (i - local + 1) * HPAD, :] = base
+    near_ref[0:1, :] = chain_row
+    near_ref[1:2, :] = real
+    base = base_scores(
+        features[:local], query_pts, high_keys, low_keys, key_pts, heads_ref, chain_all, chain_row,
+        jnp.bitwise_xor(me, nsrc) * local,
+    )
 
     planes = place(frames, [strided(pts_scr, QPTS + y, PLANE, 3) for y in range(3)])
     gap = jnp.zeros((n, 128 - PLANE), F32)
@@ -307,7 +327,7 @@
     value_ref[1] = low
 
     pair_sums, summed, peak, total = partial_attention(
-        recv_ref, (1 - upper) * local, jnp.concatenate(bases, axis=0), real, high, low,
+        recv_ref, (1 - upper) * local, base, real, high, low,
         gains_ref[0:1, S:], w_swiglu_ref, w_down_ref, wb_ref, pair_scr, attn_scr, sums_scr,
     )
     for h in range(HEADS):
@@ -327,9 +347,14 @@
 
 def second_kernel(
     recv_ref,
-    base_ref,
     value_ref,
-    real_ref,
+    near_ref,
+    keys_ref,
+    key_pts_ref,
+    query_ref,
+    query_pts_ref,
+    heads_ref,
+    rows_ref,
     gains_ref,
     wb_ref,
     w_swiglu_ref,
@@ -342,9 +367,14 @@
     sums_scr,
 ):
     nsrc, _, local, _ = recv_ref.shape
-    upper = lax.axis_index("rows") // nsrc
+    me = lax.axis_index("rows")
+    base = base_scores(
+        query_ref[...], [query_pts_ref[k] for k in range(3 * QP)], keys_ref[0], keys_ref[1],
+        [key_pts_ref[k] for k in range(3 * QP)], heads_ref, rows_ref[0:1, :], near_ref[0:1, :],
+        me * local,
+    )
     pair_sums, summed, peak, total = partial_attention(
-        recv_ref, upper * local, base_ref[...], real_ref[...], value_ref[0], value_ref[1],
+        recv_ref, me // nsrc * local, base, near_ref[1:2, :], value_ref[0], value_ref[1],
         gains_ref[0:1, S:], w_swiglu_ref, w_down_ref, wb_ref, pair_scr, attn_scr, sums_scr,
     )
     for h in range(HEADS):
@@ -528,20 +558,21 @@
         pltpu.VMEM((2 * local * HPAD, near), BF16),
         pltpu.VMEM((local * HPAD, C), F32),
     ]
-    send, base, value, real = pl.pallas_call(
+    send, *held = pl.pallas_call(
         first_kernel,
         out_shape=[
             jax.ShapeDtypeStruct((PARTS, local, 128), BF16),
-            jax.ShapeDtypeStruct((local * HPAD, near), F32),
             jax.ShapeDtypeStruct((2, near, WIDE), BF16),
-            jax.ShapeDtypeStruct((1, near), jnp.int32),
+            jax.ShapeDtypeStruct((2, near), jnp.int32),
+            jax.ShapeDtypeStruct((2, FEAT, near), BF16),
+            jax.ShapeDtypeStruct((3 * QP, HEADS, near), F32),
+            jax.ShapeDtypeStruct((local, FEAT), F32),
+            jax.ShapeDtypeStruct((3 * QP, HEADS, local), F32),
         ],
         in_specs=[whole()] * 11,
-        out_specs=[whole()] * 4,
+        out_specs=[whole()] * 7,
         scratch_shapes=[
-            pltpu.VMEM((tiles, FEAT, near // tiles), F32),
             pltpu.VMEM((tiles, QPTS + 3 * PLANE, near // tiles), F32),
-            pltpu.VMEM((FEAT, 2 * local), F32),
             pltpu.VMEM((QPTS, 2 * local), F32),
         ]
         + scratch,
@@ -557,12 +588,12 @@
             jax.ShapeDtypeStruct((local, WIDE), F32),
             jax.ShapeDtypeStruct((local, 2 * HPAD), F32),
         ],
-        in_specs=[whole()] * 8,
+        in_specs=[whole()] * 13,
         out_specs=[whole()] * 3,
         scratch_shapes=scratch,
         compiler_params=params(12 + large),
         name="second_half",
-    )(received, base, value, real, gains, wb, w_swiglu, w_pair_down)
+    )(received, *held, heads, rows, gains, wb, w_swiglu, w_pair_down)
 
     single_out = pl.pallas_call(
         finish_kernel,

time: 24.1 us -> 22.9 us (0.950)
  Pallas kernels: 10.9 us -> 9.82 us
    pallas_call x1, Pallas kernels: 2.81 us -> 1.64 us  [on_device(): pl.pallas_call(first_kernel, out_shape=[jax.ShapeDtypeStruct((PARTS, loca...]
  transfers between devices with their start and end apart: 3 -> 3, of which waited for: 2 -> 2; matrix products, arithmetic and copies ran while one was open for 0% -> 0% of each run, Pallas kernels for 21% -> 22%
where the time goes in v4:
time: 22.9 us; the launch traced here: 22.7 us
  starting transfers between devices  10.5 us (46%)
  Pallas kernels  9.82 us (43%)
  waiting for transfers between devices  1.6 us (7%)
  between operations  0.69 us (3%)
    all_to_all x1, starting transfers between devices, on_device(): lax.all_to_all(packed, 'rows', 0, 0, tiled=True, axis_index_groups=halves)  5.27 us
    pallas_call x1, Pallas kernels, on_device(): pl.pallas_call(own_kernel, out_shape=[jax.ShapeDtypeStruct(pair_grid.shap...  3.44 us
    ppermute x1, starting transfers between devices, on_device(): partner = lax.ppermute(own, 'rows', across)  2.65 us
    ppermute x1, starting transfers between devices, on_device(): got = lax.ppermute(send, 'rows', across)  2.61 us
    pallas_call x1, Pallas kernels, on_device(): pl.pallas_call(pack_kernel, out_shape=[jax.ShapeDtypeStruct((nsrc, 2 * lo...  1.76 us
    pallas_call x1, Pallas kernels, on_device(): pl.pallas_call(first_kernel, out_shape=[jax.ShapeDtypeStruct((PARTS, loca...  1.64 us
    pallas_call x1, Pallas kernels, on_device(): pl.pallas_call(second_kernel, out_shape=[jax.ShapeDtypeStruct((HEADS, loc...  1.59 us
    pallas_call x1, Pallas kernels, on_device(): pl.pallas_call(finish_kernel, out_shape=jax.ShapeDtypeStruct((local, S),...  1.38 us
  transfers between devices with their start and end apart: 3, of which 2 were waited for; matrix products, arithmetic and copies ran while one was open for 0% of the time, Pallas kernels for 22%

profile of v4, /device:TPU:0, one launch (start us, length us, event | category | flops | bytes accessed | tf_op | source)
XLA Modules:
  0.0 22.7 jit_solution(18191106502253015560)
XLA Ops:
  0.6 1.8 %pack.1 = (bf16[8,20,8,128]{3,2,1,0:T(8,128)(2,1)}, bf16[8,512]{1,0:T(8,128)(2,1)S(1)}) custom-call(bf16[2,8,8,8,128]{4,3,2,1,0:T(8,128)(2,1)} %bitcast.5, bf16[8,384]{1,0:T(8,128)(2,1)} %single_hbm.1, f32[8,12]{1,0:T(8,128)} %bitcast.8), custom_call_target="tpu_custom_call" | custom-call | tf_op jit(solution)/shard_map/pack/pallas_call | solution.py:496
  2.4 5.3 %all-to-all-start = ((bf16[8,20,8,128]{3,2,1,0:T(8,128)(2,1)}), bf16[8,20,8,128]{3,2,1,0:T(8,128)(2,1)S(1)}, u32[]{:S(2)}, u32[]{:S(2)}) async-start(bf16[8,20,8,128]{3,2,1,0:T(8,128)(2,1)} %get-tuple-element.22), calls=%async_computation | async-start | bytes 655360 | tf_op jit(solution)/shard_map/all_to_all | solution.py:511
  7.7 0.0 copy-start.1
  7.7 0.0 copy-start.2
  7.7 2.7 %collective-permute-start = (bf16[8,512]{1,0:T(8,128)(2,1)S(1)}, bf16[8,512]{1,0:T(8,128)(2,1)S(1)}, u32[]{:S(2)}, u32[]{:S(2)}) collective-permute-start(bf16[8,512]{1,0:T(8,128)(2,1)S(1)} %get-tuple-element.23.own_ref), channel_id=1, source_target_pairs={{0,8},{1,9},{2,10},{3,11},{4,12},{5,13},{6,14},{7,15},{8,0},{9,1},... | collective-permute-start | bytes 24584 | tf_op jit(solution)/shard_map/ppermute | solution.py:514
  10.3 3.4 %own_transition.1 = (bf16[128,8,128]{2,1,0:T(8,128)(2,1)}, f32[3,16,128]{2,1,0:T(8,128)S(1)}, s32[2,128]{1,0:T(2,128)S(1)}, f32[1,512]{1,0:T(1,128)S(1)}, bf16[1...) custom-call(bf16[128,8,128]{2,1,0:T(8,128)(2,1)} %refs_0_.1, ...), custom_call_target="tpu_custom_call" | custom-call | tf_op jit(solution)/shard_map/own_transition/pallas_call | solution.py:533
  13.8 0.0 copy-start
  13.8 0.0 collective-permute-done.partner_ref
  13.8 0.8 %all-to-all-done.recv_ref = bf16[8,20,8,128]{3,2,1,0:T(8,128)(2,1)S(1)} async-done(((bf16[8,20,8,128]{3,2,1,0:T(8,128)(2,1)}), bf16[8,20,8,128]{3,2,1,0:T(8,128)(2,1)S(1)}, u32[]{:S(2)}, u32[]{:S(2)}) %all-to-all-start) | async-done | bytes 327712 | tf_op jit(solution)/shard_map/all_to_all | solution.py:511
  14.6 0.0 copy-done.1
  14.6 0.0 copy-done.2
  14.6 1.6 %first_half.1 = (bf16[23,8,128]{2,1,0:T(8,128)(2,1)S(1)}, bf16[2,64,640]{2,1,0:T(8,128)(2,1)S(1)}, s32[2,64]{1,0:T(2,128)S(1)}, bf16[2,192,64]{2,1,0:T(8,128)(2,...) custom-call(bf16[8,20,8,128]{3,2,1,0:T(8,128)(2,1)S(1)} %all-to-all-done.recv_ref, ...), custom_call_target="tpu_custom_call" | custom-call | tf_op jit(solution)/shard_map/first_half/pallas_call | solution.py:561
  16.2 2.6 %collective-permute-start.1 = (bf16[23,8,128]{2,1,0:T(8,128)(2,1)S(1)}, bf16[23,8,128]{2,1,0:T(8,128)(2,1)S(1)}, u32[]{:S(2)}, u32[]{:S(2)}) collective-permute-start(bf16[23,8,128]{2,1,0:T(8,128)(2,1)S(1)} %get-tuple-element.30), channel_id=1, source_target_pairs={{0,8},{1,9},{2,10},{3,11},{4,12},{5,13},{6,14},{7,15},{8,0},{9,1},... | collective-permute-start | bytes 141320 | tf_op jit(solution)/shard_map/ppermute | solution.py:582
  18.8 1.6 %second_half.1 = (f32[12,8,128]{2,1,0:T(8,128)S(1)}, f32[8,640]{1,0:T(8,128)S(1)}, f32[8,32]{1,0:T(8,128)S(1)}) custom-call(bf16[8,20,8,128]{3,2,1,0:T(8,128)(2,1)S(1)} %all-to-all-done.recv_ref, bf16[2,64,640]{2,1,0:T(8,128)(2,1)S(1)} %get-tuple-element.31.value_ref, s32[2,64]{1,0:T(2,128)S(1)} %get-tuple-element.32.near_ref, ...), custom_call_target="tpu_custom_call" | custom-call | tf_op jit(solution)/shard_map/second_half/pallas_call | solution.py:584
  20.4 0.8 %collective-permute-done.1.got_ref = bf16[23,8,128]{2,1,0:T(8,128)(2,1)S(1)} collective-permute-done((bf16[23,8,128]{2,1,0:T(8,128)(2,1)S(1)}, bf16[23,8,128]{2,1,0:T(8,128)(2,1)S(1)}, u32[]{:S(2)}, u32[]{:S(2)}) %collective-permute-start.1) | collective-permute-done | bytes 47136 | tf_op jit(solution)/shard_map/ppermute | solution.py:582
  21.3 0.0 copy-done
  21.3 1.4 %finish.1 = bf16[8,384]{1,0:T(8,128)(2,1)} custom-call(bf16[23,8,128]{2,1,0:T(8,128)(2,1)S(1)} %collective-permute-done.1.got_ref, f32[12,8,128]{2,1,0:T(8,128)S(1)} %get-tuple-element.37.sums_ref, f32[8,640]{1,0:T(8,128)S(1)} %get-tuple-element.38.wide_ref, f32[8,32]{1,0:T(8,128)S(1)} %get-tuple-element.39.stats_ref, ...), custom_call_target="tpu_custom_call" | custom-call | tf_op jit(solution)/shard_map/finish/pallas_call | solution.py:598
Async XLA Ops:
  2.4 12.2 %all-to-all-start = ((bf16[8,20,8,128]{3,2,1,0:T(8,128)(2,1)}), bf16[8,20,8,128]{3,2,1,0:T(8,128)(2,1)S(1)}, u32[]{:S(2)}, u32[]{:S(2)}) async-start(bf16[8,20,8,128]{3,2,1,0:T(8,128)(2,1)} %get-tuple-element.22), calls=%async_computation | async-start | bytes 655360 | tf_op jit(solution)/shard_map/all_to_all | solution.py:511
  7.7 6.9 %copy-start.1 = (bf16[128,1024]{1,0:T(8,128)(2,1)S(1)}, bf16[128,1024]{1,0:T(8,128)(2,1)}, u32[]{:S(2)}) copy-start(bf16[128,1024]{1,0:T(8,128)(2,1)} %w_swiglu_ref.3) | copy-start | bytes 786436
  7.7 6.9 %copy-start.2 = (bf16[512,128]{1,0:T(8,128)(2,1)S(1)}, bf16[512,128]{1,0:T(8,128)(2,1)}, u32[]{:S(2)}) copy-start(bf16[512,128]{1,0:T(8,128)(2,1)} %w_down_ref.3) | copy-start | bytes 393220
  7.7 6.1 %collective-permute-start = (bf16[8,512]{1,0:T(8,128)(2,1)S(1)}, bf16[8,512]{1,0:T(8,128)(2,1)S(1)}, u32[]{:S(2)}, u32[]{:S(2)}) collective-permute-start(bf16[8,512]{1,0:T(8,128)(2,1)S(1)} %get-tuple-element.23.own_ref), channel_id=1, source_target_pairs={{0,8},{1,9},{2,10},{3,11},{4,12},{5,13},{6,14},{7,15},{8,0},{9,1},... | collective-permute-start | bytes 24584 | tf_op jit(solution)/shard_map/ppermute | solution.py:514
  13.8 7.5 %copy-start = (bf16[2112,384]{1,0:T(8,128)(2,1)S(1)}, bf16[2112,384]{1,0:T(8,128)(2,1)}, u32[]{:S(2)}) copy-start(bf16[2112,384]{1,0:T(8,128)(2,1)} %w_out_ref.1) | copy-start | bytes 4866052
  16.2 5.0 %collective-permute-start.1 = (bf16[23,8,128]{2,1,0:T(8,128)(2,1)S(1)}, bf16[23,8,128]{2,1,0:T(8,128)(2,1)S(1)}, u32[]{:S(2)}, u32[]{:S(2)}) collective-permute-start(bf16[23,8,128]{2,1,0:T(8,128)(2,1)S(1)} %get-tuple-element.30), channel_id=1, source_target_pairs={{0,8},{1,9},{2,10},{3,11},{4,12},{5,13},{6,14},{7,15},{8,0},{9,1},... | collective-permute-start | bytes 141320 | tf_op jit(solution)/shard_map/ppermute | solution.py:582

commit v5 on v4

--- a/solution.py
+++ b/solution.py
@@ -20,7 +20,7 @@
 PLANE = HEADS * VP
 WIDE = 256 + 3 * 128
 SMALL = S // 128 + 1
-PARTS = HEADS + 2 * (WIDE // 128) + 1
+PARTS = HEADS + WIDE // 128
 F32 = jnp.float32
 BF16 = jnp.bfloat16
 NT = (((1,), (1,)), ((), ()))
@@ -58,22 +58,30 @@
     return high, (values - high.astype(F32)).astype(BF16)
 
 
-def pack_kernel(pair_hbm, single_hbm, frames_hbm, out_ref, own_ref, frames_ref, sems):
+def pack_kernel(
+    pair_hbm, single_hbm, frames_hbm, out_hbm, own_ref, pair_ref, small_ref, frames_ref, in_sems, out_sems
+):
+    nsrc = pair_ref.shape[0]
     local = own_ref.shape[0]
-    copies = [
-        pltpu.make_async_copy(single_hbm, own_ref.at[:, :S], sems.at[0]),
-        pltpu.make_async_copy(frames_hbm, frames_ref, sems.at[1]),
-    ]
-    for half in range(2):
-        copies.append(
+    step = max(1, nsrc // 4)
+    chunks = [(half, at) for at in range(0, nsrc, step) for half in range(2)]
+    arrivals = []
+    for k, (half, at) in enumerate(chunks):
+        arrivals.append(
             pltpu.make_async_copy(
-                pair_hbm.at[half], out_ref.at[:, pl.ds(half * local, local)], sems.at[2 + half]
+                pair_hbm.at[half, pl.ds(at, step)],
+                pair_ref.at[pl.ds(at, step), pl.ds(half * local, local)],
+                in_sems.at[k],
             )
         )
-    for copy in copies:
+    rows_copies = [
+        pltpu.make_async_copy(single_hbm, own_ref.at[:, :S], in_sems.at[len(chunks)]),
+        pltpu.make_async_copy(frames_hbm, frames_ref, in_sems.at[len(chunks) + 1]),
+    ]
+    for copy in rows_copies + arrivals:
         copy.start()
-    copies[0].wait()
-    copies[1].wait()
+    for copy in rows_copies:
+        copy.wait()
     rows = frames_ref[...]
     blank = jnp.zeros((local, 128 - 36), F32)
     turned = jnp.concatenate([rows, rows, rows, blank], axis=1)
@@ -82,11 +90,27 @@
     low = turned - high - middle
     lane = iota(turned.shape, 1)
     own_ref[:, S:] = jnp.where(lane < 12, high, jnp.where(lane < 24, middle, low)).astype(BF16)
-    for dest in range(out_ref.shape[0]):
+    for dest in range(nsrc):
         for piece in range(SMALL):
-            out_ref[dest, 2 * local + piece] = own_ref[:, piece * 128 : piece * 128 + 128]
-    copies[2].wait()
-    copies[3].wait()
+            small_ref[dest, piece] = own_ref[:, piece * 128 : piece * 128 + 128]
+    departures = [
+        pltpu.make_async_copy(small_ref, out_hbm.at[:, pl.ds(2 * local, SMALL)], out_sems.at[0])
+    ]
+    departures[0].start()
+    for k in range(0, len(chunks), 2):
+        arrivals[k].wait()
+        arrivals[k + 1].wait()
+        at = chunks[k][1]
+        departures.append(
+            pltpu.make_async_copy(
+                pair_ref.at[pl.ds(at, step)],
+                out_hbm.at[pl.ds(at, step), pl.ds(0, 2 * local)],
+                out_sems.at[1 + k // 2],
+            )
+        )
+        departures[-1].start()
+    for copy in departures:
+        copy.wait()
 
 
 def strided(ref, start, count, stride):
@@ -236,12 +260,15 @@
     summed = jnp.sum(jnp.where(owned[None], every, 0.0), axis=1)
     diagonal = (iota((HPAD, HPAD), 0) == iota((HPAD, HPAD), 1))[None]
 
-    def by_head(column):
-        wide = jnp.broadcast_to(column.reshape(local, HPAD, 1), (local, HPAD, HPAD))
-        return jnp.sum(jnp.where(diagonal, wide, 0.0), axis=1)
-
+    level = jnp.broadcast_to((peak + jnp.log(total)).reshape(local, HPAD, 1), (local, HPAD, HPAD))
+    level = jnp.sum(jnp.where(diagonal, level, 0.0), axis=1)
     pair_sums = [sums_scr[pl.ds(h, local, stride=HPAD), :] for h in range(HEADS)]
-    return pair_sums, summed, by_head(peak), by_head(total)
+    return pair_sums, summed, level
+
+
+def origin(row_ref):
+    parts = row_ref[:, S:].astype(F32)
+    return parts[:, 0:12] + parts[:, 12:24] + parts[:, 24:36]
 
 
 def first_kernel(
@@ -326,23 +353,22 @@
     value_ref[0] = high
     value_ref[1] = low
 
-    pair_sums, summed, peak, total = partial_attention(
+    pair_sums, summed, level = partial_attention(
         recv_ref, (1 - upper) * local, base, real, high, low,
         gains_ref[0:1, S:], w_swiglu_ref, w_down_ref, wb_ref, pair_scr, attn_scr, sums_scr,
     )
     for h in range(HEADS):
         send_ref[h] = pair_sums[h].astype(BF16)
-    high, low = split(summed)
-    pieces = WIDE // 128
-    for k in range(pieces):
-        send_ref[HEADS + k] = high[:, k * 128 : (k + 1) * 128]
-        send_ref[HEADS + pieces + k] = low[:, k * 128 : (k + 1) * 128]
-    both = jnp.concatenate([peak, total], axis=1)
-    high = both.astype(BF16).astype(F32)
-    middle = (both - high).astype(BF16).astype(F32)
-    low = both - high - middle
-    blank = jnp.zeros((local, 128 - 6 * HPAD), F32)
-    send_ref[PARTS - 1] = jnp.concatenate([high, middle, low, blank], axis=1).astype(BF16)
+    turned = origin(partner_ref)
+    send_ref[HEADS] = summed[:, :128].astype(BF16)
+    send_ref[HEADS + 1] = summed[:, 128:256].astype(BF16)
+    high = level.astype(BF16).astype(F32)
+    middle = (level - high).astype(BF16).astype(F32)
+    low = level - high - middle
+    blank = jnp.zeros((local, 128 - PLANE - HPAD), F32)
+    for x, part in enumerate([high, middle, low]):
+        plane = summed[:, 256 + 128 * x : 256 + 128 * x + PLANE] - turned[:, 9 + x : 10 + x]
+        send_ref[HEADS + 2 + x] = jnp.concatenate([plane, part, blank], axis=1).astype(BF16)
 
 
 def second_kernel(
@@ -359,9 +385,10 @@
     wb_ref,
     w_swiglu_ref,
     w_down_ref,
+    own_ref,
     sums_ref,
     wide_ref,
-    stats_ref,
+    level_ref,
     pair_scr,
     attn_scr,
     sums_scr,
@@ -373,21 +400,27 @@
         [key_pts_ref[k] for k in range(3 * QP)], heads_ref, rows_ref[0:1, :], near_ref[0:1, :],
         me * local,
     )
-    pair_sums, summed, peak, total = partial_attention(
+    pair_sums, summed, level = partial_attention(
         recv_ref, me // nsrc * local, base, near_ref[1:2, :], value_ref[0], value_ref[1],
         gains_ref[0:1, S:], w_swiglu_ref, w_down_ref, wb_ref, pair_scr, attn_scr, sums_scr,
     )
     for h in range(HEADS):
         sums_ref[h] = pair_sums[h]
-    wide_ref[...] = summed
-    stats_ref[...] = jnp.concatenate([peak, total], axis=1)
+    turned = origin(own_ref)
+    wide_ref[:, :256] = summed[:, :256]
+    for x in range(3):
+        at = 256 + 128 * x
+        wide_ref[:, at : at + 128] = summed[:, at : at + 128] - turned[:, 9 + x : 10 + x]
+    level_ref[...] = jnp.concatenate(
+        [jnp.zeros((local, PLANE), F32), level, jnp.zeros((local, 128 - PLANE - HPAD), F32)], axis=1
+    )
 
 
 def finish_kernel(
     got_ref,
     sums_ref,
     wide_ref,
-    stats_ref,
+    level_ref,
     own_ref,
     gains_ref,
     w_out_ref,
@@ -395,39 +428,32 @@
     out_ref,
 ):
     local = own_ref.shape[0]
-    got = got_ref[PARTS - 1].astype(F32)
-    width = 2 * HPAD
-    got = got[:, :width] + got[:, width : 2 * width] + got[:, 2 * width : 3 * width]
-    mine = stats_ref[...]
-    peak = jnp.maximum(got[:, :HPAD], mine[:, :HPAD])
-    got = got[:, HPAD:] * jnp.exp(got[:, :HPAD] - peak)
-    mine = mine[:, HPAD:] * jnp.exp(mine[:, :HPAD] - peak)
-    scale = 1.0 / (got + mine)
-    got, mine = got * scale, mine * scale
-    owner = head_of_lane(local)
-    got_wide = jnp.zeros((local, WIDE), F32)
-    mine_wide = jnp.zeros((local, WIDE), F32)
+    planes = [got_ref[HEADS + 2 + x].astype(F32) for x in range(3)]
+    got = 1.0 / (1.0 + jnp.exp(level_ref[...] - (planes[0] + planes[1] + planes[2])))
+    lanes = iota((local, 128), 1)
+    low_share = jnp.zeros((local, 128), F32)
+    high_share = jnp.zeros((local, 128), F32)
+    plane_share = jnp.zeros((local, 128), F32)
     pair_total = []
     for h in range(HEADS):
-        got_share, mine_share = got[:, h : h + 1], mine[:, h : h + 1]
-        got_wide = jnp.where(owner == h, got_share, got_wide)
-        mine_wide = jnp.where(owner == h, mine_share, mine_wide)
-        pair_total.append(got_share * got_ref[h].astype(F32) + mine_share * sums_ref[h])
-    pieces = WIDE // 128
-    sent = jnp.concatenate(
-        [
-            got_ref[HEADS + k].astype(F32) + got_ref[HEADS + pieces + k].astype(F32)
-            for k in range(pieces)
-        ],
-        axis=1,
-    )
-    summed = got_wide * sent + mine_wide * wide_ref[...]
-
-    parts = own_ref[:, S:].astype(F32)
-    turned = parts[:, 0:12] + parts[:, 12:24] + parts[:, 24:36]
-    shifted = [
-        summed[:, 256 + 128 * x : 384 + 128 * x] - turned[:, 9 + x : 10 + x] for x in range(3)
+        share = jnp.broadcast_to(got[:, PLANE + h : PLANE + h + 1], (local, 128))
+        low_share = jnp.where(lanes // CH == h, share, low_share)
+        high_share = jnp.where(lanes // CH + 8 == h, share, high_share)
+        plane_share = jnp.where(lanes // VP == h, share, plane_share)
+        mine = sums_ref[h]
+        pair_total.append(mine + share * (got_ref[h].astype(F32) - mine))
+
+    def joined(at, share, theirs):
+        mine = wide_ref[:, at : at + 128]
+        return mine + share * (theirs - mine)
+
+    features = [
+        joined(0, low_share, got_ref[HEADS].astype(F32)),
+        joined(128, high_share, got_ref[HEADS + 1].astype(F32)),
     ]
+    shifted = [joined(256 + 128 * x, plane_share, planes[x]) for x in range(3)]
+
+    turned = origin(own_ref)
     local_out = [
         turned[:, y : y + 1] * shifted[0]
         + turned[:, 3 + y : 4 + y] * shifted[1]
@@ -438,7 +464,9 @@
         local_out[0] * local_out[0] + local_out[1] * local_out[1] + local_out[2] * local_out[2] + 1.0
     )
     update = jnp.dot(
-        summed[:, :FEAT].astype(BF16), w_out_ref[:FEAT, :], preferred_element_type=F32
+        jnp.concatenate(features, axis=1)[:, :FEAT].astype(BF16),
+        w_out_ref[:FEAT, :],
+        preferred_element_type=F32,
     )
     for y in range(3):
         update += jnp.dot(
@@ -500,10 +528,13 @@
             jax.ShapeDtypeStruct((local, S + 128), BF16),
         ],
         in_specs=[whole(pltpu.HBM)] * 3,
-        out_specs=[whole(), whole()],
+        out_specs=[whole(pltpu.HBM), whole()],
         scratch_shapes=[
+            pltpu.VMEM((nsrc, 2 * local, local, C), BF16),
+            pltpu.VMEM((nsrc, SMALL, local, C), BF16),
             pltpu.VMEM((local, 12), F32),
-            pltpu.SemaphoreType.DMA((4,)),
+            pltpu.SemaphoreType.DMA((10,)),
+            pltpu.SemaphoreType.DMA((5,)),
         ],
         compiler_params=params(4 + large),
         name="pack",
@@ -581,19 +612,19 @@
     )(received, own, partner, heads, rows, gains, wq, wp, wb, w_swiglu, w_pair_down)
     got = lax.ppermute(send, "rows", across)
 
-    sums, wide, stats = pl.pallas_call(
+    sums, wide, level = pl.pallas_call(
         second_kernel,
         out_shape=[
             jax.ShapeDtypeStruct((HEADS, local, 128), F32),
             jax.ShapeDtypeStruct((local, WIDE), F32),
-            jax.ShapeDtypeStruct((local, 2 * HPAD), F32),
+            jax.ShapeDtypeStruct((local, 128), F32),
         ],
-        in_specs=[whole()] * 13,
+        in_specs=[whole()] * 14,
         out_specs=[whole()] * 3,
         scratch_shapes=scratch,
         compiler_params=params(12 + large),
         name="second_half",
-    )(received, *held, heads, rows, gains, wb, w_swiglu, w_pair_down)
+    )(received, *held, heads, rows, gains, wb, w_swiglu, w_pair_down, own)
 
     single_out = pl.pallas_call(
         finish_kernel,
@@ -602,7 +633,7 @@
         out_specs=whole(),
         compiler_params=params(12),
         name="finish",
-    )(got, sums, wide, stats, own, gains, w_out, w_loc)
+    )(got, sums, wide, level, own, gains, w_out, w_loc)
     return (single_out, pair_out)
 
 

time: 22.9 us -> 22.6 us (0.987)
  Pallas kernels: 9.82 us -> 9.59 us
  transfers between devices with their start and end apart: 3 -> 3, of which waited for: 2 -> 2; matrix products, arithmetic and copies ran while one was open for 0% -> 0% of each run, Pallas kernels for 22% -> 23%
where the time goes in v5:
time: 22.6 us; the launch traced here: 22.2 us
  starting transfers between devices  10.5 us (46%)
  Pallas kernels  9.59 us (42%)
  waiting for transfers between devices  1.42 us (6%)
  between operations  0.69 us (3%)
    all_to_all x1, starting transfers between devices, on_device(): lax.all_to_all(packed, 'rows', 0, 0, tiled=True, axis_index_groups=halves)  5.27 us
    pallas_call x1, Pallas kernels, on_device(): pl.pallas_call(own_kernel, out_shape=[jax.ShapeDtypeStruct(pair_grid.shap...  3.44 us
    ppermute x1, starting transfers between devices, on_device(): partner = lax.ppermute(own, 'rows', across)  2.65 us
    ppermute x1, starting transfers between devices, on_device(): got = lax.ppermute(send, 'rows', across)  2.61 us
    pallas_call x1, Pallas kernels, on_device(): pl.pallas_call(pack_kernel, out_shape=[jax.ShapeDtypeStruct((nsrc, 2 * lo...  1.65 us
    pallas_call x1, Pallas kernels, on_device(): pl.pallas_call(second_kernel, out_shape=[jax.ShapeDtypeStruct((HEADS, loc...  1.63 us
    pallas_call x1, Pallas kernels, on_device(): pl.pallas_call(first_kernel, out_shape=[jax.ShapeDtypeStruct((PARTS, loca...  1.61 us
    pallas_call x1, Pallas kernels, on_device(): pl.pallas_call(finish_kernel, out_shape=jax.ShapeDtypeStruct((local, S),...  1.25 us
  transfers between devices with their start and end apart: 3, of which 2 were waited for; matrix products, arithmetic and copies ran while one was open for 0% of the time, Pallas kernels for 23%

profile of v5, /device:TPU:0, one launch (start us, length us, event | category | flops | bytes accessed | tf_op | source)
XLA Modules:
  0.0 22.2 jit_solution(17377785469463541946)
XLA Ops:
  0.6 1.7 %pack.1 = (bf16[8,20,8,128]{3,2,1,0:T(8,128)(2,1)}, bf16[8,512]{1,0:T(8,128)(2,1)S(1)}) custom-call(bf16[2,8,8,8,128]{4,3,2,1,0:T(8,128)(2,1)} %bitcast.5, bf16[8,384]{1,0:T(8,128)(2,1)} %single_hbm.1, f32[8,12]{1,0:T(8,128)} %bitcast.8), custom_call_target="tpu_custom_call" | custom-call | tf_op jit(solution)/shard_map/pack/pallas_call | solution.py:524
  2.3 5.3 %all-to-all-start = ((bf16[8,20,8,128]{3,2,1,0:T(8,128)(2,1)}), bf16[8,20,8,128]{3,2,1,0:T(8,128)(2,1)S(1)}, u32[]{:S(2)}, u32[]{:S(2)}) async-start(bf16[8,20,8,128]{3,2,1,0:T(8,128)(2,1)} %get-tuple-element.22), calls=%async_computation | async-start | bytes 655360 | tf_op jit(solution)/shard_map/all_to_all | solution.py:542
  7.6 0.0 copy-start.1
  7.6 0.0 copy-start.2
  7.6 2.7 %collective-permute-start = (bf16[8,512]{1,0:T(8,128)(2,1)S(1)}, bf16[8,512]{1,0:T(8,128)(2,1)S(1)}, u32[]{:S(2)}, u32[]{:S(2)}) collective-permute-start(bf16[8,512]{1,0:T(8,128)(2,1)S(1)} %get-tuple-element.23.own_ref), channel_id=1, source_target_pairs={{0,8},{1,9},{2,10},{3,11},{4,12},{5,13},{6,14},{7,15},{8,0},{9,1},... | collective-permute-start | bytes 24584 | tf_op jit(solution)/shard_map/ppermute | solution.py:545
  10.2 3.4 %own_transition.1 = (bf16[128,8,128]{2,1,0:T(8,128)(2,1)}, f32[3,16,128]{2,1,0:T(8,128)S(1)}, s32[2,128]{1,0:T(2,128)S(1)}, f32[1,512]{1,0:T(1,128)S(1)}, bf16[1...) custom-call(bf16[128,8,128]{2,1,0:T(8,128)(2,1)} %refs_0_.1, ...), custom_call_target="tpu_custom_call" | custom-call | tf_op jit(solution)/shard_map/own_transition/pallas_call | solution.py:564
  13.7 0.0 copy-start
  13.7 0.0 collective-permute-done.partner_ref
  13.7 0.8 %all-to-all-done.recv_ref = bf16[8,20,8,128]{3,2,1,0:T(8,128)(2,1)S(1)} async-done(((bf16[8,20,8,128]{3,2,1,0:T(8,128)(2,1)}), bf16[8,20,8,128]{3,2,1,0:T(8,128)(2,1)S(1)}, u32[]{:S(2)}, u32[]{:S(2)}) %all-to-all-start) | async-done | bytes 327712 | tf_op jit(solution)/shard_map/all_to_all | solution.py:542
  14.5 0.0 copy-done.1
  14.5 0.0 copy-done.2
  14.5 1.6 %first_half.1 = (bf16[17,8,128]{2,1,0:T(8,128)(2,1)S(1)}, bf16[2,64,640]{2,1,0:T(8,128)(2,1)S(1)}, s32[2,64]{1,0:T(2,128)S(1)}, bf16[2,192,64]{2,1,0:T(8,128)(2,...) custom-call(bf16[8,20,8,128]{3,2,1,0:T(8,128)(2,1)S(1)} %all-to-all-done.recv_ref, ...), custom_call_target="tpu_custom_call" | custom-call | tf_op jit(solution)/shard_map/first_half/pallas_call | solution.py:592
  16.1 2.6 %collective-permute-start.1 = (bf16[17,8,128]{2,1,0:T(8,128)(2,1)S(1)}, bf16[17,8,128]{2,1,0:T(8,128)(2,1)S(1)}, u32[]{:S(2)}, u32[]{:S(2)}) collective-permute-start(bf16[17,8,128]{2,1,0:T(8,128)(2,1)S(1)} %get-tuple-element.30), channel_id=1, source_target_pairs={{0,8},{1,9},{2,10},{3,11},{4,12},{5,13},{6,14},{7,15},{8,0},{9,1},... | collective-permute-start | bytes 104456 | tf_op jit(solution)/shard_map/ppermute | solution.py:613
  18.7 1.6 %second_half.1 = (f32[12,8,128]{2,1,0:T(8,128)S(1)}, f32[8,640]{1,0:T(8,128)S(1)}, f32[8,128]{1,0:T(8,128)S(1)}) custom-call(bf16[8,20,8,128]{3,2,1,0:T(8,128)(2,1)S(1)} %all-to-all-done.recv_ref, bf16[2,64,640]{2,1,0:T(8,128)(2,1)S(1)} %get-tuple-element.31.value_ref, s32[2,64]{1,0:T(2,128)S(1)} %get-tuple-element.32.near_ref, ...), custom_call_target="tpu_custom_call" | custom-call | tf_op jit(solution)/shard_map/second_half/pallas_call | solution.py:615
  20.3 0.7 %collective-permute-done.1.got_ref = bf16[17,8,128]{2,1,0:T(8,128)(2,1)S(1)} collective-permute-done((bf16[17,8,128]{2,1,0:T(8,128)(2,1)S(1)}, bf16[17,8,128]{2,1,0:T(8,128)(2,1)S(1)}, u32[]{:S(2)}, u32[]{:S(2)}) %collective-permute-start.1) | collective-permute-done | bytes 34848 | tf_op jit(solution)/shard_map/ppermute | solution.py:613
  21.0 0.0 copy-done
  21.0 1.2 %finish.1 = bf16[8,384]{1,0:T(8,128)(2,1)} custom-call(bf16[17,8,128]{2,1,0:T(8,128)(2,1)S(1)} %collective-permute-done.1.got_ref, f32[12,8,128]{2,1,0:T(8,128)S(1)} %get-tuple-element.37.sums_ref, f32[8,640]{1,0:T(8,128)S(1)} %get-tuple-element.38.wide_ref, f32[8,128]{1,0:T(8,128)S(1)} %get-tuple-element.39.level_ref, ...), custom_call_target="tpu_custom_call" | custom-call | tf_op jit(solution)/shard_map/finish/pallas_call | solution.py:629
Async XLA Ops:
  2.3 12.2 %all-to-all-start = ((bf16[8,20,8,128]{3,2,1,0:T(8,128)(2,1)}), bf16[8,20,8,128]{3,2,1,0:T(8,128)(2,1)S(1)}, u32[]{:S(2)}, u32[]{:S(2)}) async-start(bf16[8,20,8,128]{3,2,1,0:T(8,128)(2,1)} %get-tuple-element.22), calls=%async_computation | async-start | bytes 655360 | tf_op jit(solution)/shard_map/all_to_all | solution.py:542
  7.6 6.9 %copy-start.1 = (bf16[128,1024]{1,0:T(8,128)(2,1)S(1)}, bf16[128,1024]{1,0:T(8,128)(2,1)}, u32[]{:S(2)}) copy-start(bf16[128,1024]{1,0:T(8,128)(2,1)} %w_swiglu_ref.3) | copy-start | bytes 786436
  7.6 6.9 %copy-start.2 = (bf16[512,128]{1,0:T(8,128)(2,1)S(1)}, bf16[512,128]{1,0:T(8,128)(2,1)}, u32[]{:S(2)}) copy-start(bf16[512,128]{1,0:T(8,128)(2,1)} %w_down_ref.3) | copy-start | bytes 393220
  7.6 6.1 %collective-permute-start = (bf16[8,512]{1,0:T(8,128)(2,1)S(1)}, bf16[8,512]{1,0:T(8,128)(2,1)S(1)}, u32[]{:S(2)}, u32[]{:S(2)}) collective-permute-start(bf16[8,512]{1,0:T(8,128)(2,1)S(1)} %get-tuple-element.23.own_ref), channel_id=1, source_target_pairs={{0,8},{1,9},{2,10},{3,11},{4,12},{5,13},{6,14},{7,15},{8,0},{9,1},... | collective-permute-start | bytes 24584 | tf_op jit(solution)/shard_map/ppermute | solution.py:545
  13.7 7.3 %copy-start = (bf16[2112,384]{1,0:T(8,128)(2,1)S(1)}, bf16[2112,384]{1,0:T(8,128)(2,1)}, u32[]{:S(2)}) copy-start(bf16[2112,384]{1,0:T(8,128)(2,1)} %w_out_ref.1) | copy-start | bytes 4866052
  16.1 4.9 %collective-permute-start.1 = (bf16[17,8,128]{2,1,0:T(8,128)(2,1)S(1)}, bf16[17,8,128]{2,1,0:T(8,128)(2,1)S(1)}, u32[]{:S(2)}, u32[]{:S(2)}) collective-permute-start(bf16[17,8,128]{2,1,0:T(8,128)(2,1)S(1)} %get-tuple-element.30), channel_id=1, source_target_pairs={{0,8},{1,9},{2,10},{3,11},{4,12},{5,13},{6,14},{7,15},{8,0},{9,1},... | collective-permute-start | bytes 104456 | tf_op jit(solution)/shard_map/ppermute | solution.py:613

commit v6 on v5

--- a/solution.py
+++ b/solution.py
@@ -224,13 +224,9 @@
     return WEIGHT_L * (dots * (1.0 / math.sqrt(CH)) + chain + per_row(0) * distance)
 
 
-def partial_attention(
-    recv_ref, at, base, real, high_value, low_value, gain, w_swiglu_ref, w_down_ref, wb_ref,
-    pair_scr, attn_scr, sums_scr,
-):
+def pair_rows(recv_ref, at, gain, w_swiglu_ref, w_down_ref, pair_scr):
     nsrc, _, local, _ = recv_ref.shape
     n = nsrc * local
-    rows = local * HPAD
     group = max(1, min(local, 512 // n))
     for start in range(0, local, group):
         block = recv_ref[:, pl.ds(at + start, group)].astype(F32)
@@ -238,23 +234,30 @@
         done = transition(block, gain, w_swiglu_ref, w_down_ref)
         for k in range(group):
             pair_scr[start + k] = done[k * n : (k + 1) * n]
+
+
+def partial_attention(base, real, high_value, low_value, wb_ref, pair_scr, attn_scr, sums_scr):
+    local, n, _ = pair_scr.shape
+    rows = local * HPAD
     bias = jnp.concatenate([nt_dot(wb_ref[...], pair_scr[i]) for i in range(local)], axis=0)
     scores = base + WEIGHT_L * bias
     scores = jnp.where(jnp.broadcast_to(real, (rows, n)) > 0, scores, -1000000000.0)
     peak = jnp.max(scores, axis=-1, keepdims=True)
     expo = jnp.exp(scores - peak)
+    high, low = split(expo)
     total = jnp.sum(expo, axis=-1, keepdims=True)
-    high, low = split(expo / total)
+    share = 1.0 / total
     attn_scr[:rows] = high
     attn_scr[rows:] = low
     for i in range(local):
-        first = i * HPAD
-        sums_scr[first : first + HPAD, :] = jnp.dot(
-            high[first : first + HPAD], pair_scr[i], preferred_element_type=F32
+        at = i * HPAD
+        sums_scr[at : at + HPAD, :] = share[at : at + HPAD] * jnp.dot(
+            high[at : at + HPAD], pair_scr[i], preferred_element_type=F32
         )
     both = jnp.dot(attn_scr[...], high_value, preferred_element_type=F32)
     every = both[:rows] + both[rows:]
     every += jnp.dot(attn_scr[:rows], low_value, preferred_element_type=F32)
+    every *= share
     owned = head_of_lane(HPAD) == iota((HPAD, WIDE), 0)
     every = every.reshape(local, HPAD, WIDE)
     summed = jnp.sum(jnp.where(owned[None], every, 0.0), axis=1)
@@ -321,7 +324,7 @@
     for t in range(tiles):
         pts_scr[t] = points[:, t * lane : (t + 1) * lane]
     features = nt_dot(queries[:, :S], wq_ref[:FEAT, :])
-    qp_scr[...] = nt_dot(wp_ref[:QPTS, :], queries[:, :S])
+    qp_scr[:QPTS, :] = nt_dot(wp_ref[:QPTS, :], queries[:, :S])
 
     key_pts, query_pts = [], []
     for p in range(QP):
@@ -353,9 +356,11 @@
     value_ref[0] = high
     value_ref[1] = low
 
+    pair_rows(
+        recv_ref, (1 - upper) * local, gains_ref[0:1, S:], w_swiglu_ref, w_down_ref, pair_scr
+    )
     pair_sums, summed, level = partial_attention(
-        recv_ref, (1 - upper) * local, base, real, high, low,
-        gains_ref[0:1, S:], w_swiglu_ref, w_down_ref, wb_ref, pair_scr, attn_scr, sums_scr,
+        base, real, high, low, wb_ref, pair_scr, attn_scr, sums_scr
     )
     for h in range(HEADS):
         send_ref[h] = pair_sums[h].astype(BF16)
@@ -395,14 +400,16 @@
 ):
     nsrc, _, local, _ = recv_ref.shape
     me = lax.axis_index("rows")
+    pair_rows(
+        recv_ref, me // nsrc * local, gains_ref[0:1, S:], w_swiglu_ref, w_down_ref, pair_scr
+    )
     base = base_scores(
         query_ref[...], [query_pts_ref[k] for k in range(3 * QP)], keys_ref[0], keys_ref[1],
         [key_pts_ref[k] for k in range(3 * QP)], heads_ref, rows_ref[0:1, :], near_ref[0:1, :],
         me * local,
     )
     pair_sums, summed, level = partial_attention(
-        recv_ref, me // nsrc * local, base, near_ref[1:2, :], value_ref[0], value_ref[1],
-        gains_ref[0:1, S:], w_swiglu_ref, w_down_ref, wb_ref, pair_scr, attn_scr, sums_scr,
+        base, near_ref[1:2, :], value_ref[0], value_ref[1], wb_ref, pair_scr, attn_scr, sums_scr
     )
     for h in range(HEADS):
         sums_ref[h] = pair_sums[h]
@@ -604,7 +611,7 @@
         out_specs=[whole()] * 7,
         scratch_shapes=[
             pltpu.VMEM((tiles, QPTS + 3 * PLANE, near // tiles), F32),
-            pltpu.VMEM((QPTS, 2 * local), F32),
+            pltpu.VMEM((QPTS + 4 * 3 * QP, 2 * local), F32),
         ]
         + scratch,
         compiler_params=params(16 + large),

time: 22.6 us -> 22.5 us (level)
  transfers between devices with their start and end apart: 3 -> 3, of which waited for: 2 -> 2; matrix products, arithmetic and copies ran while one was open for 0% -> 0% of each run, Pallas kernels for 23% -> 22%
where the time goes in v6:
time: 22.5 us; the launch traced here: 22.2 us
  starting transfers between devices  10.5 us (47%)
  Pallas kernels  9.43 us (42%)
  waiting for transfers between devices  1.51 us (7%)
  between operations  0.69 us (3%)
    all_to_all x1, starting transfers between devices, on_device(): lax.all_to_all(packed, 'rows', 0, 0, tiled=True, axis_index_groups=halves)  5.27 us
    pallas_call x1, Pallas kernels, on_device(): pl.pallas_call(own_kernel, out_shape=[jax.ShapeDtypeStruct(pair_grid.shap...  3.44 us
    ppermute x1, starting transfers between devices, on_device(): partner = lax.ppermute(own, 'rows', across)  2.65 us
    ppermute x1, starting transfers between devices, on_device(): got = lax.ppermute(send, 'rows', across)  2.61 us
    pallas_call x1, Pallas kernels, on_device(): pl.pallas_call(pack_kernel, out_shape=[jax.ShapeDtypeStruct((nsrc, 2 * lo...  1.65 us
    pallas_call x1, Pallas kernels, on_device(): pl.pallas_call(second_kernel, out_shape=[jax.ShapeDtypeStruct((HEADS, loc...  1.55 us
    pallas_call x1, Pallas kernels, on_device(): pl.pallas_call(first_kernel, out_shape=[jax.ShapeDtypeStruct((PARTS, loca...  1.54 us
    pallas_call x1, Pallas kernels, on_device(): pl.pallas_call(finish_kernel, out_shape=jax.ShapeDtypeStruct((local, S),...  1.25 us
  transfers between devices with their start and end apart: 3, of which 2 were waited for; matrix products, arithmetic and copies ran while one was open for 0% of the time, Pallas kernels for 22%

profile of v6, /device:TPU:0, one launch (start us, length us, event | category | flops | bytes accessed | tf_op | source)
XLA Modules:
  0.0 22.2 jit_solution(17604860295201899351)
XLA Ops:
  0.6 1.7 %pack.1 = (bf16[8,20,8,128]{3,2,1,0:T(8,128)(2,1)}, bf16[8,512]{1,0:T(8,128)(2,1)S(1)}) custom-call(bf16[2,8,8,8,128]{4,3,2,1,0:T(8,128)(2,1)} %bitcast.5, bf16[8,384]{1,0:T(8,128)(2,1)} %single_hbm.1, f32[8,12]{1,0:T(8,128)} %bitcast.8), custom_call_target="tpu_custom_call" | custom-call | tf_op jit(solution)/shard_map/pack/pallas_call | solution.py:531
  2.3 5.3 %all-to-all-start = ((bf16[8,20,8,128]{3,2,1,0:T(8,128)(2,1)}), bf16[8,20,8,128]{3,2,1,0:T(8,128)(2,1)S(1)}, u32[]{:S(2)}, u32[]{:S(2)}) async-start(bf16[8,20,8,128]{3,2,1,0:T(8,128)(2,1)} %get-tuple-element.22), calls=%async_computation | async-start | bytes 655360 | tf_op jit(solution)/shard_map/all_to_all | solution.py:549
  7.6 0.0 copy-start.1
  7.6 0.0 copy-start.2
  7.6 2.7 %collective-permute-start = (bf16[8,512]{1,0:T(8,128)(2,1)S(1)}, bf16[8,512]{1,0:T(8,128)(2,1)S(1)}, u32[]{:S(2)}, u32[]{:S(2)}) collective-permute-start(bf16[8,512]{1,0:T(8,128)(2,1)S(1)} %get-tuple-element.23.own_ref), channel_id=1, source_target_pairs={{0,8},{1,9},{2,10},{3,11},{4,12},{5,13},{6,14},{7,15},{8,0},{9,1},... | collective-permute-start | bytes 24584 | tf_op jit(solution)/shard_map/ppermute | solution.py:552
  10.2 3.4 %own_transition.1 = (bf16[128,8,128]{2,1,0:T(8,128)(2,1)}, f32[3,16,128]{2,1,0:T(8,128)S(1)}, s32[2,128]{1,0:T(2,128)S(1)}, f32[1,512]{1,0:T(1,128)S(1)}, bf16[1...) custom-call(bf16[128,8,128]{2,1,0:T(8,128)(2,1)} %refs_0_.1, ...), custom_call_target="tpu_custom_call" | custom-call | tf_op jit(solution)/shard_map/own_transition/pallas_call | solution.py:571
  13.7 0.0 copy-start
  13.7 0.0 collective-permute-done.partner_ref
  13.7 0.8 %all-to-all-done.recv_ref = bf16[8,20,8,128]{3,2,1,0:T(8,128)(2,1)S(1)} async-done(((bf16[8,20,8,128]{3,2,1,0:T(8,128)(2,1)}), bf16[8,20,8,128]{3,2,1,0:T(8,128)(2,1)S(1)}, u32[]{:S(2)}, u32[]{:S(2)}) %all-to-all-start) | async-done | bytes 327712 | tf_op jit(solution)/shard_map/all_to_all | solution.py:549
  14.5 0.0 copy-done.1
  14.5 0.0 copy-done.2
  14.5 1.5 %first_half.1 = (bf16[17,8,128]{2,1,0:T(8,128)(2,1)S(1)}, bf16[2,64,640]{2,1,0:T(8,128)(2,1)S(1)}, s32[2,64]{1,0:T(2,128)S(1)}, bf16[2,192,64]{2,1,0:T(8,128)(2,...) custom-call(bf16[8,20,8,128]{3,2,1,0:T(8,128)(2,1)S(1)} %all-to-all-done.recv_ref, ...), custom_call_target="tpu_custom_call" | custom-call | tf_op jit(solution)/shard_map/first_half/pallas_call | solution.py:599
  16.0 2.6 %collective-permute-start.1 = (bf16[17,8,128]{2,1,0:T(8,128)(2,1)S(1)}, bf16[17,8,128]{2,1,0:T(8,128)(2,1)S(1)}, u32[]{:S(2)}, u32[]{:S(2)}) collective-permute-start(bf16[17,8,128]{2,1,0:T(8,128)(2,1)S(1)} %get-tuple-element.30), channel_id=1, source_target_pairs={{0,8},{1,9},{2,10},{3,11},{4,12},{5,13},{6,14},{7,15},{8,0},{9,1},... | collective-permute-start | bytes 104456 | tf_op jit(solution)/shard_map/ppermute | solution.py:620
  18.6 1.5 %second_half.1 = (f32[12,8,128]{2,1,0:T(8,128)S(1)}, f32[8,640]{1,0:T(8,128)S(1)}, f32[8,128]{1,0:T(8,128)S(1)}) custom-call(bf16[8,20,8,128]{3,2,1,0:T(8,128)(2,1)S(1)} %all-to-all-done.recv_ref, bf16[2,64,640]{2,1,0:T(8,128)(2,1)S(1)} %get-tuple-element.31.value_ref, s32[2,64]{1,0:T(2,128)S(1)} %get-tuple-element.32.near_ref, ...), custom_call_target="tpu_custom_call" | custom-call | tf_op jit(solution)/shard_map/second_half/pallas_call | solution.py:622
  20.2 0.7 %collective-permute-done.1.got_ref = bf16[17,8,128]{2,1,0:T(8,128)(2,1)S(1)} collective-permute-done((bf16[17,8,128]{2,1,0:T(8,128)(2,1)S(1)}, bf16[17,8,128]{2,1,0:T(8,128)(2,1)S(1)}, u32[]{:S(2)}, u32[]{:S(2)}) %collective-permute-start.1) | collective-permute-done | bytes 34848 | tf_op jit(solution)/shard_map/ppermute | solution.py:620
  20.9 0.0 copy-done
  20.9 1.2 %finish.1 = bf16[8,384]{1,0:T(8,128)(2,1)} custom-call(bf16[17,8,128]{2,1,0:T(8,128)(2,1)S(1)} %collective-permute-done.1.got_ref, f32[12,8,128]{2,1,0:T(8,128)S(1)} %get-tuple-element.37.sums_ref, f32[8,640]{1,0:T(8,128)S(1)} %get-tuple-element.38.wide_ref, f32[8,128]{1,0:T(8,128)S(1)} %get-tuple-element.39.level_ref, ...), custom_call_target="tpu_custom_call" | custom-call | tf_op jit(solution)/shard_map/finish/pallas_call | solution.py:636
Async XLA Ops:
  2.3 12.2 %all-to-all-start = ((bf16[8,20,8,128]{3,2,1,0:T(8,128)(2,1)}), bf16[8,20,8,128]{3,2,1,0:T(8,128)(2,1)S(1)}, u32[]{:S(2)}, u32[]{:S(2)}) async-start(bf16[8,20,8,128]{3,2,1,0:T(8,128)(2,1)} %get-tuple-element.22), calls=%async_computation | async-start | bytes 655360 | tf_op jit(solution)/shard_map/all_to_all | solution.py:549
  7.6 6.9 %copy-start.1 = (bf16[128,1024]{1,0:T(8,128)(2,1)S(1)}, bf16[128,1024]{1,0:T(8,128)(2,1)}, u32[]{:S(2)}) copy-start(bf16[128,1024]{1,0:T(8,128)(2,1)} %w_swiglu_ref.3) | copy-start | bytes 786436
  7.6 6.9 %copy-start.2 = (bf16[512,128]{1,0:T(8,128)(2,1)S(1)}, bf16[512,128]{1,0:T(8,128)(2,1)}, u32[]{:S(2)}) copy-start(bf16[512,128]{1,0:T(8,128)(2,1)} %w_down_ref.3) | copy-start | bytes 393220
  7.6 6.1 %collective-permute-start = (bf16[8,512]{1,0:T(8,128)(2,1)S(1)}, bf16[8,512]{1,0:T(8,128)(2,1)S(1)}, u32[]{:S(2)}, u32[]{:S(2)}) collective-permute-start(bf16[8,512]{1,0:T(8,128)(2,1)S(1)} %get-tuple-element.23.own_ref), channel_id=1, source_target_pairs={{0,8},{1,9},{2,10},{3,11},{4,12},{5,13},{6,14},{7,15},{8,0},{9,1},... | collective-permute-start | bytes 24584 | tf_op jit(solution)/shard_map/ppermute | solution.py:552
  13.7 7.2 %copy-start = (bf16[2112,384]{1,0:T(8,128)(2,1)S(1)}, bf16[2112,384]{1,0:T(8,128)(2,1)}, u32[]{:S(2)}) copy-start(bf16[2112,384]{1,0:T(8,128)(2,1)} %w_out_ref.1) | copy-start | bytes 4866052
  16.0 4.9 %collective-permute-start.1 = (bf16[17,8,128]{2,1,0:T(8,128)(2,1)S(1)}, bf16[17,8,128]{2,1,0:T(8,128)(2,1)S(1)}, u32[]{:S(2)}, u32[]{:S(2)}) collective-permute-start(bf16[17,8,128]{2,1,0:T(8,128)(2,1)S(1)} %get-tuple-element.30), channel_id=1, source_target_pairs={{0,8},{1,9},{2,10},{3,11},{4,12},{5,13},{6,14},{7,15},{8,0},{9,1},... | collective-permute-start | bytes 104456 | tf_op jit(solution)/shard_map/ppermute | solution.py:620

commit v7 on v6

--- a/solution.py
+++ b/solution.py
@@ -64,19 +64,20 @@
     nsrc = pair_ref.shape[0]
     local = own_ref.shape[0]
     step = max(1, nsrc // 4)
-    chunks = [(half, at) for at in range(0, nsrc, step) for half in range(2)]
+    upper = lax.axis_index("rows") // nsrc
+    starts = range(0, nsrc, step)
     arrivals = []
-    for k, (half, at) in enumerate(chunks):
-        arrivals.append(
-            pltpu.make_async_copy(
-                pair_hbm.at[half, pl.ds(at, step)],
-                pair_ref.at[pl.ds(at, step), pl.ds(half * local, local)],
-                in_sems.at[k],
-            )
-        )
+    for at in starts:
+        mine = [(pair_hbm.at[upper, pl.ds(at, step)], pair_ref.at[pl.ds(at, step), pl.ds(0, local)])]
+        theirs = [
+            (pair_hbm.at[1 - upper, dest ^ 1], pair_ref.at[dest, pl.ds(local, local)])
+            for dest in range(at, at + step)
+        ]
+        for source, target in mine + theirs:
+            arrivals.append(pltpu.make_async_copy(source, target, in_sems.at[len(arrivals)]))
     rows_copies = [
-        pltpu.make_async_copy(single_hbm, own_ref.at[:, :S], in_sems.at[len(chunks)]),
-        pltpu.make_async_copy(frames_hbm, frames_ref, in_sems.at[len(chunks) + 1]),
+        pltpu.make_async_copy(single_hbm, own_ref.at[:, :S], in_sems.at[len(arrivals)]),
+        pltpu.make_async_copy(frames_hbm, frames_ref, in_sems.at[len(arrivals) + 1]),
     ]
     for copy in rows_copies + arrivals:
         copy.start()
@@ -97,15 +98,14 @@
         pltpu.make_async_copy(small_ref, out_hbm.at[:, pl.ds(2 * local, SMALL)], out_sems.at[0])
     ]
     departures[0].start()
-    for k in range(0, len(chunks), 2):
-        arrivals[k].wait()
-        arrivals[k + 1].wait()
-        at = chunks[k][1]
+    for k, at in enumerate(starts):
+        for copy in arrivals[k * (step + 1) : (k + 1) * (step + 1)]:
+            copy.wait()
         departures.append(
             pltpu.make_async_copy(
                 pair_ref.at[pl.ds(at, step)],
                 out_hbm.at[pl.ds(at, step), pl.ds(0, 2 * local)],
-                out_sems.at[1 + k // 2],
+                out_sems.at[1 + k],
             )
         )
         departures[-1].start()
@@ -344,7 +344,7 @@
     near_ref[1:2, :] = real
     base = base_scores(
         features[:local], query_pts, high_keys, low_keys, key_pts, heads_ref, chain_all, chain_row,
-        jnp.bitwise_xor(me, nsrc) * local,
+        jnp.bitwise_xor(me, nsrc + 1) * local,
     )
 
     planes = place(frames, [strided(pts_scr, QPTS + y, PLANE, 3) for y in range(3)])
@@ -357,7 +357,7 @@
     value_ref[1] = low
 
     pair_rows(
-        recv_ref, (1 - upper) * local, gains_ref[0:1, S:], w_swiglu_ref, w_down_ref, pair_scr
+        recv_ref, local, gains_ref[0:1, S:], w_swiglu_ref, w_down_ref, pair_scr
     )
     pair_sums, summed, level = partial_attention(
         base, real, high, low, wb_ref, pair_scr, attn_scr, sums_scr
@@ -401,7 +401,7 @@
     nsrc, _, local, _ = recv_ref.shape
     me = lax.axis_index("rows")
     pair_rows(
-        recv_ref, me // nsrc * local, gains_ref[0:1, S:], w_swiglu_ref, w_down_ref, pair_scr
+        recv_ref, 0, gains_ref[0:1, S:], w_swiglu_ref, w_down_ref, pair_scr
     )
     base = base_scores(
         query_ref[...], [query_pts_ref[k] for k in range(3 * QP)], keys_ref[0], keys_ref[1],
@@ -526,7 +526,7 @@
     tiles = max(1, near // 128)
     large = 4 * (n // 128)
     halves = [list(range(nsrc)), list(range(nsrc, size))]
-    across = [(i, i ^ nsrc) for i in range(size)]
+    across = [(i, i ^ (nsrc + 1)) for i in range(size)]
 
     packed, own = pl.pallas_call(
         pack_kernel,
@@ -540,7 +540,7 @@
             pltpu.VMEM((nsrc, 2 * local, local, C), BF16),
             pltpu.VMEM((nsrc, SMALL, local, C), BF16),
             pltpu.VMEM((local, 12), F32),
-            pltpu.SemaphoreType.DMA((10,)),
+            pltpu.SemaphoreType.DMA((nsrc + 6,)),
             pltpu.SemaphoreType.DMA((5,)),
         ],
         compiler_params=params(4 + large),

time: 22.5 us -> 22.2 us (0.987)
  starting transfers between devices: 10.5 us -> 9.81 us
  waiting for transfers between devices: 1.51 us -> 1.82 us
    ppermute x1, starting transfers between devices: 2.61 us -> 1.84 us  [on_device(): got = lax.ppermute(send, 'rows', across)]
    ppermute x1, waiting for transfers between devices: 0.74 us -> 1.09 us  [on_device(): got = lax.ppermute(send, 'rows', across)]
  transfers between devices with their start and end apart: 3 -> 3, of which waited for: 2 -> 2; matrix products, arithmetic and copies ran while one was open for 0% -> 0% of each run, Pallas kernels for 22% -> 23%
where the time goes in v7:
time: 22.2 us; the launch traced here: 21.8 us
  starting transfers between devices  9.81 us (44%)
  Pallas kernels  9.51 us (43%)
  waiting for transfers between devices  1.82 us (8%)
  between operations  0.69 us (3%)
    all_to_all x1, starting transfers between devices, on_device(): lax.all_to_all(packed, 'rows', 0, 0, tiled=True, axis_index_groups=halves)  5.27 us
    pallas_call x1, Pallas kernels, on_device(): pl.pallas_call(own_kernel, out_shape=[jax.ShapeDtypeStruct(pair_grid.shap...  3.44 us
    ppermute x1, starting transfers between devices, on_device(): partner = lax.ppermute(own, 'rows', across)  2.7 us
    ppermute x1, starting transfers between devices, on_device(): got = lax.ppermute(send, 'rows', across)  1.84 us
    pallas_call x1, Pallas kernels, on_device(): pl.pallas_call(pack_kernel, out_shape=[jax.ShapeDtypeStruct((nsrc, 2 * lo...  1.7 us
    pallas_call x1, Pallas kernels, on_device(): pl.pallas_call(first_kernel, out_shape=[jax.ShapeDtypeStruct((PARTS, loca...  1.56 us
    pallas_call x1, Pallas kernels, on_device(): pl.pallas_call(second_kernel, out_shape=[jax.ShapeDtypeStruct((HEADS, loc...  1.56 us
    pallas_call x1, Pallas kernels, on_device(): pl.pallas_call(finish_kernel, out_shape=jax.ShapeDtypeStruct((local, S),...  1.25 us
  transfers between devices with their start and end apart: 3, of which 2 were waited for; matrix products, arithmetic and copies ran while one was open for 0% of the time, Pallas kernels for 23%

profile of v7, /device:TPU:0, one launch (start us, length us, event | category | flops | bytes accessed | tf_op | source)
XLA Modules:
  0.0 21.8 jit_solution(10859292781911951190)
XLA Ops:
  0.6 1.7 %pack.1 = (bf16[8,20,8,128]{3,2,1,0:T(8,128)(2,1)}, bf16[8,512]{1,0:T(8,128)(2,1)S(1)}) custom-call(bf16[2,8,8,8,128]{4,3,2,1,0:T(8,128)(2,1)} %bitcast.5, bf16[8,384]{1,0:T(8,128)(2,1)} %single_hbm.1, f32[8,12]{1,0:T(8,128)} %bitcast.8), custom_call_target="tpu_custom_call" | custom-call | tf_op jit(solution)/shard_map/pack/pallas_call | solution.py:531
  2.3 5.3 %all-to-all-start = ((bf16[8,20,8,128]{3,2,1,0:T(8,128)(2,1)}), bf16[8,20,8,128]{3,2,1,0:T(8,128)(2,1)S(1)}, u32[]{:S(2)}, u32[]{:S(2)}) async-start(bf16[8,20,8,128]{3,2,1,0:T(8,128)(2,1)} %get-tuple-element.22), calls=%async_computation | async-start | bytes 655360 | tf_op jit(solution)/shard_map/all_to_all | solution.py:549
  7.6 0.0 copy-start.1
  7.6 0.0 copy-start.2
  7.6 2.7 %collective-permute-start = (bf16[8,512]{1,0:T(8,128)(2,1)S(1)}, bf16[8,512]{1,0:T(8,128)(2,1)S(1)}, u32[]{:S(2)}, u32[]{:S(2)}) collective-permute-start(bf16[8,512]{1,0:T(8,128)(2,1)S(1)} %get-tuple-element.23.own_ref), channel_id=1, source_target_pairs={{0,9},{1,8},{2,11},{3,10},{4,13},{5,12},{6,15},{7,14},{8,1},{9,0},... | collective-permute-start | bytes 24584 | tf_op jit(solution)/shard_map/ppermute | solution.py:552
  10.3 3.4 %own_transition.1 = (bf16[128,8,128]{2,1,0:T(8,128)(2,1)}, f32[3,16,128]{2,1,0:T(8,128)S(1)}, s32[2,128]{1,0:T(2,128)S(1)}, f32[1,512]{1,0:T(1,128)S(1)}, bf16[1...) custom-call(bf16[128,8,128]{2,1,0:T(8,128)(2,1)} %refs_0_.1, ...), custom_call_target="tpu_custom_call" | custom-call | tf_op jit(solution)/shard_map/own_transition/pallas_call | solution.py:571
  13.8 0.0 copy-start
  13.8 0.0 collective-permute-done.partner_ref
  13.8 0.7 %all-to-all-done.recv_ref = bf16[8,20,8,128]{3,2,1,0:T(8,128)(2,1)S(1)} async-done(((bf16[8,20,8,128]{3,2,1,0:T(8,128)(2,1)}), bf16[8,20,8,128]{3,2,1,0:T(8,128)(2,1)S(1)}, u32[]{:S(2)}, u32[]{:S(2)}) %all-to-all-start) | async-done | bytes 327712 | tf_op jit(solution)/shard_map/all_to_all | solution.py:549
  14.5 0.0 copy-done.1
  14.5 0.0 copy-done.2
  14.5 1.6 %first_half.1 = (bf16[17,8,128]{2,1,0:T(8,128)(2,1)S(1)}, bf16[2,64,640]{2,1,0:T(8,128)(2,1)S(1)}, s32[2,64]{1,0:T(2,128)S(1)}, bf16[2,192,64]{2,1,0:T(8,128)(2,...) custom-call(bf16[8,20,8,128]{3,2,1,0:T(8,128)(2,1)S(1)} %all-to-all-done.recv_ref, ...), custom_call_target="tpu_custom_call" | custom-call | tf_op jit(solution)/shard_map/first_half/pallas_call | solution.py:599
  16.1 1.8 %collective-permute-start.1 = (bf16[17,8,128]{2,1,0:T(8,128)(2,1)S(1)}, bf16[17,8,128]{2,1,0:T(8,128)(2,1)S(1)}, u32[]{:S(2)}, u32[]{:S(2)}) collective-permute-start(bf16[17,8,128]{2,1,0:T(8,128)(2,1)S(1)} %get-tuple-element.30), channel_id=1, source_target_pairs={{0,9},{1,8},{2,11},{3,10},{4,13},{5,12},{6,15},{7,14},{8,1},{9,0},... | collective-permute-start | bytes 104456 | tf_op jit(solution)/shard_map/ppermute | solution.py:620
  17.9 1.6 %second_half.1 = (f32[12,8,128]{2,1,0:T(8,128)S(1)}, f32[8,640]{1,0:T(8,128)S(1)}, f32[8,128]{1,0:T(8,128)S(1)}) custom-call(bf16[8,20,8,128]{3,2,1,0:T(8,128)(2,1)S(1)} %all-to-all-done.recv_ref, bf16[2,64,640]{2,1,0:T(8,128)(2,1)S(1)} %get-tuple-element.31.value_ref, s32[2,64]{1,0:T(2,128)S(1)} %get-tuple-element.32.near_ref, ...), custom_call_target="tpu_custom_call" | custom-call | tf_op jit(solution)/shard_map/second_half/pallas_call | solution.py:622
  19.5 1.1 %collective-permute-done.1.got_ref = bf16[17,8,128]{2,1,0:T(8,128)(2,1)S(1)} collective-permute-done((bf16[17,8,128]{2,1,0:T(8,128)(2,1)S(1)}, bf16[17,8,128]{2,1,0:T(8,128)(2,1)S(1)}, u32[]{:S(2)}, u32[]{:S(2)}) %collective-permute-start.1) | collective-permute-done | bytes 34848 | tf_op jit(solution)/shard_map/ppermute | solution.py:620
  20.6 0.0 copy-done
  20.6 1.2 %finish.1 = bf16[8,384]{1,0:T(8,128)(2,1)} custom-call(bf16[17,8,128]{2,1,0:T(8,128)(2,1)S(1)} %collective-permute-done.1.got_ref, f32[12,8,128]{2,1,0:T(8,128)S(1)} %get-tuple-element.37.sums_ref, f32[8,640]{1,0:T(8,128)S(1)} %get-tuple-element.38.wide_ref, f32[8,128]{1,0:T(8,128)S(1)} %get-tuple-element.39.level_ref, ...), custom_call_target="tpu_custom_call" | custom-call | tf_op jit(solution)/shard_map/finish/pallas_call | solution.py:636
Async XLA Ops:
  2.3 12.2 %all-to-all-start = ((bf16[8,20,8,128]{3,2,1,0:T(8,128)(2,1)}), bf16[8,20,8,128]{3,2,1,0:T(8,128)(2,1)S(1)}, u32[]{:S(2)}, u32[]{:S(2)}) async-start(bf16[8,20,8,128]{3,2,1,0:T(8,128)(2,1)} %get-tuple-element.22), calls=%async_computation | async-start | bytes 655360 | tf_op jit(solution)/shard_map/all_to_all | solution.py:549
  7.6 6.9 %copy-start.1 = (bf16[128,1024]{1,0:T(8,128)(2,1)S(1)}, bf16[128,1024]{1,0:T(8,128)(2,1)}, u32[]{:S(2)}) copy-start(bf16[128,1024]{1,0:T(8,128)(2,1)} %w_swiglu_ref.3) | copy-start | bytes 786436
  7.6 6.9 %copy-start.2 = (bf16[512,128]{1,0:T(8,128)(2,1)S(1)}, bf16[512,128]{1,0:T(8,128)(2,1)}, u32[]{:S(2)}) copy-start(bf16[512,128]{1,0:T(8,128)(2,1)} %w_down_ref.3) | copy-start | bytes 393220
  7.6 6.2 %collective-permute-start = (bf16[8,512]{1,0:T(8,128)(2,1)S(1)}, bf16[8,512]{1,0:T(8,128)(2,1)S(1)}, u32[]{:S(2)}, u32[]{:S(2)}) collective-permute-start(bf16[8,512]{1,0:T(8,128)(2,1)S(1)} %get-tuple-element.23.own_ref), channel_id=1, source_target_pairs={{0,9},{1,8},{2,11},{3,10},{4,13},{5,12},{6,15},{7,14},{8,1},{9,0},... | collective-permute-start | bytes 24584 | tf_op jit(solution)/shard_map/ppermute | solution.py:552
  13.8 6.8 %copy-start = (bf16[2112,384]{1,0:T(8,128)(2,1)S(1)}, bf16[2112,384]{1,0:T(8,128)(2,1)}, u32[]{:S(2)}) copy-start(bf16[2112,384]{1,0:T(8,128)(2,1)} %w_out_ref.1) | copy-start | bytes 4866052
  16.1 4.5 %collective-permute-start.1 = (bf16[17,8,128]{2,1,0:T(8,128)(2,1)S(1)}, bf16[17,8,128]{2,1,0:T(8,128)(2,1)S(1)}, u32[]{:S(2)}, u32[]{:S(2)}) collective-permute-start(bf16[17,8,128]{2,1,0:T(8,128)(2,1)S(1)} %get-tuple-element.30), channel_id=1, source_target_pairs={{0,9},{1,8},{2,11},{3,10},{4,13},{5,12},{6,15},{7,14},{8,1},{9,0},... | collective-permute-start | bytes 104456 | tf_op jit(solution)/shard_map/ppermute | solution.py:620

commit v8 on v7

--- a/solution.py
+++ b/solution.py
@@ -272,6 +272,19 @@
 def origin(row_ref):
     parts = row_ref[:, S:].astype(F32)
     return parts[:, 0:12] + parts[:, 12:24] + parts[:, 24:36]
+
+
+def into_frame(row_ref, summed):
+    turned = origin(row_ref)
+    shifted = [
+        summed[:, 256 + 128 * x : 384 + 128 * x] - turned[:, 9 + x : 10 + x] for x in range(3)
+    ]
+    return [
+        turned[:, y : y + 1] * shifted[0]
+        + turned[:, 3 + y : 4 + y] * shifted[1]
+        + turned[:, 6 + y : 7 + y] * shifted[2]
+        for y in range(3)
+    ]
 
 
 def first_kernel(
@@ -364,7 +377,7 @@
     )
     for h in range(HEADS):
         send_ref[h] = pair_sums[h].astype(BF16)
-    turned = origin(partner_ref)
+    planes = into_frame(partner_ref, summed)
     send_ref[HEADS] = summed[:, :128].astype(BF16)
     send_ref[HEADS + 1] = summed[:, 128:256].astype(BF16)
     high = level.astype(BF16).astype(F32)
@@ -372,7 +385,7 @@
     low = level - high - middle
     blank = jnp.zeros((local, 128 - PLANE - HPAD), F32)
     for x, part in enumerate([high, middle, low]):
-        plane = summed[:, 256 + 128 * x : 256 + 128 * x + PLANE] - turned[:, 9 + x : 10 + x]
+        plane = planes[x][:, :PLANE]
         send_ref[HEADS + 2 + x] = jnp.concatenate([plane, part, blank], axis=1).astype(BF16)
 
 
@@ -413,11 +426,9 @@
     )
     for h in range(HEADS):
         sums_ref[h] = pair_sums[h]
-    turned = origin(own_ref)
     wide_ref[:, :256] = summed[:, :256]
-    for x in range(3):
-        at = 256 + 128 * x
-        wide_ref[:, at : at + 128] = summed[:, at : at + 128] - turned[:, 9 + x : 10 + x]
+    for x, plane in enumerate(into_frame(own_ref, summed)):
+        wide_ref[:, 256 + 128 * x : 384 + 128 * x] = plane
     level_ref[...] = jnp.concatenate(
         [jnp.zeros((local, PLANE), F32), level, jnp.zeros((local, 128 - PLANE - HPAD), F32)], axis=1
     )
@@ -458,34 +469,29 @@
         joined(0, low_share, got_ref[HEADS].astype(F32)),
         joined(128, high_share, got_ref[HEADS + 1].astype(F32)),
     ]
-    shifted = [joined(256 + 128 * x, plane_share, planes[x]) for x in range(3)]
-
-    turned = origin(own_ref)
-    local_out = [
-        turned[:, y : y + 1] * shifted[0]
-        + turned[:, 3 + y : 4 + y] * shifted[1]
-        + turned[:, 6 + y : 7 + y] * shifted[2]
-        for y in range(3)
-    ]
-    lengths = jnp.sqrt(
-        local_out[0] * local_out[0] + local_out[1] * local_out[1] + local_out[2] * local_out[2] + 1.0
-    )
-    update = jnp.dot(
+    local_out = [joined(256 + 128 * x, plane_share, planes[x]) for x in range(3)]
+
+    pair_total = jnp.concatenate(pair_total, axis=1).astype(BF16)
+    at = FEAT + 4 * PLANE
+    update = jnp.dot(pair_total, w_out_ref[at:, :], preferred_element_type=F32)
+    update += jnp.dot(
         jnp.concatenate(features, axis=1)[:, :FEAT].astype(BF16),
         w_out_ref[:FEAT, :],
         preferred_element_type=F32,
+    )
+
+    lengths = jnp.sqrt(
+        local_out[0] * local_out[0] + local_out[1] * local_out[1] + local_out[2] * local_out[2] + 1.0
     )
     for y in range(3):
         update += jnp.dot(
             local_out[y][:, :PLANE].astype(BF16), w_loc_ref[y], preferred_element_type=F32
         )
-    at = FEAT + 3 * PLANE
     update += jnp.dot(
-        lengths[:, :PLANE].astype(BF16), w_out_ref[at : at + PLANE, :], preferred_element_type=F32
-    )
-    at += PLANE
-    pair_total = jnp.concatenate(pair_total, axis=1).astype(BF16)
-    update += jnp.dot(pair_total, w_out_ref[at:, :], preferred_element_type=F32)
+        lengths[:, :PLANE].astype(BF16),
+        w_out_ref[at - PLANE : at, :],
+        preferred_element_type=F32,
+    )
     own_single = own_ref[:, :S].astype(F32)
     out_ref[...] = layer_norm(own_single + update, gains_ref[0:1, :S]).astype(BF16)
 

time: 22.2 us -> 22.1 us (level)
  no operation moved by 1% of the time
where the time goes in v8:
time: 22.1 us; the launch traced here: 21.8 us
  starting transfers between devices  9.8 us (44%)
  Pallas kernels  9.49 us (43%)
  waiting for transfers between devices  1.8 us (8%)
  between operations  0.69 us (3%)
    all_to_all x1, starting transfers between devices, on_device(): lax.all_to_all(packed, 'rows', 0, 0, tiled=True, axis_index_groups=halves)  5.27 us
    pallas_call x1, Pallas kernels, on_device(): pl.pallas_call(own_kernel, out_shape=[jax.ShapeDtypeStruct(pair_grid.shap...  3.44 us
    ppermute x1, starting transfers between devices, on_device(): partner = lax.ppermute(own, 'rows', across)  2.7 us
    ppermute x1, starting transfers between devices, on_device(): got = lax.ppermute(send, 'rows', across)  1.84 us
    pallas_call x1, Pallas kernels, on_device(): pl.pallas_call(pack_kernel, out_shape=[jax.ShapeDtypeStruct((nsrc, 2 * lo...  1.7 us
    pallas_call x1, Pallas kernels, on_device(): pl.pallas_call(second_kernel, out_shape=[jax.ShapeDtypeStruct((HEADS, loc...  1.58 us
    pallas_call x1, Pallas kernels, on_device(): pl.pallas_call(first_kernel, out_shape=[jax.ShapeDtypeStruct((PARTS, loca...  1.58 us
    pallas_call x1, Pallas kernels, on_device(): pl.pallas_call(finish_kernel, out_shape=jax.ShapeDtypeStruct((local, S),...  1.19 us
  transfers between devices with their start and end apart: 3, of which 2 were waited for; matrix products, arithmetic and copies ran while one was open for 0% of the time, Pallas kernels for 23%

profile of v8, /device:TPU:0, one launch (start us, length us, event | category | flops | bytes accessed | tf_op | source)
XLA Modules:
  0.0 21.8 jit_solution(212637700761825733)
XLA Ops:
  0.6 1.7 %pack.1 = (bf16[8,20,8,128]{3,2,1,0:T(8,128)(2,1)}, bf16[8,512]{1,0:T(8,128)(2,1)S(1)}) custom-call(bf16[2,8,8,8,128]{4,3,2,1,0:T(8,128)(2,1)} %bitcast.5, bf16[8,384]{1,0:T(8,128)(2,1)} %single_hbm.1, f32[8,12]{1,0:T(8,128)} %bitcast.8), custom_call_target="tpu_custom_call" | custom-call | tf_op jit(solution)/shard_map/pack/pallas_call | solution.py:537
  2.3 5.3 %all-to-all-start = ((bf16[8,20,8,128]{3,2,1,0:T(8,128)(2,1)}), bf16[8,20,8,128]{3,2,1,0:T(8,128)(2,1)S(1)}, u32[]{:S(2)}, u32[]{:S(2)}) async-start(bf16[8,20,8,128]{3,2,1,0:T(8,128)(2,1)} %get-tuple-element.22), calls=%async_computation | async-start | bytes 655360 | tf_op jit(solution)/shard_map/all_to_all | solution.py:555
  7.6 0.0 copy-start.1
  7.6 0.0 copy-start.2
  7.6 2.7 %collective-permute-start = (bf16[8,512]{1,0:T(8,128)(2,1)S(1)}, bf16[8,512]{1,0:T(8,128)(2,1)S(1)}, u32[]{:S(2)}, u32[]{:S(2)}) collective-permute-start(bf16[8,512]{1,0:T(8,128)(2,1)S(1)} %get-tuple-element.23.own_ref), channel_id=1, source_target_pairs={{0,9},{1,8},{2,11},{3,10},{4,13},{5,12},{6,15},{7,14},{8,1},{9,0},... | collective-permute-start | bytes 24584 | tf_op jit(solution)/shard_map/ppermute | solution.py:558
  10.3 3.4 %own_transition.1 = (bf16[128,8,128]{2,1,0:T(8,128)(2,1)}, f32[3,16,128]{2,1,0:T(8,128)S(1)}, s32[2,128]{1,0:T(2,128)S(1)}, f32[1,512]{1,0:T(1,128)S(1)}, bf16[1...) custom-call(bf16[128,8,128]{2,1,0:T(8,128)(2,1)} %refs_0_.1, ...), custom_call_target="tpu_custom_call" | custom-call | tf_op jit(solution)/shard_map/own_transition/pallas_call | solution.py:577
  13.8 0.0 copy-start
  13.8 0.0 collective-permute-done.partner_ref
  13.8 0.7 %all-to-all-done.recv_ref = bf16[8,20,8,128]{3,2,1,0:T(8,128)(2,1)S(1)} async-done(((bf16[8,20,8,128]{3,2,1,0:T(8,128)(2,1)}), bf16[8,20,8,128]{3,2,1,0:T(8,128)(2,1)S(1)}, u32[]{:S(2)}, u32[]{:S(2)}) %all-to-all-start) | async-done | bytes 327712 | tf_op jit(solution)/shard_map/all_to_all | solution.py:555
  14.5 0.0 copy-done.1
  14.5 0.0 copy-done.2
  14.5 1.6 %first_half.1 = (bf16[17,8,128]{2,1,0:T(8,128)(2,1)S(1)}, bf16[2,64,640]{2,1,0:T(8,128)(2,1)S(1)}, s32[2,64]{1,0:T(2,128)S(1)}, bf16[2,192,64]{2,1,0:T(8,128)(2,...) custom-call(bf16[8,20,8,128]{3,2,1,0:T(8,128)(2,1)S(1)} %all-to-all-done.recv_ref, ...), custom_call_target="tpu_custom_call" | custom-call | tf_op jit(solution)/shard_map/first_half/pallas_call | solution.py:605
  16.1 1.8 %collective-permute-start.1 = (bf16[17,8,128]{2,1,0:T(8,128)(2,1)S(1)}, bf16[17,8,128]{2,1,0:T(8,128)(2,1)S(1)}, u32[]{:S(2)}, u32[]{:S(2)}) collective-permute-start(bf16[17,8,128]{2,1,0:T(8,128)(2,1)S(1)} %get-tuple-element.30), channel_id=1, source_target_pairs={{0,9},{1,8},{2,11},{3,10},{4,13},{5,12},{6,15},{7,14},{8,1},{9,0},... | collective-permute-start | bytes 104456 | tf_op jit(solution)/shard_map/ppermute | solution.py:626
  17.9 1.6 %second_half.1 = (f32[12,8,128]{2,1,0:T(8,128)S(1)}, f32[8,640]{1,0:T(8,128)S(1)}, f32[8,128]{1,0:T(8,128)S(1)}) custom-call(bf16[8,20,8,128]{3,2,1,0:T(8,128)(2,1)S(1)} %all-to-all-done.recv_ref, bf16[2,64,640]{2,1,0:T(8,128)(2,1)S(1)} %get-tuple-element.31.value_ref, s32[2,64]{1,0:T(2,128)S(1)} %get-tuple-element.32.near_ref, ...), custom_call_target="tpu_custom_call" | custom-call | tf_op jit(solution)/shard_map/second_half/pallas_call | solution.py:628
  19.5 1.1 %collective-permute-done.1.got_ref = bf16[17,8,128]{2,1,0:T(8,128)(2,1)S(1)} collective-permute-done((bf16[17,8,128]{2,1,0:T(8,128)(2,1)S(1)}, bf16[17,8,128]{2,1,0:T(8,128)(2,1)S(1)}, u32[]{:S(2)}, u32[]{:S(2)}) %collective-permute-start.1) | collective-permute-done | bytes 34848 | tf_op jit(solution)/shard_map/ppermute | solution.py:626
  20.6 0.0 copy-done
  20.6 1.2 %finish.1 = bf16[8,384]{1,0:T(8,128)(2,1)} custom-call(bf16[17,8,128]{2,1,0:T(8,128)(2,1)S(1)} %collective-permute-done.1.got_ref, f32[12,8,128]{2,1,0:T(8,128)S(1)} %get-tuple-element.37.sums_ref, f32[8,640]{1,0:T(8,128)S(1)} %get-tuple-element.38.wide_ref, f32[8,128]{1,0:T(8,128)S(1)} %get-tuple-element.39.level_ref, ...), custom_call_target="tpu_custom_call" | custom-call | tf_op jit(solution)/shard_map/finish/pallas_call | solution.py:642
Async XLA Ops:
  2.3 12.2 %all-to-all-start = ((bf16[8,20,8,128]{3,2,1,0:T(8,128)(2,1)}), bf16[8,20,8,128]{3,2,1,0:T(8,128)(2,1)S(1)}, u32[]{:S(2)}, u32[]{:S(2)}) async-start(bf16[8,20,8,128]{3,2,1,0:T(8,128)(2,1)} %get-tuple-element.22), calls=%async_computation | async-start | bytes 655360 | tf_op jit(solution)/shard_map/all_to_all | solution.py:555
  7.6 6.9 %copy-start.1 = (bf16[128,1024]{1,0:T(8,128)(2,1)S(1)}, bf16[128,1024]{1,0:T(8,128)(2,1)}, u32[]{:S(2)}) copy-start(bf16[128,1024]{1,0:T(8,128)(2,1)} %w_swiglu_ref.3) | copy-start | bytes 786436
  7.6 6.9 %copy-start.2 = (bf16[512,128]{1,0:T(8,128)(2,1)S(1)}, bf16[512,128]{1,0:T(8,128)(2,1)}, u32[]{:S(2)}) copy-start(bf16[512,128]{1,0:T(8,128)(2,1)} %w_down_ref.3) | copy-start | bytes 393220
  7.6 6.2 %collective-permute-start = (bf16[8,512]{1,0:T(8,128)(2,1)S(1)}, bf16[8,512]{1,0:T(8,128)(2,1)S(1)}, u32[]{:S(2)}, u32[]{:S(2)}) collective-permute-start(bf16[8,512]{1,0:T(8,128)(2,1)S(1)} %get-tuple-element.23.own_ref), channel_id=1, source_target_pairs={{0,9},{1,8},{2,11},{3,10},{4,13},{5,12},{6,15},{7,14},{8,1},{9,0},... | collective-permute-start | bytes 24584 | tf_op jit(solution)/shard_map/ppermute | solution.py:558
  13.8 6.8 %copy-start = (bf16[2112,384]{1,0:T(8,128)(2,1)S(1)}, bf16[2112,384]{1,0:T(8,128)(2,1)}, u32[]{:S(2)}) copy-start(bf16[2112,384]{1,0:T(8,128)(2,1)} %w_out_ref.1) | copy-start | bytes 4866052
  16.1 4.5 %collective-permute-start.1 = (bf16[17,8,128]{2,1,0:T(8,128)(2,1)S(1)}, bf16[17,8,128]{2,1,0:T(8,128)(2,1)S(1)}, u32[]{:S(2)}, u32[]{:S(2)}) collective-permute-start(bf16[17,8,128]{2,1,0:T(8,128)(2,1)S(1)} %get-tuple-element.30), channel_id=1, source_target_pairs={{0,9},{1,8},{2,11},{3,10},{4,13},{5,12},{6,15},{7,14},{8,1},{9,0},... | collective-permute-start | bytes 104456 | tf_op jit(solution)/shard_map/ppermute | solution.py:626

commit v9 on v8

--- a/solution.py
+++ b/solution.py
@@ -20,6 +20,7 @@
 PLANE = HEADS * VP
 WIDE = 256 + 3 * 128
 SMALL = S // 128 + 1
+PIECES = 2
 PARTS = HEADS + WIDE // 128
 F32 = jnp.float32
 BF16 = jnp.bfloat16
@@ -61,19 +62,23 @@
 def pack_kernel(
     pair_hbm, single_hbm, frames_hbm, out_hbm, own_ref, pair_ref, small_ref, frames_ref, in_sems, out_sems
 ):
-    nsrc = pair_ref.shape[0]
+    chips = pair_ref.shape[0]
     local = own_ref.shape[0]
-    step = max(1, nsrc // 4)
-    upper = lax.axis_index("rows") // nsrc
-    starts = range(0, nsrc, step)
+    upper = lax.axis_index("rows") // (2 * chips)
+    step = max(1, chips // PIECES)
+    starts = range(0, chips, step)
     arrivals = []
     for at in starts:
-        mine = [(pair_hbm.at[upper, pl.ds(at, step)], pair_ref.at[pl.ds(at, step), pl.ds(0, local)])]
-        theirs = [
-            (pair_hbm.at[1 - upper, dest ^ 1], pair_ref.at[dest, pl.ds(local, local)])
-            for dest in range(at, at + step)
-        ]
-        for source, target in mine + theirs:
+        span = pl.ds(at, step)
+        moves = [(pair_hbm.at[upper, span], pair_ref.at[span, :, pl.ds(0, local)])]
+        for core in range(2):
+            moves.append(
+                (
+                    pair_hbm.at[1 - upper, span, 1 - core],
+                    pair_ref.at[span, core, pl.ds(local, local)],
+                )
+            )
+        for source, target in moves:
             arrivals.append(pltpu.make_async_copy(source, target, in_sems.at[len(arrivals)]))
     rows_copies = [
         pltpu.make_async_copy(single_hbm, own_ref.at[:, :S], in_sems.at[len(arrivals)]),
@@ -91,20 +96,21 @@
     low = turned - high - middle
     lane = iota(turned.shape, 1)
     own_ref[:, S:] = jnp.where(lane < 12, high, jnp.where(lane < 24, middle, low)).astype(BF16)
-    for dest in range(nsrc):
-        for piece in range(SMALL):
-            small_ref[dest, piece] = own_ref[:, piece * 128 : piece * 128 + 128]
+    for chip in range(chips):
+        for core in range(2):
+            for piece in range(SMALL):
+                small_ref[chip, core, piece] = own_ref[:, piece * 128 : piece * 128 + 128]
     departures = [
-        pltpu.make_async_copy(small_ref, out_hbm.at[:, pl.ds(2 * local, SMALL)], out_sems.at[0])
+        pltpu.make_async_copy(small_ref, out_hbm.at[:, :, pl.ds(2 * local, SMALL)], out_sems.at[0])
     ]
     departures[0].start()
     for k, at in enumerate(starts):
-        for copy in arrivals[k * (step + 1) : (k + 1) * (step + 1)]:
+        for copy in arrivals[3 * k : 3 * k + 3]:
             copy.wait()
         departures.append(
             pltpu.make_async_copy(
                 pair_ref.at[pl.ds(at, step)],
-                out_hbm.at[pl.ds(at, step), pl.ds(0, 2 * local)],
+                out_hbm.at[pl.ds(at, step), :, pl.ds(0, 2 * local)],
                 out_sems.at[1 + k],
             )
         )
@@ -537,23 +543,23 @@
     packed, own = pl.pallas_call(
         pack_kernel,
         out_shape=[
-            jax.ShapeDtypeStruct((nsrc, 2 * local + SMALL, local, C), BF16),
+            jax.ShapeDtypeStruct((nsrc // 2, 2, 2 * local + SMALL, local, C), BF16),
             jax.ShapeDtypeStruct((local, S + 128), BF16),
         ],
         in_specs=[whole(pltpu.HBM)] * 3,
         out_specs=[whole(pltpu.HBM), whole()],
         scratch_shapes=[
-            pltpu.VMEM((nsrc, 2 * local, local, C), BF16),
-            pltpu.VMEM((nsrc, SMALL, local, C), BF16),
+            pltpu.VMEM((nsrc // 2, 2, 2 * local, local, C), BF16),
+            pltpu.VMEM((nsrc // 2, 2, SMALL, local, C), BF16),
             pltpu.VMEM((local, 12), F32),
-            pltpu.SemaphoreType.DMA((nsrc + 6,)),
-            pltpu.SemaphoreType.DMA((5,)),
+            pltpu.SemaphoreType.DMA((3 * PIECES + 2,)),
+            pltpu.SemaphoreType.DMA((PIECES + 1,)),
         ],
         compiler_params=params(4 + large),
         name="pack",
-    )(*in_hbm([pair_grid.reshape(2, nsrc, local, local, C), single_rep, frames.T]))
+    )(*in_hbm([pair_grid.reshape(2, nsrc // 2, 2, local, local, C), single_rep, frames.T]))
     received = lax.all_to_all(
-        packed, "rows", 0, 0, tiled=True, axis_index_groups=halves
+        packed.reshape(nsrc, 2 * local + SMALL, local, C), "rows", 0, 0, tiled=True, axis_index_groups=halves
     )
     partner = lax.ppermute(own, "rows", across)
 

time: 22.1 us -> 22.1 us (level)
  no operation moved by 1% of the time
where the time goes in v9:
time: 22.1 us; the launch traced here: 21.8 us
  starting transfers between devices  9.81 us (44%)
  Pallas kernels  9.47 us (43%)
  waiting for transfers between devices  1.8 us (8%)
  between operations  0.69 us (3%)
    all_to_all x1, starting transfers between devices, on_device(): lax.all_to_all(packed.reshape(nsrc, 2 * local + SMALL, local, C), 'rows',...  5.27 us
    pallas_call x1, Pallas kernels, on_device(): pl.pallas_call(own_kernel, out_shape=[jax.ShapeDtypeStruct(pair_grid.shap...  3.44 us
    ppermute x1, starting transfers between devices, on_device(): partner = lax.ppermute(own, 'rows', across)  2.7 us
    ppermute x1, starting transfers between devices, on_device(): got = lax.ppermute(send, 'rows', across)  1.84 us
    pallas_call x1, Pallas kernels, on_device(): pl.pallas_call(pack_kernel, out_shape=[jax.ShapeDtypeStruct((nsrc // 2, 2...  1.68 us
    pallas_call x1, Pallas kernels, on_device(): pl.pallas_call(second_kernel, out_shape=[jax.ShapeDtypeStruct((HEADS, loc...  1.58 us
    pallas_call x1, Pallas kernels, on_device(): pl.pallas_call(first_kernel, out_shape=[jax.ShapeDtypeStruct((PARTS, loca...  1.57 us
    pallas_call x1, Pallas kernels, on_device(): pl.pallas_call(finish_kernel, out_shape=jax.ShapeDtypeStruct((local, S),...  1.19 us
  transfers between devices with their start and end apart: 3, of which 2 were waited for; matrix products, arithmetic and copies ran while one was open for 0% of the time, Pallas kernels for 23%

profile of v9, /device:TPU:0, one launch (start us, length us, event | category | flops | bytes accessed | tf_op | source)
XLA Modules:
  0.0 21.8 jit_solution(9473281774228379818)
XLA Ops:
  0.6 1.7 %pack.1 = (bf16[4,2,20,8,128]{4,3,2,1,0:T(8,128)(2,1)}, bf16[8,512]{1,0:T(8,128)(2,1)S(1)}) custom-call(bf16[2,4,2,8,8,128]{5,4,3,2,1,0:T(8,128)(2,1)} %bitcast.6, bf16[8,384]{1,0:T(8,128)(2,1)} %single_hbm.1, f32[8,12]{1,0:T(8,128)} %bitcast.9), custom_call_target="tpu_custom_call" | custom-call | tf_op jit(solution)/shard_map/pack/pallas_call | solution.py:543
  2.3 5.3 %all-to-all-start = ((bf16[8,20,8,128]{3,2,1,0:T(8,128)(2,1)}), bf16[8,20,8,128]{3,2,1,0:T(8,128)(2,1)S(1)}, u32[]{:S(2)}, u32[]{:S(2)}) async-start(bf16[8,20,8,128]{3,2,1,0:T(8,128)(2,1)} %bitcast.2), calls=%async_computation | async-start | bytes 655360 | tf_op jit(solution)/shard_map/all_to_all | solution.py:561
  7.6 0.0 copy-start.1
  7.6 0.0 copy-start.2
  7.6 2.7 %collective-permute-start = (bf16[8,512]{1,0:T(8,128)(2,1)S(1)}, bf16[8,512]{1,0:T(8,128)(2,1)S(1)}, u32[]{:S(2)}, u32[]{:S(2)}) collective-permute-start(bf16[8,512]{1,0:T(8,128)(2,1)S(1)} %get-tuple-element.23.own_ref), channel_id=1, source_target_pairs={{0,9},{1,8},{2,11},{3,10},{4,13},{5,12},{6,15},{7,14},{8,1},{9,0},... | collective-permute-start | bytes 24584 | tf_op jit(solution)/shard_map/ppermute | solution.py:564
  10.3 3.4 %own_transition.1 = (bf16[128,8,128]{2,1,0:T(8,128)(2,1)}, f32[3,16,128]{2,1,0:T(8,128)S(1)}, s32[2,128]{1,0:T(2,128)S(1)}, f32[1,512]{1,0:T(1,128)S(1)}, bf16[1...) custom-call(bf16[128,8,128]{2,1,0:T(8,128)(2,1)} %refs_0_.1, ...), custom_call_target="tpu_custom_call" | custom-call | tf_op jit(solution)/shard_map/own_transition/pallas_call | solution.py:583
  13.8 0.0 copy-start
  13.8 0.0 collective-permute-done.partner_ref
  13.8 0.7 %all-to-all-done.recv_ref = bf16[8,20,8,128]{3,2,1,0:T(8,128)(2,1)S(1)} async-done(((bf16[8,20,8,128]{3,2,1,0:T(8,128)(2,1)}), bf16[8,20,8,128]{3,2,1,0:T(8,128)(2,1)S(1)}, u32[]{:S(2)}, u32[]{:S(2)}) %all-to-all-start) | async-done | bytes 327712 | tf_op jit(solution)/shard_map/all_to_all | solution.py:561
  14.5 0.0 copy-done.1
  14.5 0.0 copy-done.2
  14.5 1.6 %first_half.1 = (bf16[17,8,128]{2,1,0:T(8,128)(2,1)S(1)}, bf16[2,64,640]{2,1,0:T(8,128)(2,1)S(1)}, s32[2,64]{1,0:T(2,128)S(1)}, bf16[2,192,64]{2,1,0:T(8,128)(2,...) custom-call(bf16[8,20,8,128]{3,2,1,0:T(8,128)(2,1)S(1)} %all-to-all-done.recv_ref, ...), custom_call_target="tpu_custom_call" | custom-call | tf_op jit(solution)/shard_map/first_half/pallas_call | solution.py:611
  16.1 1.8 %collective-permute-start.1 = (bf16[17,8,128]{2,1,0:T(8,128)(2,1)S(1)}, bf16[17,8,128]{2,1,0:T(8,128)(2,1)S(1)}, u32[]{:S(2)}, u32[]{:S(2)}) collective-permute-start(bf16[17,8,128]{2,1,0:T(8,128)(2,1)S(1)} %get-tuple-element.30), channel_id=1, source_target_pairs={{0,9},{1,8},{2,11},{3,10},{4,13},{5,12},{6,15},{7,14},{8,1},{9,0},... | collective-permute-start | bytes 104456 | tf_op jit(solution)/shard_map/ppermute | solution.py:632
  17.9 1.6 %second_half.1 = (f32[12,8,128]{2,1,0:T(8,128)S(1)}, f32[8,640]{1,0:T(8,128)S(1)}, f32[8,128]{1,0:T(8,128)S(1)}) custom-call(bf16[8,20,8,128]{3,2,1,0:T(8,128)(2,1)S(1)} %all-to-all-done.recv_ref, bf16[2,64,640]{2,1,0:T(8,128)(2,1)S(1)} %get-tuple-element.31.value_ref, s32[2,64]{1,0:T(2,128)S(1)} %get-tuple-element.32.near_ref, ...), custom_call_target="tpu_custom_call" | custom-call | tf_op jit(solution)/shard_map/second_half/pallas_call | solution.py:634
  19.5 1.1 %collective-permute-done.1.got_ref = bf16[17,8,128]{2,1,0:T(8,128)(2,1)S(1)} collective-permute-done((bf16[17,8,128]{2,1,0:T(8,128)(2,1)S(1)}, bf16[17,8,128]{2,1,0:T(8,128)(2,1)S(1)}, u32[]{:S(2)}, u32[]{:S(2)}) %collective-permute-start.1) | collective-permute-done | bytes 34848 | tf_op jit(solution)/shard_map/ppermute | solution.py:632
  20.6 0.0 copy-done
  20.6 1.2 %finish.1 = bf16[8,384]{1,0:T(8,128)(2,1)} custom-call(bf16[17,8,128]{2,1,0:T(8,128)(2,1)S(1)} %collective-permute-done.1.got_ref, f32[12,8,128]{2,1,0:T(8,128)S(1)} %get-tuple-element.37.sums_ref, f32[8,640]{1,0:T(8,128)S(1)} %get-tuple-element.38.wide_ref, f32[8,128]{1,0:T(8,128)S(1)} %get-tuple-element.39.level_ref, ...), custom_call_target="tpu_custom_call" | custom-call | tf_op jit(solution)/shard_map/finish/pallas_call | solution.py:648
Async XLA Ops:
  2.3 12.2 %all-to-all-start = ((bf16[8,20,8,128]{3,2,1,0:T(8,128)(2,1)}), bf16[8,20,8,128]{3,2,1,0:T(8,128)(2,1)S(1)}, u32[]{:S(2)}, u32[]{:S(2)}) async-start(bf16[8,20,8,128]{3,2,1,0:T(8,128)(2,1)} %bitcast.2), calls=%async_computation | async-start | bytes 655360 | tf_op jit(solution)/shard_map/all_to_all | solution.py:561
  7.6 6.9 %copy-start.1 = (bf16[128,1024]{1,0:T(8,128)(2,1)S(1)}, bf16[128,1024]{1,0:T(8,128)(2,1)}, u32[]{:S(2)}) copy-start(bf16[128,1024]{1,0:T(8,128)(2,1)} %w_swiglu_ref.3) | copy-start | bytes 786436
  7.6 6.9 %copy-start.2 = (bf16[512,128]{1,0:T(8,128)(2,1)S(1)}, bf16[512,128]{1,0:T(8,128)(2,1)}, u32[]{:S(2)}) copy-start(bf16[512,128]{1,0:T(8,128)(2,1)} %w_down_ref.3) | copy-start | bytes 393220
  7.6 6.2 %collective-permute-start = (bf16[8,512]{1,0:T(8,128)(2,1)S(1)}, bf16[8,512]{1,0:T(8,128)(2,1)S(1)}, u32[]{:S(2)}, u32[]{:S(2)}) collective-permute-start(bf16[8,512]{1,0:T(8,128)(2,1)S(1)} %get-tuple-element.23.own_ref), channel_id=1, source_target_pairs={{0,9},{1,8},{2,11},{3,10},{4,13},{5,12},{6,15},{7,14},{8,1},{9,0},... | collective-permute-start | bytes 24584 | tf_op jit(solution)/shard_map/ppermute | solution.py:564
  13.8 6.8 %copy-start = (bf16[2112,384]{1,0:T(8,128)(2,1)S(1)}, bf16[2112,384]{1,0:T(8,128)(2,1)}, u32[]{:S(2)}) copy-start(bf16[2112,384]{1,0:T(8,128)(2,1)} %w_out_ref.1) | copy-start | bytes 4866052
  16.1 4.5 %collective-permute-start.1 = (bf16[17,8,128]{2,1,0:T(8,128)(2,1)S(1)}, bf16[17,8,128]{2,1,0:T(8,128)(2,1)S(1)}, u32[]{:S(2)}, u32[]{:S(2)}) collective-permute-start(bf16[17,8,128]{2,1,0:T(8,128)(2,1)S(1)} %get-tuple-element.30), channel_id=1, source_target_pairs={{0,9},{1,8},{2,11},{3,10},{4,13},{5,12},{6,15},{7,14},{8,1},{9,0},... | collective-permute-start | bytes 104456 | tf_op jit(solution)/shard_map/ppermute | solution.py:632

commit v10 on v9

--- a/solution.py
+++ b/solution.py
@@ -127,9 +127,9 @@
 
 def own_kernel(*refs):
     sources, refs = refs[:13], refs[13:]
-    out_ref, heads_ref, rows_ref, gains_ref, wb_out_ref, w_loc_ref, wq_ref, wp_ref = refs[:8]
+    out_hbm, heads_ref, rows_ref, gains_ref, wb_out_ref, w_loc_ref, wq_ref, wp_ref = refs[:8]
     held, refs = refs[8:19], refs[19:]
-    loc_scr, sems = refs
+    done_ref, loc_scr, sems, out_sem = refs
     pair_hbm, *_ = sources
     n, local, _ = pair_hbm.shape
     targets = list(held) + [wq_ref, wp_ref]
@@ -149,12 +149,14 @@
     def step(at):
         values = pair_ref[pl.ds(at, block)].astype(F32).reshape(-1, C)
         done = transition(values, gain, w_swiglu_ref, w_down_ref)
-        out_ref[pl.ds(at, block)] = done.astype(F32).reshape(-1, local, C).astype(BF16)
+        done_ref[pl.ds(at, block)] = done.astype(F32).reshape(-1, local, C).astype(BF16)
 
     if n == block:
         step(0)
     else:
         pl.loop(0, n, step=block)(step)
+    leaving = pltpu.make_async_copy(done_ref, out_hbm, out_sem.at[0])
+    leaving.start()
     for copy in copies[4:]:
         copy.wait()
 
@@ -180,6 +182,7 @@
         loc_scr[t] = local_rows[:, t * 128 : (t + 1) * 128]
     for y in range(3):
         w_loc_ref[y] = strided(loc_scr, y, PLANE, 3).astype(BF16)
+    leaving.wait()
 
 
 def place(frame, triple):
@@ -453,7 +456,8 @@
 ):
     local = own_ref.shape[0]
     planes = [got_ref[HEADS + 2 + x].astype(F32) for x in range(3)]
-    got = 1.0 / (1.0 + jnp.exp(level_ref[...] - (planes[0] + planes[1] + planes[2])))
+    ahead = planes[0] + planes[1] + planes[2] - level_ref[...]
+    got = 0.5 + 0.5 * jnp.tanh(0.5 * ahead)
     lanes = iota((local, 128), 1)
     low_share = jnp.zeros((local, 128), F32)
     high_share = jnp.zeros((local, 128), F32)
@@ -593,11 +597,13 @@
             jax.ShapeDtypeStruct(sources[12].shape, BF16),
         ],
         in_specs=[whole(pltpu.HBM)] * len(sources),
-        out_specs=[whole()] * 8,
+        out_specs=[whole(pltpu.HBM)] + [whole()] * 7,
         scratch_shapes=held
         + [
+            pltpu.VMEM(pair_grid.shape, BF16),
             pltpu.VMEM((S // 128, 3 * PLANE, 128), F32),
             pltpu.SemaphoreType.DMA((len(sources),)),
+            pltpu.SemaphoreType.DMA((1,)),
         ],
         compiler_params=params(18 + large),
         name="own_transition",

time: 22.1 us -> 22.1 us (level)
  no operation moved by 1% of the time
where the time goes in v10:
time: 22.1 us; the launch traced here: 21.8 us
  starting transfers between devices  9.81 us (44%)
  Pallas kernels  9.39 us (42%)
  waiting for transfers between devices  1.87 us (8%)
  between operations  0.69 us (3%)
    all_to_all x1, starting transfers between devices, on_device(): lax.all_to_all(packed.reshape(nsrc, 2 * local + SMALL, local, C), 'rows',...  5.27 us
    pallas_call x1, Pallas kernels, on_device(): pl.pallas_call(own_kernel, out_shape=[jax.ShapeDtypeStruct(pair_grid.shap...  3.37 us
    ppermute x1, starting transfers between devices, on_device(): partner = lax.ppermute(own, 'rows', across)  2.7 us
    ppermute x1, starting transfers between devices, on_device(): got = lax.ppermute(send, 'rows', across)  1.84 us
    pallas_call x1, Pallas kernels, on_device(): pl.pallas_call(pack_kernel, out_shape=[jax.ShapeDtypeStruct((nsrc // 2, 2...  1.68 us
    pallas_call x1, Pallas kernels, on_device(): pl.pallas_call(second_kernel, out_shape=[jax.ShapeDtypeStruct((HEADS, loc...  1.58 us
    pallas_call x1, Pallas kernels, on_device(): pl.pallas_call(first_kernel, out_shape=[jax.ShapeDtypeStruct((PARTS, loca...  1.57 us
    pallas_call x1, Pallas kernels, on_device(): pl.pallas_call(finish_kernel, out_shape=jax.ShapeDtypeStruct((local, S),...  1.19 us
  transfers between devices with their start and end apart: 3, of which 2 were waited for; matrix products, arithmetic and copies ran while one was open for 0% of the time, Pallas kernels for 23%

profile of v10, /device:TPU:0, one launch (start us, length us, event | category | flops | bytes accessed | tf_op | source)
XLA Modules:
  0.0 21.8 jit_solution(17793365650988431243)
XLA Ops:
  0.6 1.7 %pack.1 = (bf16[4,2,20,8,128]{4,3,2,1,0:T(8,128)(2,1)}, bf16[8,512]{1,0:T(8,128)(2,1)S(1)}) custom-call(bf16[2,4,2,8,8,128]{5,4,3,2,1,0:T(8,128)(2,1)} %bitcast.6, bf16[8,384]{1,0:T(8,128)(2,1)} %single_hbm.1, f32[8,12]{1,0:T(8,128)} %bitcast.9), custom_call_target="tpu_custom_call" | custom-call | tf_op jit(solution)/shard_map/pack/pallas_call | solution.py:547
  2.3 5.3 %all-to-all-start = ((bf16[8,20,8,128]{3,2,1,0:T(8,128)(2,1)}), bf16[8,20,8,128]{3,2,1,0:T(8,128)(2,1)S(1)}, u32[]{:S(2)}, u32[]{:S(2)}) async-start(bf16[8,20,8,128]{3,2,1,0:T(8,128)(2,1)} %bitcast.2), calls=%async_computation | async-start | bytes 655360 | tf_op jit(solution)/shard_map/all_to_all | solution.py:565
  7.6 0.0 copy-start.1
  7.6 0.0 copy-start.2
  7.6 2.7 %collective-permute-start = (bf16[8,512]{1,0:T(8,128)(2,1)S(1)}, bf16[8,512]{1,0:T(8,128)(2,1)S(1)}, u32[]{:S(2)}, u32[]{:S(2)}) collective-permute-start(bf16[8,512]{1,0:T(8,128)(2,1)S(1)} %get-tuple-element.23.own_ref), channel_id=1, source_target_pairs={{0,9},{1,8},{2,11},{3,10},{4,13},{5,12},{6,15},{7,14},{8,1},{9,0},... | collective-permute-start | bytes 24584 | tf_op jit(solution)/shard_map/ppermute | solution.py:568
  10.3 3.4 %own_transition.1 = (bf16[128,8,128]{2,1,0:T(8,128)(2,1)}, f32[3,16,128]{2,1,0:T(8,128)S(1)}, s32[2,128]{1,0:T(2,128)S(1)}, f32[1,512]{1,0:T(1,128)S(1)}, bf16[1...) custom-call(bf16[128,8,128]{2,1,0:T(8,128)(2,1)} %refs_0_.1, ...), custom_call_target="tpu_custom_call" | custom-call | tf_op jit(solution)/shard_map/own_transition/pallas_call | solution.py:587
  13.7 0.0 copy-start
  13.7 0.0 collective-permute-done.partner_ref
  13.7 0.8 %all-to-all-done.recv_ref = bf16[8,20,8,128]{3,2,1,0:T(8,128)(2,1)S(1)} async-done(((bf16[8,20,8,128]{3,2,1,0:T(8,128)(2,1)}), bf16[8,20,8,128]{3,2,1,0:T(8,128)(2,1)S(1)}, u32[]{:S(2)}, u32[]{:S(2)}) %all-to-all-start) | async-done | bytes 327712 | tf_op jit(solution)/shard_map/all_to_all | solution.py:565
  14.5 0.0 copy-done.1
  14.5 0.0 copy-done.2
  14.5 1.6 %first_half.1 = (bf16[17,8,128]{2,1,0:T(8,128)(2,1)S(1)}, bf16[2,64,640]{2,1,0:T(8,128)(2,1)S(1)}, s32[2,64]{1,0:T(2,128)S(1)}, bf16[2,192,64]{2,1,0:T(8,128)(2,...) custom-call(bf16[8,20,8,128]{3,2,1,0:T(8,128)(2,1)S(1)} %all-to-all-done.recv_ref, ...), custom_call_target="tpu_custom_call" | custom-call | tf_op jit(solution)/shard_map/first_half/pallas_call | solution.py:617
  16.1 1.8 %collective-permute-start.1 = (bf16[17,8,128]{2,1,0:T(8,128)(2,1)S(1)}, bf16[17,8,128]{2,1,0:T(8,128)(2,1)S(1)}, u32[]{:S(2)}, u32[]{:S(2)}) collective-permute-start(bf16[17,8,128]{2,1,0:T(8,128)(2,1)S(1)} %get-tuple-element.30), channel_id=1, source_target_pairs={{0,9},{1,8},{2,11},{3,10},{4,13},{5,12},{6,15},{7,14},{8,1},{9,0},... | collective-permute-start | bytes 104456 | tf_op jit(solution)/shard_map/ppermute | solution.py:638
  17.9 1.6 %second_half.1 = (f32[12,8,128]{2,1,0:T(8,128)S(1)}, f32[8,640]{1,0:T(8,128)S(1)}, f32[8,128]{1,0:T(8,128)S(1)}) custom-call(bf16[8,20,8,128]{3,2,1,0:T(8,128)(2,1)S(1)} %all-to-all-done.recv_ref, bf16[2,64,640]{2,1,0:T(8,128)(2,1)S(1)} %get-tuple-element.31.value_ref, s32[2,64]{1,0:T(2,128)S(1)} %get-tuple-element.32.near_ref, ...), custom_call_target="tpu_custom_call" | custom-call | tf_op jit(solution)/shard_map/second_half/pallas_call | solution.py:640
  19.5 1.1 %collective-permute-done.1.got_ref = bf16[17,8,128]{2,1,0:T(8,128)(2,1)S(1)} collective-permute-done((bf16[17,8,128]{2,1,0:T(8,128)(2,1)S(1)}, bf16[17,8,128]{2,1,0:T(8,128)(2,1)S(1)}, u32[]{:S(2)}, u32[]{:S(2)}) %collective-permute-start.1) | collective-permute-done | bytes 34848 | tf_op jit(solution)/shard_map/ppermute | solution.py:638
  20.6 0.0 copy-done
  20.6 1.2 %finish.1 = bf16[8,384]{1,0:T(8,128)(2,1)} custom-call(bf16[17,8,128]{2,1,0:T(8,128)(2,1)S(1)} %collective-permute-done.1.got_ref, f32[12,8,128]{2,1,0:T(8,128)S(1)} %get-tuple-element.37.sums_ref, f32[8,640]{1,0:T(8,128)S(1)} %get-tuple-element.38.wide_ref, f32[8,128]{1,0:T(8,128)S(1)} %get-tuple-element.39.level_ref, ...), custom_call_target="tpu_custom_call" | custom-call | tf_op jit(solution)/shard_map/finish/pallas_call | solution.py:654
Async XLA Ops:
  2.3 12.2 %all-to-all-start = ((bf16[8,20,8,128]{3,2,1,0:T(8,128)(2,1)}), bf16[8,20,8,128]{3,2,1,0:T(8,128)(2,1)S(1)}, u32[]{:S(2)}, u32[]{:S(2)}) async-start(bf16[8,20,8,128]{3,2,1,0:T(8,128)(2,1)} %bitcast.2), calls=%async_computation | async-start | bytes 655360 | tf_op jit(solution)/shard_map/all_to_all | solution.py:565
  7.6 6.9 %copy-start.1 = (bf16[128,1024]{1,0:T(8,128)(2,1)S(1)}, bf16[128,1024]{1,0:T(8,128)(2,1)}, u32[]{:S(2)}) copy-start(bf16[128,1024]{1,0:T(8,128)(2,1)} %w_swiglu_ref.3) | copy-start | bytes 786436
  7.6 6.9 %copy-start.2 = (bf16[512,128]{1,0:T(8,128)(2,1)S(1)}, bf16[512,128]{1,0:T(8,128)(2,1)}, u32[]{:S(2)}) copy-start(bf16[512,128]{1,0:T(8,128)(2,1)} %w_down_ref.3) | copy-start | bytes 393220
  7.6 6.1 %collective-permute-start = (bf16[8,512]{1,0:T(8,128)(2,1)S(1)}, bf16[8,512]{1,0:T(8,128)(2,1)S(1)}, u32[]{:S(2)}, u32[]{:S(2)}) collective-permute-start(bf16[8,512]{1,0:T(8,128)(2,1)S(1)} %get-tuple-element.23.own_ref), channel_id=1, source_target_pairs={{0,9},{1,8},{2,11},{3,10},{4,13},{5,12},{6,15},{7,14},{8,1},{9,0},... | collective-permute-start | bytes 24584 | tf_op jit(solution)/shard_map/ppermute | solution.py:568
  13.7 6.9 %copy-start = (bf16[2112,384]{1,0:T(8,128)(2,1)S(1)}, bf16[2112,384]{1,0:T(8,128)(2,1)}, u32[]{:S(2)}) copy-start(bf16[2112,384]{1,0:T(8,128)(2,1)} %w_out_ref.1) | copy-start | bytes 4866052
  16.1 4.5 %collective-permute-start.1 = (bf16[17,8,128]{2,1,0:T(8,128)(2,1)S(1)}, bf16[17,8,128]{2,1,0:T(8,128)(2,1)S(1)}, u32[]{:S(2)}, u32[]{:S(2)}) collective-permute-start(bf16[17,8,128]{2,1,0:T(8,128)(2,1)S(1)} %get-tuple-element.30), channel_id=1, source_target_pairs={{0,9},{1,8},{2,11},{3,10},{4,13},{5,12},{6,15},{7,14},{8,1},{9,0},... | collective-permute-start | bytes 104456 | tf_op jit(solution)/shard_map/ppermute | solution.py:638

commit v11 on v9

--- a/solution.py
+++ b/solution.py
@@ -453,7 +453,8 @@
 ):
     local = own_ref.shape[0]
     planes = [got_ref[HEADS + 2 + x].astype(F32) for x in range(3)]
-    got = 1.0 / (1.0 + jnp.exp(level_ref[...] - (planes[0] + planes[1] + planes[2])))
+    ahead = planes[0] + planes[1] + planes[2] - level_ref[...]
+    got = 0.5 + 0.5 * jnp.tanh(0.5 * ahead)
     lanes = iota((local, 128), 1)
     low_share = jnp.zeros((local, 128), F32)
     high_share = jnp.zeros((local, 128), F32)

time: 22.1 us -> 22.1 us (level)
  no operation moved by 1% of the time
where the time goes in v11:
time: 22.1 us; the launch traced here: 21.8 us
  starting transfers between devices  9.81 us (44%)
  Pallas kernels  9.46 us (43%)
  waiting for transfers between devices  1.8 us (8%)
  between operations  0.69 us (3%)
    all_to_all x1, starting transfers between devices, on_device(): lax.all_to_all(packed.reshape(nsrc, 2 * local + SMALL, local, C), 'rows',...  5.27 us
    pallas_call x1, Pallas kernels, on_device(): pl.pallas_call(own_kernel, out_shape=[jax.ShapeDtypeStruct(pair_grid.shap...  3.44 us
    ppermute x1, starting transfers between devices, on_device(): partner = lax.ppermute(own, 'rows', across)  2.7 us
    ppermute x1, starting transfers between devices, on_device(): got = lax.ppermute(send, 'rows', across)  1.84 us
    pallas_call x1, Pallas kernels, on_device(): pl.pallas_call(pack_kernel, out_shape=[jax.ShapeDtypeStruct((nsrc // 2, 2...  1.68 us
    pallas_call x1, Pallas kernels, on_device(): pl.pallas_call(second_kernel, out_shape=[jax.ShapeDtypeStruct((HEADS, loc...  1.58 us
    pallas_call x1, Pallas kernels, on_device(): pl.pallas_call(first_kernel, out_shape=[jax.ShapeDtypeStruct((PARTS, loca...  1.57 us
    pallas_call x1, Pallas kernels, on_device(): pl.pallas_call(finish_kernel, out_shape=jax.ShapeDtypeStruct((local, S),...  1.19 us
  transfers between devices with their start and end apart: 3, of which 2 were waited for; matrix products, arithmetic and copies ran while one was open for 0% of the time, Pallas kernels for 23%

profile of v11, /device:TPU:0, one launch (start us, length us, event | category | flops | bytes accessed | tf_op | source)
XLA Modules:
  0.0 21.8 jit_solution(1676072969853427756)
XLA Ops:
  0.6 1.7 %pack.1 = (bf16[4,2,20,8,128]{4,3,2,1,0:T(8,128)(2,1)}, bf16[8,512]{1,0:T(8,128)(2,1)S(1)}) custom-call(bf16[2,4,2,8,8,128]{5,4,3,2,1,0:T(8,128)(2,1)} %bitcast.6, bf16[8,384]{1,0:T(8,128)(2,1)} %single_hbm.1, f32[8,12]{1,0:T(8,128)} %bitcast.9), custom_call_target="tpu_custom_call" | custom-call | tf_op jit(solution)/shard_map/pack/pallas_call | solution.py:544
  2.3 5.3 %all-to-all-start = ((bf16[8,20,8,128]{3,2,1,0:T(8,128)(2,1)}), bf16[8,20,8,128]{3,2,1,0:T(8,128)(2,1)S(1)}, u32[]{:S(2)}, u32[]{:S(2)}) async-start(bf16[8,20,8,128]{3,2,1,0:T(8,128)(2,1)} %bitcast.2), calls=%async_computation | async-start | bytes 655360 | tf_op jit(solution)/shard_map/all_to_all | solution.py:562
  7.6 0.0 copy-start.1
  7.6 0.0 copy-start.2
  7.6 2.7 %collective-permute-start = (bf16[8,512]{1,0:T(8,128)(2,1)S(1)}, bf16[8,512]{1,0:T(8,128)(2,1)S(1)}, u32[]{:S(2)}, u32[]{:S(2)}) collective-permute-start(bf16[8,512]{1,0:T(8,128)(2,1)S(1)} %get-tuple-element.23.own_ref), channel_id=1, source_target_pairs={{0,9},{1,8},{2,11},{3,10},{4,13},{5,12},{6,15},{7,14},{8,1},{9,0},... | collective-permute-start | bytes 24584 | tf_op jit(solution)/shard_map/ppermute | solution.py:565
  10.3 3.4 %own_transition.1 = (bf16[128,8,128]{2,1,0:T(8,128)(2,1)}, f32[3,16,128]{2,1,0:T(8,128)S(1)}, s32[2,128]{1,0:T(2,128)S(1)}, f32[1,512]{1,0:T(1,128)S(1)}, bf16[1...) custom-call(bf16[128,8,128]{2,1,0:T(8,128)(2,1)} %refs_0_.1, ...), custom_call_target="tpu_custom_call" | custom-call | tf_op jit(solution)/shard_map/own_transition/pallas_call | solution.py:584
  13.8 0.0 copy-start
  13.8 0.0 collective-permute-done.partner_ref
  13.8 0.7 %all-to-all-done.recv_ref = bf16[8,20,8,128]{3,2,1,0:T(8,128)(2,1)S(1)} async-done(((bf16[8,20,8,128]{3,2,1,0:T(8,128)(2,1)}), bf16[8,20,8,128]{3,2,1,0:T(8,128)(2,1)S(1)}, u32[]{:S(2)}, u32[]{:S(2)}) %all-to-all-start) | async-done | bytes 327712 | tf_op jit(solution)/shard_map/all_to_all | solution.py:562
  14.5 0.0 copy-done.1
  14.5 0.0 copy-done.2
  14.5 1.6 %first_half.1 = (bf16[17,8,128]{2,1,0:T(8,128)(2,1)S(1)}, bf16[2,64,640]{2,1,0:T(8,128)(2,1)S(1)}, s32[2,64]{1,0:T(2,128)S(1)}, bf16[2,192,64]{2,1,0:T(8,128)(2,...) custom-call(bf16[8,20,8,128]{3,2,1,0:T(8,128)(2,1)S(1)} %all-to-all-done.recv_ref, ...), custom_call_target="tpu_custom_call" | custom-call | tf_op jit(solution)/shard_map/first_half/pallas_call | solution.py:612
  16.1 1.8 %collective-permute-start.1 = (bf16[17,8,128]{2,1,0:T(8,128)(2,1)S(1)}, bf16[17,8,128]{2,1,0:T(8,128)(2,1)S(1)}, u32[]{:S(2)}, u32[]{:S(2)}) collective-permute-start(bf16[17,8,128]{2,1,0:T(8,128)(2,1)S(1)} %get-tuple-element.30), channel_id=1, source_target_pairs={{0,9},{1,8},{2,11},{3,10},{4,13},{5,12},{6,15},{7,14},{8,1},{9,0},... | collective-permute-start | bytes 104456 | tf_op jit(solution)/shard_map/ppermute | solution.py:633
  17.9 1.6 %second_half.1 = (f32[12,8,128]{2,1,0:T(8,128)S(1)}, f32[8,640]{1,0:T(8,128)S(1)}, f32[8,128]{1,0:T(8,128)S(1)}) custom-call(bf16[8,20,8,128]{3,2,1,0:T(8,128)(2,1)S(1)} %all-to-all-done.recv_ref, bf16[2,64,640]{2,1,0:T(8,128)(2,1)S(1)} %get-tuple-element.31.value_ref, s32[2,64]{1,0:T(2,128)S(1)} %get-tuple-element.32.near_ref, ...), custom_call_target="tpu_custom_call" | custom-call | tf_op jit(solution)/shard_map/second_half/pallas_call | solution.py:635
  19.5 1.1 %collective-permute-done.1.got_ref = bf16[17,8,128]{2,1,0:T(8,128)(2,1)S(1)} collective-permute-done((bf16[17,8,128]{2,1,0:T(8,128)(2,1)S(1)}, bf16[17,8,128]{2,1,0:T(8,128)(2,1)S(1)}, u32[]{:S(2)}, u32[]{:S(2)}) %collective-permute-start.1) | collective-permute-done | bytes 34848 | tf_op jit(solution)/shard_map/ppermute | solution.py:633
  20.6 0.0 copy-done
  20.6 1.2 %finish.1 = bf16[8,384]{1,0:T(8,128)(2,1)} custom-call(bf16[17,8,128]{2,1,0:T(8,128)(2,1)S(1)} %collective-permute-done.1.got_ref, f32[12,8,128]{2,1,0:T(8,128)S(1)} %get-tuple-element.37.sums_ref, f32[8,640]{1,0:T(8,128)S(1)} %get-tuple-element.38.wide_ref, f32[8,128]{1,0:T(8,128)S(1)} %get-tuple-element.39.level_ref, ...), custom_call_target="tpu_custom_call" | custom-call | tf_op jit(solution)/shard_map/finish/pallas_call | solution.py:649
Async XLA Ops:
  2.3 12.2 %all-to-all-start = ((bf16[8,20,8,128]{3,2,1,0:T(8,128)(2,1)}), bf16[8,20,8,128]{3,2,1,0:T(8,128)(2,1)S(1)}, u32[]{:S(2)}, u32[]{:S(2)}) async-start(bf16[8,20,8,128]{3,2,1,0:T(8,128)(2,1)} %bitcast.2), calls=%async_computation | async-start | bytes 655360 | tf_op jit(solution)/shard_map/all_to_all | solution.py:562
  7.6 6.9 %copy-start.1 = (bf16[128,1024]{1,0:T(8,128)(2,1)S(1)}, bf16[128,1024]{1,0:T(8,128)(2,1)}, u32[]{:S(2)}) copy-start(bf16[128,1024]{1,0:T(8,128)(2,1)} %w_swiglu_ref.3) | copy-start | bytes 786436
  7.6 6.9 %copy-start.2 = (bf16[512,128]{1,0:T(8,128)(2,1)S(1)}, bf16[512,128]{1,0:T(8,128)(2,1)}, u32[]{:S(2)}) copy-start(bf16[512,128]{1,0:T(8,128)(2,1)} %w_down_ref.3) | copy-start | bytes 393220
  7.6 6.2 %collective-permute-start = (bf16[8,512]{1,0:T(8,128)(2,1)S(1)}, bf16[8,512]{1,0:T(8,128)(2,1)S(1)}, u32[]{:S(2)}, u32[]{:S(2)}) collective-permute-start(bf16[8,512]{1,0:T(8,128)(2,1)S(1)} %get-tuple-element.23.own_ref), channel_id=1, source_target_pairs={{0,9},{1,8},{2,11},{3,10},{4,13},{5,12},{6,15},{7,14},{8,1},{9,0},... | collective-permute-start | bytes 24584 | tf_op jit(solution)/shard_map/ppermute | solution.py:565
  13.8 6.8 %copy-start = (bf16[2112,384]{1,0:T(8,128)(2,1)S(1)}, bf16[2112,384]{1,0:T(8,128)(2,1)}, u32[]{:S(2)}) copy-start(bf16[2112,384]{1,0:T(8,128)(2,1)} %w_out_ref.1) | copy-start | bytes 4866052
  16.1 4.5 %collective-permute-start.1 = (bf16[17,8,128]{2,1,0:T(8,128)(2,1)S(1)}, bf16[17,8,128]{2,1,0:T(8,128)(2,1)S(1)}, u32[]{:S(2)}, u32[]{:S(2)}) collective-permute-start(bf16[17,8,128]{2,1,0:T(8,128)(2,1)S(1)} %get-tuple-element.30), channel_id=1, source_target_pairs={{0,9},{1,8},{2,11},{3,10},{4,13},{5,12},{6,15},{7,14},{8,1},{9,0},... | collective-permute-start | bytes 104456 | tf_op jit(solution)/shard_map/ppermute | solution.py:633
